TPU v7x, 32 devices: a whole 2x2x4 slice. The times are simulated.
32 devices in a mesh: grp: 8 (over z, x), exp: 4 (over y, core).
Axes of the slice: x: 2, y: 2, z: 4, core: 2. Of those that a mesh axis runs over, the one named last changes fastest.
Arguments:
- step_inputs: bfloat16 [8, 4, 4, 2048], P('grp'), may hold values from -10 to 10
- parents: int32 [8, 4, 4], P('grp'), may hold values from 0 to 7
- routes: int32 [8, 4, 4, 6], P('grp'), may hold values from 0 to 63, all different within a row; in each aligned block of 16 rows (0 to 15, 16 to 31, ..., all dimensions but the last counted through in order) at most 3 rows name the same one
- w_qkv: bfloat16 [2048, 3, 2048], P(None, None, 'exp'), may hold values from -0.125 to 0.125
- w_out: bfloat16 [2048, 2048], P('exp'), may hold values from -0.125 to 0.125
- prompt_keys: bfloat16 [8, 1024, 2048], P('grp', None, 'exp'), may hold values from -128 to 128, as said below
- prompt_values: bfloat16 [8, 1024, 2048], P('grp', None, 'exp'), may hold values from -6 to 6
- prompt_parts: int32 [8], P('grp'), may hold values from 1 to 1024, as said below
- tail_keys: bfloat16 [8, 4, 60, 2048], P('grp', None, None, 'exp'), may hold values from -18 to 18
- tail_values: bfloat16 [8, 4, 60, 2048], P('grp', None, None, 'exp'), may hold values from -6 to 6
- w_router: bfloat16 [2048, 64], P('exp'), may hold values from -0.022097087 to 0.022097087
- norm_gain: float32 [2048], P('exp'), may hold values from 0.1 to 1.9
- w_gate_up: bfloat16 [64, 2048, 2816], P('grp', 'exp'), may hold values from -0.125 to 0.125
- w_down: bfloat16 [64, 2048, 1408], P('grp', 'exp'), may hold values from -0.15625 to 0.15625
Outputs:
- layer_out: bfloat16 [8, 4, 4, 2048], P('grp', None, None, 'exp')
Inputs may be any that keep to these rules, and one draw needn't show every extreme that they name: `prompt_keys`: keys of order a few units. `prompt_parts`: each part holds 1 to 1024 valid positions; in every draw some part holds exactly 1024. `routes`: within the rows of one slot no expert is named more than 3 times, and in every draw some expert is named exactly 3 times by the rows of some slot.
All inputs are finite; a program needn't handle non-finite values.
Results may differ from a plain program's by a relative error of at most 0.013.
Values may be sent and summed in bfloat16 or wider, within the bound.
No kernel may reach another device: no remote copies, remote signals or barrier semaphores. Data moves between devices by JAX's collectives and lax.ppermute only.
A program may use at most 128 MiB of HBM per device.

v0:
```python
import jax
import jax.numpy as jnp
from jax import lax
from jax.sharding import PartitionSpec as P

D = 2048
HDIM = 128
EXPERTS = 64
FFE = 1408
TOPK = 6
BEAMS = 8
STEPS = 4
TAIL = 64
CAP = 1024
CAP_E = 3
HALF = 4
PREV = 60


NEGATIVE = -1e30
EPSILON = 1e-06


def swapped(value, axis, stride):
    mask = 2**stride
    pairs = [(source, source ^ mask) for source in range(lax.axis_size(axis))]
    return lax.ppermute(value, axis, pairs)


def ordered(low_first, own_part, other_part):
    return jnp.concatenate(
        [jnp.where(low_first, own_part, other_part), jnp.where(low_first, other_part, own_part)],
        axis=0,
    )


def on_device(
    step_inputs,
    parents,
    routes,
    w_qkv,
    w_out,
    prompt_keys,
    prompt_values,
    prompt_parts,
    tail_keys,
    tail_values,
    w_router,
    norm_gain,
    w_gate_up,
    w_down,
):
    pair_half = lax.axis_index("grp") % 2
    column = lax.axis_index("exp")
    low_first = pair_half == 0
    own_inputs = step_inputs[0]
    own_parents = parents[0]
    other_inputs, other_parents = swapped((own_inputs, own_parents), "grp", 0)
    inputs_all = jnp.concatenate(
        [
            jnp.where(low_first, own_inputs, other_inputs),
            jnp.where(low_first, other_inputs, own_inputs),
        ],
        axis=1,
    )
    local_width = w_qkv.shape[2]
    local_heads = local_width // HDIM
    packed = jnp.dot(
        inputs_all.reshape(STEPS * BEAMS, D),
        w_qkv.reshape(D, 3 * local_width),
        preferred_element_type=jnp.float32,
    )
    packed = packed.astype(jnp.bfloat16).reshape(STEPS, BEAMS, 3, local_heads, HDIM)
    query_all = packed[:, :, 0]
    key_new = packed[:, :, 1]
    value_new = packed[:, :, 2]
    score_scale = HDIM ** (-0.5)
    own_start = pair_half * HALF
    other_start = (1 - pair_half) * HALF
    keys_here = prompt_keys[0].reshape(CAP, local_heads, HDIM)
    values_here = prompt_values[0].reshape(CAP, local_heads, HDIM)
    live_pos = jnp.arange(CAP, dtype=jnp.int32) < prompt_parts[0]
    prompt_scores = (
        jnp.einsum("sbhd,nhd->sbhn", query_all, keys_here, preferred_element_type=jnp.float32)
        * score_scale
    )
    prompt_scores = jnp.where(live_pos, prompt_scores, NEGATIVE)
    prompt_top = jnp.max(prompt_scores, axis=3)
    prompt_weights = jnp.exp(prompt_scores - prompt_top[..., None])
    prompt_total = jnp.sum(prompt_weights, axis=3)
    prompt_mix = jnp.einsum(
        "sbhn,nhd->sbhd",
        prompt_weights,
        values_here.astype(jnp.float32),
        precision=lax.Precision.HIGHEST,
    )

    def take_beams(array, start):
        return lax.dynamic_slice_in_dim(array, start, HALF, 1)

    far_top, far_total, far_mix = swapped(
        (
            take_beams(prompt_top, other_start),
            take_beams(prompt_total, other_start),
            take_beams(prompt_mix, other_start),
        ),
        "grp",
        0,
    )
    own_ids = own_start + jnp.arange(HALF, dtype=jnp.int32)
    keys_flat = key_new.reshape(STEPS, BEAMS, local_width)
    values_flat = value_new.reshape(STEPS, BEAMS, local_width)
    step_keys = []
    step_values = []
    tail_k = jnp.pad(tail_keys[0], ((0, 0), (0, STEPS), (0, 0)))
    tail_v = jnp.pad(tail_values[0], ((0, 0), (0, STEPS), (0, 0)))
    for step_index in range(STEPS):
        far_k, far_v = swapped((tail_k, tail_v), "grp", 0)
        every_k = ordered(low_first, tail_k, far_k)
        every_v = ordered(low_first, tail_v, far_v)
        chosen = own_parents[step_index]
        tail_k = every_k[chosen].at[:, PREV + step_index].set(keys_flat[step_index][own_ids])
        tail_v = every_v[chosen].at[:, PREV + step_index].set(values_flat[step_index][own_ids])
        step_keys.append(tail_k)
        step_values.append(tail_v)
    tail_k_all = jnp.stack(step_keys).reshape(STEPS, HALF, TAIL, local_heads, HDIM)
    tail_v_all = jnp.stack(step_values).reshape(STEPS, HALF, TAIL, local_heads, HDIM)
    own_query = take_beams(query_all, own_start)
    tail_scores = (
        jnp.einsum("sbhd,sbnhd->sbhn", own_query, tail_k_all, preferred_element_type=jnp.float32)
        * score_scale
    )
    tail_live = (
        jnp.arange(TAIL, dtype=jnp.int32)[None, :]
        <= PREV + jnp.arange(STEPS, dtype=jnp.int32)[:, None]
    )
    tail_scores = jnp.where(tail_live[:, None, None, :], tail_scores, NEGATIVE)
    tail_top = jnp.max(tail_scores, axis=3)
    tail_weights = jnp.exp(tail_scores - tail_top[..., None])
    tail_total = jnp.sum(tail_weights, axis=3)
    tail_mix = jnp.einsum(
        "sbhn,sbnhd->sbhd",
        tail_weights,
        tail_v_all.astype(jnp.float32),
        precision=lax.Precision.HIGHEST,
    )
    near_top = take_beams(prompt_top, own_start)
    near_total = take_beams(prompt_total, own_start)
    near_mix = take_beams(prompt_mix, own_start)
    best_top = jnp.maximum(jnp.maximum(near_top, tail_top), far_top)
    near_factor = jnp.exp(near_top - best_top)
    tail_factor = jnp.exp(tail_top - best_top)
    far_factor = jnp.exp(far_top - best_top)
    whole_total = near_total * near_factor + tail_total * tail_factor + far_total * far_factor
    whole_mix = (
        near_mix * near_factor[..., None]
        + tail_mix * tail_factor[..., None]
        + far_mix * far_factor[..., None]
    )
    row_count = STEPS * HALF
    attention = (
        (whole_mix / whole_total[..., None]).astype(jnp.bfloat16).reshape(row_count, local_width)
    )
    proj_terms = jnp.dot(attention, w_out, preferred_element_type=jnp.float32)
    attn_proj = lax.psum_scatter(proj_terms, "exp", scatter_dimension=1, tiled=True)
    feature_count = attn_proj.shape[1]
    residual_in = lax.dynamic_slice_in_dim(
        own_inputs.reshape(row_count, D), column * feature_count, feature_count, 1
    ).astype(jnp.float32)
    residual_rows = residual_in + attn_proj
    square_total = lax.psum(jnp.sum(residual_rows * residual_rows, axis=1), "exp")
    normed = (residual_rows * lax.rsqrt(square_total[:, None] / D + EPSILON) * norm_gain).astype(
        jnp.bfloat16
    )
    logits = lax.psum(jnp.dot(normed, w_router, preferred_element_type=jnp.float32), "exp")
    probs = jax.nn.softmax(logits, axis=1)
    chosen_routes = routes[0].reshape(row_count, TOPK)
    route_match = chosen_routes[:, :, None] == jnp.arange(EXPERTS, dtype=jnp.int32)[None, None, :]
    picked = jnp.sum(jnp.where(route_match, probs[:, None, :], 0.0), axis=2)
    route_share = picked / jnp.sum(picked, axis=1, keepdims=True)
    flat_match = route_match.reshape(row_count * TOPK, EXPERTS).astype(jnp.int32)
    earlier = jnp.cumsum(flat_match, axis=0) - flat_match
    slot_rank = jnp.sum(flat_match * earlier, axis=1)
    target = chosen_routes.reshape(row_count * TOPK) * CAP_E + slot_rank
    slot_place = target[:, None] == jnp.arange(EXPERTS * CAP_E, dtype=jnp.int32)[None, :]
    token_place = jnp.sum(
        slot_place.reshape(row_count, TOPK, EXPERTS * CAP_E).astype(jnp.float32), axis=1
    ).astype(jnp.bfloat16)
    share_matrix = jnp.sum(
        (slot_place.astype(jnp.float32) * route_share.reshape(row_count * TOPK)[:, None]).reshape(
            row_count, TOPK, EXPERTS * CAP_E
        ),
        axis=1,
    )
    outgoing = jnp.dot(token_place.T, normed, preferred_element_type=jnp.float32).astype(
        jnp.bfloat16
    )
    incoming = lax.all_to_all(outgoing, "grp", split_axis=0, concat_axis=0, tiled=True)
    groups = lax.axis_size("grp")
    local_experts = w_gate_up.shape[0]
    expert_input = incoming.reshape(groups, local_experts, CAP_E, feature_count)
    partial_units = jnp.einsum(
        "slcd,ldf->slcf", expert_input, w_gate_up, preferred_element_type=jnp.float32
    )
    summed_units = lax.psum(partial_units.astype(jnp.bfloat16), "exp").astype(jnp.float32)
    hidden_units = (jax.nn.silu(summed_units[..., :FFE]) * summed_units[..., FFE:]).astype(
        jnp.bfloat16
    )
    expert_result = jnp.einsum(
        "slcf,ldf->slcd", hidden_units, w_down, preferred_element_type=jnp.float32
    ).astype(jnp.bfloat16)
    returned = lax.all_to_all(
        expert_result.reshape(groups * local_experts * CAP_E, feature_count),
        "grp",
        split_axis=0,
        concat_axis=0,
        tiled=True,
    )
    expert_mix = jnp.dot(
        share_matrix, returned.astype(jnp.float32), precision=lax.Precision.HIGHEST
    )
    return (residual_rows + expert_mix).astype(jnp.bfloat16).reshape(1, STEPS, HALF, feature_count)


def solution(mesh):
    placed = (
        P("grp", None, None, None),
        P("grp", None, None),
        P("grp", None, None, None),
        P(None, None, "exp"),
        P("exp", None),
        P("grp", None, "exp"),
        P("grp", None, "exp"),
        P("grp"),
        P("grp", None, None, "exp"),
        P("grp", None, None, "exp"),
        P("exp", None),
        P("exp"),
        P("grp", "exp", None),
        P("grp", "exp", None),
    )
    return jax.shard_map(
        on_device,
        mesh=mesh,
        in_specs=placed,
        out_specs=P("grp", None, None, "exp"),
        check_vma=False,
    )
```

profile of v0, /device:TPU:0, one launch (start us, length us, event | category | flops | bytes accessed | tf_op | source)
XLA Modules:
  0.0 230.1 jit_solution(2928871737425489708)
XLA Ops:
  6.5 2.9 %collective-permute-start = (bf16[4,4,2048]{2,1,0:T(4,128)(2,1)}, bf16[4,4,2048]{2,1,0:T(4,128)(2,1)}, u32[]{:S(2)}, u32[]{:S(2)}) collective-permute-start(bf16[4,4,2048]{2,1,0:T(4,128)(2,1)} %bitcast.155), channel_id=1, source_target_pairs={{0,4},{4,0},{8,12},{12,8},{16,20},{20,16},{24,28},{28,24},{1,5},{5... | collective-permute-start | bytes 196616 | tf_op jit(solution)/shard_map/ppermute | solution.py:27
  9.5 1.0 copy.140
  11.5 1.0 copy.139
  13.2 1.9 collective-permute-start.6
  15.1 8.9 %copy.72 = bf16[2048,3,512]{0,2,1:T(8,128)(2,1)} copy(bf16[2048,3,512]{2,0,1:T(8,128)(2,1)} %param.33) | data formatting | bytes 12582912 | tf_op args[3]
  27.6 1.1 reshape_squeeze.12
  29.4 1.3 reshape_squeeze.13
  32.2 0.9 broadcast_select_fusion.17
  33.1 4.7 %convolution_convert_fusion = bf16[32,1536]{1,0:T(8,128)(2,1)S(1)} fusion(bf16[2048,1536]{0,1:T(8,128)(2,1)} %bitcast.139, bf16[4,4,2048]{2,1,0:T(4,128)(2,1)S(1)} %get-tuple-element.128, bf16[4,4,2048]{2,1,0:T(4,128)(2,1)S(1)} %get-tuple-element.127), kind=kOutput, calls=%fused_computation.22 | convolution fusion | flops 201637888 | bytes 6520832 | tf_op jit(solution)/shard_map/dot_general | solution.py:68
  38.5 2.0 gather_fusion.1
  40.4 1.3 copy.77
  41.7 1.3 gather_fusion.3
  43.0 1.3 copy.78
  44.3 1.8 fusion.53
  47.8 1.9 collective-permute-start.5
  51.6 1.4 gather_fusion.5
  58.5 1.1 broadcast_select_fusion.15
  60.4 1.9 collective-permute-start.2
  63.1 1.0 broadcast_select_fusion.7
  65.3 4.1 %collective-permute-done.2 = bf16[4,64,512]{2,1,0:T(8,128)(2,1)} collective-permute-done((bf16[4,64,512]{2,1,0:T(8,128)(2,1)S(1)}, bf16[4,64,512]{2,1,0:T(8,128)(2,1)}, u32[]{:S(2)}, u32[]{:S(2)}) %collective-permute-start.2) | collective-permute-done | bytes 262176 | tf_op jit(solution)/shard_map/ppermute | solution.py:27
  69.4 1.0 broadcast_select_fusion.13
  71.2 2.3 collective-permute-start.3
  75.0 1.0 broadcast_select_fusion.5
  76.8 2.3 collective-permute-start.8
  79.9 0.9 collective-permute-done.3
  80.8 1.0 broadcast_select_fusion.11
  82.7 2.1 collective-permute-start.4
  85.5 0.9 collective-permute-done.8
  86.5 1.0 broadcast_select_fusion.3
  88.3 2.1 collective-permute-start.9
  91.1 1.0 collective-permute-done.4
  92.1 1.0 broadcast_select_fusion.9
  94.0 2.1 pad_maximum_fusion
  97.0 1.0 broadcast_select_fusion.1
  99.1 1.9 pad_maximum_fusion.1
  101.1 0.9 fusion.20
  103.1 0.9 fusion.36
  104.0 1.0 fusion.38
  105.6 20.7 %reduce-scatter.2.cloned.1.call-done = f32[16,512]{1,0:T(8,128)} async-done(((f32[16,2048]{1,0:T(8,128)}), f32[16,512]{1,0:T(8,128)}) %reduce-scatter.2.cloned.1.call-update) | async-done | bytes 32784 | tf_op jit(solution)/shard_map/reduce_scatter | solution.py:165
  126.3 0.9 multiply_reduce_fusion
  127.2 5.8 %psum.21 = f32[16]{0:T(128)S(1)} all-reduce(f32[16]{0:T(128)S(1)} %multiply_reduce_fusion), channel_id=1, replica_groups=mesh['grp'=8,'exp'=4] {'exp'}, use_global_device_ids=true, to_apply=%region_8.9 | all-reduce | flops 16 | bytes 128 | tf_op jit(solution)/shard_map/psum | solution.py:171
  133.9 5.9 %psum.22 = f32[16,64]{1,0:T(8,128)S(1)} all-reduce(f32[16,64]{1,0:T(8,128)S(1)} %fusion.54), channel_id=1, replica_groups=mesh['grp'=8,'exp'=4] {'exp'}, use_global_device_ids=true, to_apply=%region_9.10 | all-reduce | flops 1024 | bytes 8192 | tf_op jit(solution)/shard_map/psum | solution.py:175
  140.8 13.4 %all_to_all.21 = bf16[8,24,512]{2,1,0:T(8,128)(2,1)S(1)} all-to-all(bf16[8,24,512]{2,1,0:T(8,128)(2,1)S(1)} %bitcast.150), channel_id=1, replica_groups=mesh['grp'=8,'exp'=4] {'grp'}, dimensions={0} | all-to-all | bytes 393216 | tf_op jit(solution)/shard_map/all_to_all | solution.py:198
  154.3 11.7 %fusion.7 = bf16[8,8,3,2816]{3,0,2,1:T(8,128)(2,1)} fusion(bf16[8,8,3,512]{3,0,2,1:T(8,128)(2,1)S(1)} %bitcast.148, bf16[8,512,2816]{2,1,0:T(8,128)(2,1)} %param.42), kind=kOutput, calls=%fused_computation.21 | convolution fusion | flops 554188800 | bytes 24346624 | tf_op jit(solution)/shard_map/slcd,ldf->slcf/dot_general | solution.py:202
  166.0 34.3 %all-reduce.4.cloned.1.call-done = bf16[8,8,3,2816]{3,0,2,1:T(8,128)(2,1)} async-done(((bf16[8,8,3,2816]{3,0,2,1:T(8,128)(2,1)}), bf16[8,8,3,2816]{3,0,2,1:T(8,128)(2,1)}) %all-reduce.4.cloned.1.call-update) | async-done | bytes 1081360 | tf_op jit(solution)/shard_map/psum | solution.py:205
  200.3 1.4 convert_element_type.62
  201.7 7.5 %fusion.12 = bf16[8,8,3,512]{3,1,2,0:T(8,128)(2,1)S(1)} fusion(bf16[8,512,1408]{2,1,0:T(8,128)(2,1)} %param.43, f32[8,8,3,2816]{3,0,2,1:T(8,128)S(1)} %convert_element_type.62), kind=kOutput, calls=%fused_computation.27 | convolution fusion | flops 278544384 | bytes 13893632 | tf_op jit(solution)/shard_map/slcf,ldf->slcd/dot_general | solution.py:209
  209.3 13.1 %all_to_all.22 = bf16[8,24,512]{2,1,0:T(8,128)(2,1)S(1)} all-to-all(bf16[8,24,512]{2,1,0:T(8,128)(2,1)S(1)} %copy.93), channel_id=1, replica_groups=mesh['grp'=8,'exp'=4] {'grp'}, dimensions={0} | all-to-all | bytes 393216 | tf_op jit(solution)/shard_map/all_to_all | solution.py:212
  (159 shorter events, 33.5 us)
Async XLA Ops:
  6.5 97.5 %copy-start = (bf16[512,2048]{1,0:T(8,128)(2,1)S(1)}, bf16[512,2048]{1,0:T(8,128)(2,1)}, u32[]{:S(2)}) copy-start(bf16[512,2048]{1,0:T(8,128)(2,1)} %param.34) | copy-start | bytes 6291460
  6.5 119.8 %reduce-scatter.2.cloned.1.call-start = ((), (), s32[]{:S(2)}) async-start(), calls=%async_computation.3 | async-start | bytes 163840 | tf_op jit(solution)/shard_map/reduce_scatter | solution.py:165
  6.5 25.7 %collective-permute-start = (bf16[4,4,2048]{2,1,0:T(4,128)(2,1)}, bf16[4,4,2048]{2,1,0:T(4,128)(2,1)}, u32[]{:S(2)}, u32[]{:S(2)}) collective-permute-start(bf16[4,4,2048]{2,1,0:T(4,128)(2,1)} %bitcast.155), channel_id=1, source_target_pairs={{0,4},{4,0},{8,12},{12,8},{16,20},{20,16},{24,28},{28,24},{1,5},{5... | collective-permute-start | bytes 196616 | tf_op jit(solution)/shard_map/ppermute | solution.py:27
  10.5 0.9 copy-start.2
  11.3 47.2 %collective-permute-start.1 = (bf16[4,64,512]{2,1,0:T(8,128)(2,1)}, bf16[4,64,512]{2,1,0:T(8,128)(2,1)}, u32[]{:S(2)}, u32[]{:S(2)}) collective-permute-start(bf16[4,64,512]{2,1,0:T(8,128)(2,1)} %pad.23), channel_id=1, source_target_pairs={{0,4},{4,0},{8,12},{12,8},{16,20},{20,16},{24,28},{28,24},{1,5},{5... | collective-permute-start | bytes 786440 | tf_op jit(solution)/shard_map/ppermute | solution.py:27
  13.2 50.0 %collective-permute-start.6 = (bf16[4,64,512]{2,1,0:T(8,128)(2,1)}, bf16[4,64,512]{2,1,0:T(8,128)(2,1)}, u32[]{:S(2)}, u32[]{:S(2)}) collective-permute-start(bf16[4,64,512]{2,1,0:T(8,128)(2,1)} %pad.24), channel_id=1, source_target_pairs={{0,4},{4,0},{8,12},{12,8},{16,20},{20,16},{24,28},{28,24},{1,5},{5... | collective-permute-start | bytes 786440 | tf_op jit(solution)/shard_map/ppermute | solution.py:27
  15.1 8.9 %copy-start.25 = (s32[1,4,4]{2,1,0:T(4,128)S(1)}, s32[1,4,4]{2,1,0:T(4,128)}, u32[]{:S(2)}) copy-start(s32[1,4,4]{2,1,0:T(4,128)} %param.31) | copy-start | bytes 196
  15.1 12.5 %copy-start.3 = (bf16[1,1024,512]{2,1,0:T(8,128)(2,1)S(1)}, bf16[1,1024,512]{2,1,0:T(8,128)(2,1)}, u32[]{:S(2)}) copy-start(bf16[1,1024,512]{2,1,0:T(8,128)(2,1)} %param.35) | copy-start | bytes 3145732
  24.0 6.8 %copy-start.13 = (s32[1,4,4,6]{3,2,1,0:T(4,128)S(1)}, s32[1,4,4,6]{3,2,1,0:T(4,128)}, u32[]{:S(2)}) copy-start(s32[1,4,4,6]{3,2,1,0:T(4,128)} %param.32) | copy-start | bytes 1156
  27.6 4.6 %copy-start.8 = (bf16[1,4,4,2048]{3,2,1,0:T(4,128)(2,1)S(1)}, bf16[1,4,4,2048]{3,2,1,0:T(4,128)(2,1)}, u32[]{:S(2)}) copy-start(bf16[1,4,4,2048]{3,2,1,0:T(4,128)(2,1)} %param.30) | copy-start | bytes 196612
  30.8 7.0 %copy-start.21 = (s32[96]{0:T(128)}, s32[96]{0:T(128)S(1)}, u32[]{:S(2)}) copy-start(s32[96]{0:T(128)S(1)} %eq.43) | copy-start | bytes 1156
  46.3 3.4 %copy-start.11 = (f32[4,8,4]{1,0,2:T(4,128)}, f32[4,8,4]{1,0,2:T(4,128)S(1)}, u32[]{:S(2)}) copy-start(f32[4,8,4]{1,0,2:T(4,128)S(1)} %fusion.26) | copy-start | bytes 1540
  47.6 54.6 %collective-permute-start.11 = (f32[4,4,4]{1,0,2:T(4,128)}, f32[4,4,4]{1,0,2:T(4,128)}, u32[]{:S(2)}, u32[]{:S(2)}) collective-permute-start(f32[4,4,4]{1,0,2:T(4,128)} %constant_dynamic-slice_fusion), channel_id=1, source_target_pairs={{0,4},{4,0},{8,12},{12,8},{16,20},{20,16},{24,28},{28,24},{1,5},{5... | collective-permute-start | bytes 776 | tf_op jit(solution)/shard_map/ppermute | solution.py:27
  47.8 54.4 %collective-permute-start.5 = (f32[4,4,4]{1,0,2:T(4,128)}, f32[4,4,4]{1,0,2:T(4,128)}, u32[]{:S(2)}, u32[]{:S(2)}) collective-permute-start(f32[4,4,4]{1,0,2:T(4,128)} %constant_dynamic-slice_fusion.1), channel_id=1, source_target_pairs={{0,4},{4,0},{8,12},{12,8},{16,20},{20,16},{24,28},{28,24},{1,5},{5... | collective-permute-start | bytes 776 | tf_op jit(solution)/shard_map/ppermute | solution.py:27
  50.3 0.6 copy-start.6
  50.9 9.4 %copy-start.19 = (bf16[4,1,512]{2,1,0:T(2,128)(2,1)S(1)}, bf16[4,1,512]{2,1,0:T(2,128)(2,1)}, u32[]{:S(2)}) copy-start(bf16[4,1,512]{2,1,0:T(2,128)(2,1)} %copy.77) | copy-start | bytes 12292
  57.6 45.4 %collective-permute-start.10 = (f32[4,4,4,128]{3,1,0,2:T(4,128)}, f32[4,4,4,128]{3,1,0,2:T(4,128)}, u32[]{:S(2)}, u32[]{:S(2)}) collective-permute-start(f32[4,4,4,128]{3,1,0,2:T(4,128)} %dynamic-slice_bitcast_fusion), channel_id=1, source_target_pairs={{0,4},{4,0},{8,12},{12,8},{16,20},{20,16},{24,28},{28,24},{1,5},{5... | collective-permute-start | bytes 98312 | tf_op jit(solution)/shard_map/ppermute | solution.py:27
  60.4 8.9 %collective-permute-start.2 = (bf16[4,64,512]{2,1,0:T(8,128)(2,1)S(1)}, bf16[4,64,512]{2,1,0:T(8,128)(2,1)}, u32[]{:S(2)}, u32[]{:S(2)}) collective-permute-start(bf16[4,64,512]{2,1,0:T(8,128)(2,1)S(1)} %scatter.26), channel_id=1, source_target_pairs={{0,4},{4,0},{8,12},{12,8},{16,20},{20,16},{24,28},{28,24},{1,5},{5... | collective-permute-start | bytes 786440 | tf_op jit(solution)/shard_map/ppermute | solution.py:27
  64.2 6.9 %copy-start.18 = (bf16[4,1,512]{2,1,0:T(2,128)(2,1)S(1)}, bf16[4,1,512]{2,1,0:T(2,128)(2,1)}, u32[]{:S(2)}) copy-start(bf16[4,1,512]{2,1,0:T(2,128)(2,1)} %copy.78) | copy-start | bytes 12292
  65.0 10.0 %collective-permute-start.7 = (bf16[4,64,512]{2,1,0:T(8,128)(2,1)S(1)}, bf16[4,64,512]{2,1,0:T(8,128)(2,1)}, u32[]{:S(2)}, u32[]{:S(2)}) collective-permute-start(bf16[4,64,512]{2,1,0:T(8,128)(2,1)S(1)} %scatter.34), channel_id=1, source_target_pairs={{0,4},{4,0},{8,12},{12,8},{16,20},{20,16},{24,28},{28,24},{1,5},{5... | collective-permute-start | bytes 786440 | tf_op jit(solution)/shard_map/ppermute | solution.py:27
  71.2 9.6 %collective-permute-start.3 = (bf16[4,64,512]{2,1,0:T(8,128)(2,1)S(1)}, bf16[4,64,512]{2,1,0:T(8,128)(2,1)}, u32[]{:S(2)}, u32[]{:S(2)}) collective-permute-start(bf16[4,64,512]{2,1,0:T(8,128)(2,1)S(1)} %scatter.29), channel_id=1, source_target_pairs={{0,4},{4,0},{8,12},{12,8},{16,20},{20,16},{24,28},{28,24},{1,5},{5... | collective-permute-start | bytes 786440 | tf_op jit(solution)/shard_map/ppermute | solution.py:27
  76.0 6.6 %copy-start.17 = (bf16[4,1,512]{2,1,0:T(2,128)(2,1)S(1)}, bf16[4,1,512]{2,1,0:T(2,128)(2,1)}, u32[]{:S(2)}) copy-start(bf16[4,1,512]{2,1,0:T(2,128)(2,1)} %copy.79) | copy-start | bytes 12292
  76.8 9.6 %collective-permute-start.8 = (bf16[4,64,512]{2,1,0:T(8,128)(2,1)S(1)}, bf16[4,64,512]{2,1,0:T(8,128)(2,1)}, u32[]{:S(2)}, u32[]{:S(2)}) collective-permute-start(bf16[4,64,512]{2,1,0:T(8,128)(2,1)S(1)} %scatter.35), channel_id=1, source_target_pairs={{0,4},{4,0},{8,12},{12,8},{16,20},{20,16},{24,28},{28,24},{1,5},{5... | collective-permute-start | bytes 786440 | tf_op jit(solution)/shard_map/ppermute | solution.py:27
  82.7 9.4 %collective-permute-start.4 = (bf16[4,64,512]{2,1,0:T(8,128)(2,1)S(1)}, bf16[4,64,512]{2,1,0:T(8,128)(2,1)}, u32[]{:S(2)}, u32[]{:S(2)}) collective-permute-start(bf16[4,64,512]{2,1,0:T(8,128)(2,1)S(1)} %scatter.30), channel_id=1, source_target_pairs={{0,4},{4,0},{8,12},{12,8},{16,20},{20,16},{24,28},{28,24},{1,5},{5... | collective-permute-start | bytes 786440 | tf_op jit(solution)/shard_map/ppermute | solution.py:27
  87.4 6.4 %copy-start.16 = (bf16[1,4,1,512]{3,2,1,0:T(2,128)(2,1)S(1)}, bf16[1,4,1,512]{3,2,1,0:T(2,128)(2,1)}, u32[]{:S(2)}) copy-start(bf16[1,4,1,512]{3,2,1,0:T(2,128)(2,1)} %copy.80) | copy-start | bytes 12292
  88.3 8.8 %collective-permute-start.9 = (bf16[4,64,512]{2,1,0:T(8,128)(2,1)S(1)}, bf16[4,64,512]{2,1,0:T(8,128)(2,1)}, u32[]{:S(2)}, u32[]{:S(2)}) collective-permute-start(bf16[4,64,512]{2,1,0:T(8,128)(2,1)S(1)} %scatter.36), channel_id=1, source_target_pairs={{0,4},{4,0},{8,12},{12,8},{16,20},{20,16},{24,28},{28,24},{1,5},{5... | collective-permute-start | bytes 786440 | tf_op jit(solution)/shard_map/ppermute | solution.py:27
  93.1 3.0 %copy-start.20 = (bf16[4,4,4,128,1]{3,1,0,2,4:T(4,128)(2,1)S(1)}, bf16[4,4,4,128,1]{3,1,0,2,4:T(4,128)(2,1)}, u32[]{:S(2)}) copy-start(bf16[4,4,4,128,1]{3,1,0,2,4:T(4,128)(2,1)} %dynamic-slice_bitcast_fusion.1) | copy-start | bytes 49156
  93.1 3.6 %copy-start.24 = (pred[4,64]{1,0:T(4,128)(4,1)S(1)}, pred[4,64]{1,0:T(4,128)(4,1)}, u32[]{:S(2)}) copy-start(pred[4,64]{1,0:T(4,128)(4,1)} %iota_compare_fusion.4) | copy-start | bytes 772
  96.1 3.0 %copy-start.4 = (bf16[1,4,64,4,128]{4,3,2,1,0:T(4,128)(2,1)S(1)}, bf16[1,4,64,4,128]{4,3,2,1,0:T(4,128)(2,1)}, u32[]{:S(2)}) copy-start(bf16[1,4,64,4,128]{4,3,2,1,0:T(4,128)(2,1)} %stack.46) | copy-start | bytes 786436
  98.1 4.1 %copy-start.12 = (f32[4,8,4]{1,0,2:T(4,128)S(1)}, f32[4,8,4]{1,0,2:T(4,128)}, u32[]{:S(2)}) copy-start(f32[4,8,4]{1,0,2:T(4,128)} %copy-done.11) | copy-start | bytes 1540
  98.1 5.0 %copy-start.7 = (f32[4,4,8,128]{3,2,1,0:T(8,128)S(1)}, f32[4,4,8,128]{3,2,1,0:T(8,128)}, u32[]{:S(2)}) copy-start(f32[4,4,8,128]{3,2,1,0:T(8,128)} %copy-done.6) | copy-start | bytes 196612
  101.0 4.1 %copy-start.10 = (s32[96,64]{1,0:T(8,128)S(1)}, s32[96,64]{1,0:T(8,128)}, u32[]{:S(2)}) copy-start(s32[96,64]{1,0:T(8,128)} %reduce_window_sum.11) | copy-start | bytes 73732
  101.0 4.1 %copy-start.22 = (s32[96]{0:T(128)S(1)}, s32[96]{0:T(128)}, u32[]{:S(2)}) copy-start(s32[96]{0:T(128)} %copy-done.21) | copy-start | bytes 1156
  101.0 4.3 %copy-start.9 = (bf16[1,4,4,2048]{3,2,1,0:T(4,128)(2,1)S(1)}, bf16[1,4,4,2048]{3,2,1,0:T(4,128)(2,1)}, u32[]{:S(2)}) copy-start(bf16[1,4,4,2048]{3,2,1,0:T(4,128)(2,1)} %param.30) | copy-start | bytes 196612
  101.0 4.3 %copy-start.14 = (s32[1,4,4,6]{3,2,1,0:T(4,128)S(1)}, s32[1,4,4,6]{3,2,1,0:T(4,128)}, u32[]{:S(2)}) copy-start(s32[1,4,4,6]{3,2,1,0:T(4,128)} %param.32) | copy-start | bytes 1156
  101.0 31.9 %copy-start.23 = (f32[512]{0:T(512)S(1)}, f32[512]{0:T(512)}, u32[]{:S(2)}) copy-start(f32[512]{0:T(512)} %param.41) | copy-start | bytes 6148
  101.0 32.8 %copy-start.15 = (bf16[512,64]{0,1:T(8,128)(2,1)S(1)}, bf16[512,64]{0,1:T(8,128)(2,1)}, u32[]{:S(2)}) copy-start(bf16[512,64]{0,1:T(8,128)(2,1)} %param.40) | copy-start | bytes 196612
  105.1 95.3 %all-reduce.4.cloned.1.call-start = ((), (), s32[]{:S(2)}) async-start(), calls=%async_computation.4 | async-start | bytes 2162688 | tf_op jit(solution)/shard_map/psum | solution.py:205
  201.7 20.7 %copy-start.5 = (f32[16,512]{1,0:T(8,128)S(1)}, f32[16,512]{1,0:T(8,128)}, u32[]{:S(2)}) copy-start(f32[16,512]{1,0:T(8,128)} %reduce-scatter.2.cloned.1.call-done) | copy-start | bytes 98308
  201.7 21.5 %copy-start.1 = (bf16[512,2048]{1,0:T(8,128)(2,1)S(1)}, bf16[512,2048]{1,0:T(8,128)(2,1)}, u32[]{:S(2)}) copy-start(bf16[512,2048]{1,0:T(8,128)(2,1)} %param.34) | copy-start | bytes 6291460
Sparse Core Ops, SparseCore 0:
  105.2 21.1 reduce-scatter.1
  166.1 34.1 all-reduce.3
where the time goes:
time: 232 us; the launch traced here: 230 us
  waiting for transfers between devices  62.8 us (27%)
  local copies, waits for them, and re-layouts  42.1 us (18%)
  blocking collectives  38.2 us (16%)
  matrix products  29.5 us (13%)
  other arithmetic  24.6 us (11%)
  starting transfers between devices  18.2 us (8%)
  between operations  14.8 us (6%)
    psum x1, waiting for transfers between devices, on_device(): lax.psum(partial_units.astype(jnp.bfloat16), 'exp').astype(jnp.float32)  34.3 us
    reduce_scatter x1, waiting for transfers between devices, on_device(): lax.psum_scatter(proj_terms, 'exp', scatter_dimension=1, tiled=True)  20.7 us
    ppermute x12, starting transfers between devices, swapped(): return lax.ppermute(value, axis, pairs)  18.1 us
    all_to_all x1, blocking collectives, on_device(): lax.all_to_all(outgoing, 'grp', split_axis=0, concat_axis=0, tiled=True)  13.4 us
    all_to_all x1, blocking collectives, on_device(): lax.all_to_all(expert_result.reshape(groups * local_experts * CAP_E, feat...  13.1 us
    dot_general x1, matrix products, on_device(): jnp.einsum('slcd,ldf->slcf', expert_input, w_gate_up, preferred_element_t...  11.7 us
    unnamed x55, local copies, waits for them, and re-layouts  11.6 us
    select_n x8, other arithmetic, ordered(): jnp.where(low_first, own_part, other_part)  8.1 us
  transfers between devices with their start and end apart: 14, of which 7 were waited for; matrix products, arithmetic and copies ran while one was open for 30% of the time, Pallas kernels for 0%

commit v1 on v0

v1 whole, which is shorter than its diff:
```python
import functools

import jax
import jax.numpy as jnp
from jax import lax
from jax.experimental import pallas as pl
from jax.experimental.pallas import tpu as pltpu
from jax.sharding import PartitionSpec as P

HDIM = 128
EXPERTS = 64
FFE = 1408
TOPK = 6
BEAMS = 8
STEPS = 4
CAP_E = 3
HALF = 4
PREV = 60
LANES = 128
ROWS = STEPS * HALF
PAIR = 2 * ROWS
STATS = 1 + TOPK

NEGATIVE = -1e30
EPSILON = 1e-06
MIB = 1024 * 1024
BF = jnp.bfloat16
F32 = jnp.float32

VMEM = pl.BlockSpec(memory_space=pltpu.VMEM)
SMEM = pl.BlockSpec(memory_space=pltpu.SMEM)
ANY = pl.BlockSpec(memory_space=pl.ANY)


def iota(shape, dim):
    return lax.broadcasted_iota(jnp.int32, shape, dim)


def dot(a, b):
    return jnp.dot(a, b, preferred_element_type=F32)


def dot_t(a, b):
    return lax.dot_general(a, b, (((1,), (1,)), ((), ())), preferred_element_type=F32)


def t_dot(a, b):
    return lax.dot_general(a, b, (((0,), (0,)), ((), ())), preferred_element_type=F32)


def exchanged(value, axis, mask):
    pairs = [(source, source ^ mask) for source in range(lax.axis_size(axis))]
    return lax.ppermute(value, axis, pairs)


def call(body, outs, in_specs, *args, scratch=(), limit=32, flops=0, nbytes=0):
    return pl.pallas_call(
        body,
        out_shape=outs,
        in_specs=in_specs,
        out_specs=jax.tree.map(lambda _: VMEM, outs),
        scratch_shapes=list(scratch),
        compiler_params=pltpu.CompilerParams(vmem_limit_bytes=limit * MIB),
        cost_estimate=pl.CostEstimate(flops=flops, bytes_accessed=nbytes, transcendentals=0),
    )(*args)


def shape(dims, dtype):
    return jax.ShapeDtypeStruct(tuple(dims), dtype)


def attend_kernel(parts, par, x, wqkv, kp, vp, tk, tv, out):
    half = lax.axis_index("grp") % 2
    width = wqkv.shape[2]
    heads = width // HDIM
    rows = x[...]
    query = dot(rows, wqkv[0]).astype(BF)
    key_new = dot(rows, wqkv[1]).astype(BF)
    value_new = dot(rows, wqkv[2]).astype(BF)
    lane = iota((BEAMS, LANES), 1)
    beam = iota((BEAMS, LANES), 0)
    state = (lane == beam).astype(F32)
    states = []
    for step in range(STEPS):
        parent = par[:, step : step + 1]
        taken = jnp.zeros((BEAMS, LANES), F32)
        for j in range(BEAMS):
            taken = taken + jnp.where(parent == j, state[j : j + 1, :], 0.0)
        state = jnp.where(lane == BEAMS + BEAMS * step + beam, 1.0, taken)
        states.append(state)
    held = jnp.concatenate(states, axis=0).astype(BF)
    to_row = iota((PAIR, PAIR), 0)
    from_row = iota((PAIR, PAIR), 1)
    wanted = (to_row % ROWS // HALF) * BEAMS + (to_row // ROWS) * HALF + to_row % HALF
    held = dot((from_row == wanted).astype(BF), held).astype(BF)
    tails = tk.shape[0]
    place = iota((LANES, tails), 0)
    column = iota((LANES, tails), 1)
    tail_mask = dot(held, (place == half * HALF + column % HALF).astype(BF)) > 0.5
    place = iota((LANES, PAIR), 0)
    column = iota((LANES, PAIR), 1)
    new_at = BEAMS + BEAMS * (column % ROWS // HALF) + (column // ROWS) * HALF + column % HALF
    new_mask = dot(held, ((place == new_at) & (column // ROWS == half)).astype(BF)) > 0.5
    cap = kp.shape[0]
    live = iota((PAIR, cap), 1) < parts[0]
    scale = HDIM ** (-0.5)
    info = jnp.zeros((PAIR, LANES), F32)
    info_lane = iota((PAIR, LANES), 1)
    for head in range(heads):
        at = slice(head * HDIM, (head + 1) * HDIM)
        q = query[:, at]
        s_p = jnp.where(live, dot_t(q, kp[:, at]) * scale, NEGATIVE)
        s_t = jnp.where(tail_mask, dot_t(q, tk[:, at]) * scale, NEGATIVE)
        s_n = jnp.where(new_mask, dot_t(q, key_new[:, at]) * scale, NEGATIVE)
        top = jnp.maximum(
            jnp.max(s_p, axis=1, keepdims=True),
            jnp.maximum(
                jnp.max(s_t, axis=1, keepdims=True), jnp.max(s_n, axis=1, keepdims=True)
            ),
        )
        p_p = jnp.exp(s_p - top)
        p_t = jnp.exp(s_t - top)
        p_n = jnp.exp(s_n - top)
        total = (
            jnp.sum(p_p, axis=1, keepdims=True)
            + jnp.sum(p_t, axis=1, keepdims=True)
            + jnp.sum(p_n, axis=1, keepdims=True)
        )
        mix = (
            dot(p_p.astype(BF), vp[:, at])
            + dot(p_t.astype(BF), tv[:, at])
            + dot(p_n.astype(BF), value_new[:, at])
        )
        out[:, at] = mix
        info = jnp.where(info_lane == head, top, info)
        info = jnp.where(info_lane == heads + head, total, info)
    out[:, width:] = info


def project_kernel(near, far, w_out, *outs):
    me = lax.axis_index("exp")
    width = w_out.shape[0]
    heads = width // HDIM
    parts = []
    for head in range(heads):
        at = slice(head * HDIM, (head + 1) * HDIM)
        m_at = slice(width + head, width + head + 1)
        l_at = slice(width + heads + head, width + heads + head + 1)
        top = jnp.maximum(near[:, m_at], far[:, m_at])
        f_near = jnp.exp(near[:, m_at] - top)
        f_far = jnp.exp(far[:, m_at] - top)
        total = near[:, l_at] * f_near + far[:, l_at] * f_far
        mix = near[:, at] * f_near + far[:, at] * f_far
        parts.append((mix / total).astype(BF))
    attention = jnp.concatenate(parts, axis=1)
    features = outs[0].shape[1]
    for k, out in enumerate(outs):
        start = pl.multiple_of((me ^ k) * features, LANES)
        out[...] = dot(attention, w_out[:, pl.ds(start, features)]).astype(out.dtype)


def residual_kernel(x, gain, w_router, routes, own, *rest):
    others, (residual_out, message) = rest[:-2], rest[-2:]
    me = lax.axis_index("exp")
    features = own.shape[1]
    start = pl.multiple_of(me * features, LANES)
    residual = x[:, pl.ds(start, features)].astype(F32) + own[...]
    for other in others:
        residual = residual + other[...].astype(F32)
    residual_out[...] = residual
    rows = (residual * gain[...]).astype(BF)
    message[:, :features] = rows
    logits = dot(rows, w_router[...])
    expert = iota(logits.shape, 1)
    lane = iota((PAIR, LANES), 1)
    info = jnp.zeros((PAIR, LANES), F32)
    columns = [jnp.sum(residual * residual, axis=1, keepdims=True)]
    for k in range(TOPK):
        route = routes[:, k : k + 1]
        columns.append(jnp.sum(jnp.where(expert == route, logits, 0.0), axis=1, keepdims=True))
        info = jnp.where(lane == 2 * STATS + k, route.astype(F32), info)
    for at, column in enumerate(columns):
        high = column.astype(BF).astype(F32)
        info = jnp.where(lane == at, high, info)
        info = jnp.where(lane == STATS + at, column - high, info)
    message[:, features:] = info.astype(BF)


def gather_kernel(local, *refs):
    messages, (picked, stats, target, choice, rows) = refs[:-5], refs[-5:]
    blocks = len(messages)
    tokens = blocks * PAIR
    features = rows.shape[1]
    infos = []
    for k, message in enumerate(messages):
        rows[k * PAIR : (k + 1) * PAIR, :] = message[:, :features]
        infos.append(message[:, features:].astype(F32))
    info = jnp.concatenate(infos, axis=0).T
    stats[...] = jnp.concatenate(
        [info[:STATS] + info[STATS : 2 * STATS], jnp.zeros((8 - STATS, tokens), F32)], axis=0
    )
    first = (lax.axis_index("grp") * local).astype(F32)
    expert = iota((8, tokens), 0).astype(F32)
    chosen = jnp.full((8, tokens), -1.0, F32)
    for k in range(TOPK):
        route = info[2 * STATS + k : 2 * STATS + k + 1] - first
        chosen = jnp.where((route == expert) & (expert < local), float(k), chosen)
    choice[...] = chosen
    named = chosen >= 0.0
    before = iota((tokens, tokens), 0)
    after = iota((tokens, tokens), 1)
    earlier = ((before < after) & (before // ROWS == after // ROWS)).astype(BF)
    rank = dot(named.astype(BF), earlier)
    slot = (iota((8, tokens), 1) // ROWS).astype(F32)
    goal = jnp.where(named, slot * CAP_E + rank, -1.0)
    target[...] = goal
    capacity = picked.shape[0] // local
    row = iota((capacity, tokens), 0).astype(F32)
    places = [(row == goal[e : e + 1]).astype(BF) for e in range(local)]
    picked[...] = dot(jnp.concatenate(places, axis=0), rows[...]).astype(BF)


def gate_kernel(mask, block, has_far, keep, picked, weights, *refs):
    far = refs[0] if has_far else None
    out, buffer, sems = refs[-3:]
    me = lax.axis_index("exp")
    first = (me ^ mask) * block
    width = weights.shape[2] // 2
    copies = []
    for e in range(block):
        for part in range(2):
            at = pl.ds(part * width, width)
            copies.append(
                pltpu.make_async_copy(
                    weights.at[first + e, :, at], buffer.at[e, :, at], sems.at[2 * e + part]
                )
            )
    for copy in copies:
        copy.start()
    capacity = out.shape[0] // block
    start = pl.multiple_of(first * capacity, block * capacity)
    rows = picked[pl.ds(start, block * capacity), :]
    for part in range(2):
        sums = []
        for e in range(block):
            copies[2 * e + part].wait()
            sums.append(
                dot(
                    rows[e * capacity : (e + 1) * capacity],
                    buffer[e, :, part * width : (part + 1) * width],
                )
            )
        result = jnp.concatenate(sums, axis=0)
        at = slice(part * width, (part + 1) * width)
        if has_far:
            result = result + far[:, at].astype(F32)
        out[:, at] = result.astype(out.dtype)


def gate_block(mask, block, picked, weights, far, dtype):
    local, depth, width = weights.shape
    rows = picked.shape[0] // local * block
    args = (picked, weights) + (() if far is None else (far,))
    return call(
        functools.partial(gate_kernel, mask, block, far is not None, 0),
        shape((rows, width), dtype),
        [VMEM, ANY] + [VMEM] * (far is not None),
        *args,
        scratch=[
            pltpu.VMEM((block, depth, width), BF),
            pltpu.SemaphoreType.DMA((2 * block,)),
        ],
        flops=2 * rows * depth * width,
        nbytes=2 * block * depth * width,
    )


def hidden_kernel(block, near, far, target, stat0, stat1, stat2, stat3, hidden, total):
    me = lax.axis_index("exp")
    stats = (stat0[...] + stat1[...]) + (stat2[...] + stat3[...])
    total[...] = stats
    rows = near.shape[0]
    capacity = rows // block
    depth = 2048
    inverse = lax.rsqrt(stats[0:1] / depth + EPSILON)
    row = iota((capacity, target.shape[1]), 0).astype(F32)
    scales = []
    for e in range(block):
        goal = target[pl.ds(me * block + e, 1), :]
        scales.append(jnp.sum(jnp.where(row == goal, inverse, 0.0), axis=1, keepdims=True))
    scale = jnp.concatenate(scales, axis=0)
    width = near.shape[1] // 2
    gate = (near[:, :width] + far[:, :width].astype(F32)) * scale
    up = (near[:, width:] + far[:, width:].astype(F32)) * scale
    hidden[...] = (gate / (1.0 + jnp.exp(-gate)) * up).astype(BF)


def shares_of(stats):
    inverse = lax.rsqrt(stats[0:1] / 2048 + EPSILON)
    logits = [stats[1 + k : 2 + k] * inverse for k in range(TOPK)]
    top = functools.reduce(jnp.maximum, logits)
    weights = [jnp.exp(logit - top) for logit in logits]
    whole = functools.reduce(lambda a, b: a + b, weights)
    return [weight / whole for weight in weights]


def down_kernel(masks, block, mode, weights, stats, target, choice, *refs):
    count = len(masks)
    hiddens, refs = refs[:count], refs[count:]
    before = None
    if mode != "first":
        before, refs = refs[0], refs[1:]
    buffer, sems = refs[-2:]
    outs = refs[:-2]
    me = lax.axis_index("exp")
    copies = []
    for i, mask in enumerate(masks):
        for e in range(block):
            copies.append(
                pltpu.make_async_copy(
                    weights.at[(me ^ mask) * block + e],
                    buffer.at[i * block + e],
                    sems.at[i * block + e],
                )
            )
    for copy in copies:
        copy.start()
    shares = shares_of(stats[...])
    tokens = target.shape[1]
    capacity = hiddens[0].shape[0] // block
    row = iota((capacity, tokens), 0).astype(F32)
    places, results = [], []
    for i, mask in enumerate(masks):
        for e in range(block):
            at = (me ^ mask) * block + e
            goal = target[pl.ds(at, 1), :]
            picked = choice[pl.ds(at, 1), :]
            share = jnp.zeros((1, tokens), F32)
            for k in range(TOPK):
                share = jnp.where(picked == float(k), shares[k], share)
            places.append(jnp.where(row == goal, share, 0.0))
            copies[i * block + e].wait()
            units = hiddens[i][...].astype(F32)[e * capacity : (e + 1) * capacity].astype(BF)
            results.append(dot_t(units, buffer[i * block + e]))
    place = jnp.concatenate(places, axis=0)
    result = jnp.concatenate(results, axis=0).astype(BF)
    high = place.astype(BF)
    low = (place - high.astype(F32)).astype(BF)
    mixed = t_dot(high, result) + t_dot(low, result)
    if before is not None:
        mixed = mixed + before[...]
    if mode != "last":
        outs[0][...] = mixed
        return
    keep, send = outs
    half = lax.axis_index("grp") % 2
    for k in range(tokens // PAIR):
        low_rows = mixed[k * PAIR : k * PAIR + ROWS]
        high_rows = mixed[k * PAIR + ROWS : (k + 1) * PAIR]
        at = slice(k * ROWS, (k + 1) * ROWS)
        keep[at, :] = jnp.where(half == 0, low_rows, high_rows)
        send[at, :] = jnp.where(half == 0, high_rows, low_rows).astype(BF)


def down_blocks(masks, block, mode, weights, stats, target, choice, hiddens, before):
    features, width = weights.shape[1:]
    tokens = target.shape[1]
    if mode == "last":
        outs = (shape((tokens // 2, features), F32), shape((tokens // 2, features), BF))
    else:
        outs = (shape((tokens, features), F32),)
    args = (weights, stats, target, choice) + tuple(hiddens)
    if before is not None:
        args = args + (before,)
    experts = len(masks) * block
    return call(
        functools.partial(down_kernel, masks, block, mode),
        outs,
        [ANY] + [VMEM] * (len(args) - 1),
        *args,
        scratch=[
            pltpu.VMEM((experts, features, width), BF),
            pltpu.SemaphoreType.DMA((experts,)),
        ],
        flops=2 * experts * hiddens[0].shape[0] // block * features * width,
        nbytes=2 * experts * features * width,
    )


def fold_kernel(keep, far, *outs):
    for k, out in enumerate(outs):
        at = slice(k * ROWS, (k + 1) * ROWS)
        out[...] = (keep[at, :] + far[at, :].astype(F32)).astype(out.dtype)


def finish_kernel(residual, own, *rest):
    others, out = rest[:-1], rest[-1]
    half = lax.axis_index("grp") % 2
    value = residual[pl.ds(pl.multiple_of(half * ROWS, ROWS), ROWS), :] + own[...]
    for other in others:
        value = value + other[...].astype(F32)
    out[...] = value.astype(out.dtype)


def on_device(
    step_inputs,
    parents,
    routes,
    w_qkv,
    w_out,
    prompt_keys,
    prompt_values,
    prompt_parts,
    tail_keys,
    tail_values,
    w_router,
    norm_gain,
    w_gate_up,
    w_down,
):
    groups = lax.axis_size("grp")
    splits = lax.axis_size("exp")
    requests = groups // 2
    low_first = lax.axis_index("grp") % 2 == 0
    model = w_qkv.shape[0]
    width = w_qkv.shape[2]
    features = norm_gain.shape[0]
    local = w_gate_up.shape[0]
    tokens = requests * PAIR

    def both(own, other, dims):
        own, other = own.reshape(dims), other.reshape(dims)
        return jnp.concatenate(
            [jnp.where(low_first, own, other), jnp.where(low_first, other, own)], axis=0
        )

    own_inputs, own_parents, own_routes = step_inputs[0], parents[0], routes[0]
    far_inputs, far_parents, far_routes = exchanged(
        (own_inputs, own_parents, own_routes), "grp", 1
    )
    x = both(own_inputs, far_inputs, (ROWS, model))
    routes_all = both(own_routes, far_routes, (ROWS, TOPK))
    par = both(own_parents.T, far_parents.T, (HALF, STEPS))
    tail_k = tail_keys[0].transpose(1, 0, 2).reshape(PREV * HALF, width)
    tail_v = tail_values[0].transpose(1, 0, 2).reshape(PREV * HALF, width)
    near = call(
        attend_kernel,
        shape((PAIR, width + LANES), F32),
        [SMEM] + [VMEM] * 7,
        prompt_parts,
        par,
        x,
        w_qkv.transpose(1, 0, 2),
        prompt_keys[0],
        prompt_values[0],
        tail_k,
        tail_v,
        flops=2 * PAIR * model * 3 * width,
        nbytes=6 * model * width,
    )
    far = exchanged(near, "grp", 1)
    terms = call(
        project_kernel,
        tuple(shape((PAIR, features), F32 if k == 0 else BF) for k in range(splits)),
        [VMEM] * 3,
        near,
        far,
        w_out,
        flops=2 * PAIR * width * model,
        nbytes=2 * width * model,
    )
    arrived = [exchanged(terms[k], "exp", k) for k in range(1, splits)]
    residual, message = call(
        residual_kernel,
        (shape((PAIR, features), F32), shape((PAIR, features + LANES), BF)),
        [VMEM] * (5 + len(arrived)),
        x,
        norm_gain.reshape(1, features),
        w_router,
        routes_all,
        terms[0],
        *arrived,
    )
    messages = [message] + [exchanged(message, "grp", 2 * k) for k in range(1, requests)]
    picked, stats, target, choice = call(
        functools.partial(gather_kernel, local),
        (
            shape((EXPERTS * CAP_E, features), BF),
            shape((8, tokens), F32),
            shape((8, tokens), F32),
            shape((8, tokens), F32),
        ),
        [VMEM] * requests,
        *messages,
        scratch=[pltpu.VMEM((tokens, features), BF)],
    )
    if splits == 4 and local % splits == 0:
        block = local // splits
        gate = functools.partial(gate_block, block=block, picked=picked, weights=w_gate_up)
        far_stats = [exchanged(stats, "exp", k) for k in range(1, splits)]
        sums_a = gate(3, far=None, dtype=BF)
        far_a = exchanged(sums_a, "exp", 1)
        sums_b = gate(1, far=None, dtype=BF)
        sums_c = gate(2, far=far_a, dtype=BF)
        far_b = exchanged(sums_b, "exp", 1)
        far_c = exchanged(sums_c, "exp", 2)
        sums_d = gate(0, far=far_b, dtype=F32)
        hidden, stats = call(
            functools.partial(hidden_kernel, block),
            (shape((sums_d.shape[0], FFE), BF), shape((8, tokens), F32)),
            [VMEM] * 7,
            sums_d,
            far_c,
            target,
            stats,
            *far_stats,
        )
        down = functools.partial(
            down_blocks, block=block, weights=w_down, stats=stats, target=target, choice=choice
        )
        hidden_y = exchanged(hidden, "exp", 2)
        hidden_c = exchanged(hidden, "exp", 1)
        hidden_f = exchanged(hidden_y, "exp", 1)
        (mixed,) = down((0, 1), mode="first", hiddens=(hidden, hidden_c), before=None)
        (mixed,) = down((2,), mode="more", hiddens=(hidden_y,), before=mixed)
        keep, send = down((3,), mode="last", hiddens=(hidden_f,), before=mixed)
    else:
        stats = lax.psum(stats, "exp")
        rows = picked.reshape(local, -1, features)
        sums = jnp.einsum("lcd,ldf->lcf", rows, w_gate_up, preferred_element_type=F32)
        sums = lax.psum(sums.astype(BF), "exp").astype(F32)
        inverse = lax.rsqrt(stats[0] / model + EPSILON)
        goal, pick = target[:local], choice[:local]
        place = goal[:, None, :] == jnp.arange(rows.shape[1], dtype=F32)[None, :, None]
        sums = sums * jnp.sum(jnp.where(place, inverse, 0.0), axis=2, keepdims=True)
        hidden = (jax.nn.silu(sums[..., :FFE]) * sums[..., FFE:]).astype(BF)
        result = jnp.einsum("lcf,ldf->lcd", hidden, w_down, preferred_element_type=F32)
        share = jax.nn.softmax(stats[1:STATS] * inverse, axis=0)
        ids = jnp.arange(TOPK, dtype=F32)[None, :, None]
        weight = jnp.sum(jnp.where(pick[:, None, :] == ids, share[None], 0.0), axis=1)
        mixed = jnp.einsum(
            "lct,lcd->td",
            jnp.where(place, weight[:, None, :], 0.0),
            result.astype(BF).astype(F32),
            precision=lax.Precision.HIGHEST,
        ).reshape(requests, 2, ROWS, features)
        pair_half = lax.axis_index("grp") % 2
        keep = lax.dynamic_index_in_dim(mixed, pair_half, 1, False).reshape(-1, features)
        send = lax.dynamic_index_in_dim(mixed, 1 - pair_half, 1, False)
        send = send.reshape(-1, features).astype(BF)
    folded = call(
        fold_kernel,
        tuple(shape((ROWS, features), F32 if k == 0 else BF) for k in range(requests)),
        [VMEM] * 2,
        keep,
        exchanged(send, "grp", 1),
    )
    back = [exchanged(folded[k], "grp", 2 * k) for k in range(1, requests)]
    result = call(
        finish_kernel,
        shape((ROWS, features), BF),
        [VMEM] * (2 + len(back)),
        residual,
        folded[0],
        *back,
    )
    return result.reshape(1, STEPS, HALF, features)


def solution(mesh):
    placed = (
        P("grp", None, None, None),
        P("grp", None, None),
        P("grp", None, None, None),
        P(None, None, "exp"),
        P("exp", None),
        P("grp", None, "exp"),
        P("grp", None, "exp"),
        P("grp"),
        P("grp", None, None, "exp"),
        P("grp", None, None, "exp"),
        P("exp", None),
        P("exp"),
        P("grp", "exp", None),
        P("grp", "exp", None),
    )
    return jax.shard_map(
        on_device,
        mesh=mesh,
        in_specs=placed,
        out_specs=P("grp", None, None, "exp"),
        check_vma=False,
    )
```

time: 232 us -> 86.1 us (0.37)
  blocking collectives: 38.2 us -> 0 us
  waiting for transfers between devices: 62.8 us -> 25.1 us
  local copies, waits for them, and re-layouts: 42.1 us -> 12.1 us
  matrix products: 29.5 us -> 0 us
  Pallas kernels: 0 us -> 26 us
  other arithmetic: 24.6 us -> 0.75 us
  between operations: 14.8 us -> 0.92 us
  starting transfers between devices: 18.2 us -> 20.8 us
    psum x1 -> x0, waiting for transfers between devices: 34.3 us -> none  [on_device(): lax.psum(partial_units.astype(jnp.bfloat16), 'exp').astype(jnp.float32)]
    dot_general x11 -> x0, matrix products: 29.5 us -> none  [the longest x1 11.7 us: on_device(): jnp.einsum('slcd,ldf->slcf', expert_input, w_gate_up, preferred_element_t...]
    all_to_all x2 -> x0, blocking collectives: 26.5 us -> none  [the longest x1 13.4 us: on_device(): lax.all_to_all(outgoing, 'grp', split_axis=0, concat_axis=0, tiled=True)]
    pallas_call x0 -> x14, Pallas kernels: none -> 26 us  [call(): pl.pallas_call(body, out_shape=outs, in_specs=in_specs, out_specs=jax.tre...]
    reduce_scatter x1 -> x0, waiting for transfers between devices: 20.7 us -> none  [on_device(): lax.psum_scatter(proj_terms, 'exp', scatter_dimension=1, tiled=True)]
    ppermute x12 -> x23, waiting for transfers between devices: 7.68 us -> 25.1 us  [exchanged(): return lax.ppermute(value, axis, pairs)]
    gather x16 -> x0, local copies, waits for them, and re-layouts: 13.7 us -> none  [the longest x4 5.32 us: on_device(): keys_flat[step_index][own_ids]]
    psum x2 -> x0, blocking collectives: 11.7 us -> none  [the longest x1 5.93 us: on_device(): lax.psum(jnp.dot(normed, w_router, preferred_element_type=jnp.float32), '...]
  transfers between devices with their start and end apart: 14 -> 23, of which waited for: 7 -> 10; matrix products, arithmetic and copies ran while one was open for 30% -> 6% of each run, Pallas kernels for 0% -> 22%
where the time goes in v1:
time: 86.1 us; the launch traced here: 85.6 us
  Pallas kernels  26 us (30%)
  waiting for transfers between devices  25.1 us (29%)
  starting transfers between devices  20.8 us (24%)
  local copies, waits for them, and re-layouts  12.1 us (14%)
  between operations  0.92 us (1%)
    pallas_call x14, Pallas kernels, call(): pl.pallas_call(body, out_shape=outs, in_specs=in_specs, out_specs=jax.tre...  26 us
    ppermute x23, waiting for transfers between devices, exchanged(): return lax.ppermute(value, axis, pairs)  25.1 us
    ppermute x23, starting transfers between devices, exchanged(): return lax.ppermute(value, axis, pairs)  20.8 us
    unnamed x17, local copies, waits for them, and re-layouts  7.79 us
  transfers between devices with their start and end apart: 23, of which 10 were waited for; matrix products, arithmetic and copies ran while one was open for 6% of the time, Pallas kernels for 22%

profile of v1, /device:TPU:0, one launch (start us, length us, event | category | flops | bytes accessed | tf_op | source)
XLA Modules:
  0.0 85.6 jit_solution(6741090774529350206)
XLA Ops:
  0.0 2.9 %collective-permute-start = (bf16[4,4,2048]{2,1,0:T(4,128)(2,1)}, bf16[4,4,2048]{2,1,0:T(4,128)(2,1)S(1)}, u32[]{:S(2)}, u32[]{:S(2)}) collective-permute-start(bf16[4,4,2048]{2,1,0:T(4,128)(2,1)} %bitcast.27), channel_id=1, source_target_pairs={{0,4},{4,0},{8,12},{12,8},{16,20},{20,16},{24,28},{28,24},{1,5},{5... | collective-permute-start | bytes 196616 | tf_op jit(solution)/shard_map/ppermute | solution.py:53
  2.9 0.8 copy.27
  3.7 2.0 %collective-permute-start.1 = (s32[4,4,6]{2,1,0:T(4,128)}, s32[4,4,6]{2,1,0:T(4,128)S(1)}, u32[]{:S(2)}, u32[]{:S(2)}) collective-permute-start(s32[4,4,6]{2,1,0:T(4,128)} %bitcast.28), channel_id=1, source_target_pairs={{0,4},{4,0},{8,12},{12,8},{16,20},{20,16},{24,28},{28,24},{1,5},{5... | collective-permute-start | bytes 1160 | tf_op jit(solution)/shard_map/ppermute | solution.py:53
  5.7 0.9 %reshape_squeeze.6 = bf16[16,2048]{1,0:T(8,128)(2,1)S(1)} reshape(bf16[1,4,4,2048]{3,2,1,0:T(4,128)(2,1)} %param.14) | data formatting | bytes 131072 | tf_op jit(solution)/shard_map/reshape;squeeze | solution.py:432
  6.6 1.0 %reshape.21.tk = bf16[240,512]{1,0:T(8,128)(2,1)S(1)} reshape(bf16[60,4,512]{2,1,0:T(4,128)(2,1)} %bitcast.25) | data formatting | bytes 491520 | tf_op jit(solution)/shard_map/reshape | solution.py:444
  7.6 1.0 %reshape.22.tv = bf16[240,512]{1,0:T(8,128)(2,1)S(1)} reshape(bf16[60,4,512]{2,1,0:T(4,128)(2,1)} %bitcast.26) | data formatting | bytes 491520 | tf_op jit(solution)/shard_map/reshape | solution.py:445
  9.3 1.0 %copy.29.w_router = bf16[512,64]{1,0:T(8,128)(2,1)S(1)} copy(bf16[512,64]{0,1:T(8,128)(2,1)} %param.24) | data formatting | bytes 131072 | tf_op args[10]
  10.4 2.8 %copy-done = bf16[2048,3,512]{2,0,1:T(8,128)(2,1)S(1)} copy-done((bf16[2048,3,512]{2,0,1:T(8,128)(2,1)S(1)}, bf16[2048,3,512]{2,0,1:T(8,128)(2,1)}, u32[]{:S(2)}) %copy-start) | copy-done | bytes 6291480
  13.2 1.2 %copy-done.2 = bf16[1,1024,512]{2,1,0:T(8,128)(2,1)S(1)} copy-done((bf16[1,1024,512]{2,1,0:T(8,128)(2,1)S(1)}, bf16[1,1024,512]{2,1,0:T(8,128)(2,1)}, u32[]{:S(2)}) %copy-start.2) | copy-done | bytes 1048600
  14.4 1.2 %copy-done.3 = bf16[1,1024,512]{2,1,0:T(8,128)(2,1)S(1)} copy-done((bf16[1,1024,512]{2,1,0:T(8,128)(2,1)S(1)}, bf16[1,1024,512]{2,1,0:T(8,128)(2,1)}, u32[]{:S(2)}) %copy-start.3) | copy-done | bytes 1048600
  15.6 2.9 %shard_map.136.near = f32[32,640]{1,0:T(8,128)S(1)} custom-call(s32[1]{0:T(128)S(6)} %copy.30.parts, s32[8,4]{1,0:T(8,128)S(1)} %pad_add_fusion.1.par, bf16[32,2048]{1,0:T(8,128)(2,1)S(1)} %pad_maximum_fusion.x, bf16[3,2048,512]{2,1,0:T(8,128)(2,1)S(1)} %bitcast.21, bf16[1024,512]{1,0:T(8,128)(2,1)S(1)} %bitcast.22, bf16[1024,512]{1,0:T(8,128)(2,1)S(1)} %bitcast.23, ...), custom_call_target="tpu_custom_call" | custom-call | flops 201326592 | bytes 6291456 | tf_op jit(solution)/shard_map/pallas_call | solution.py:57
  18.6 0.7 broadcast_select_fusion.3
  19.3 3.7 %collective-permute-done.3.far = f32[32,640]{1,0:T(8,128)S(1)} collective-permute-done((f32[32,640]{1,0:T(8,128)S(1)}, f32[32,640]{1,0:T(8,128)S(1)}, u32[]{:S(2)}, u32[]{:S(2)}) %collective-permute-start.3) | collective-permute-done | bytes 81952 | tf_op jit(solution)/shard_map/ppermute | solution.py:53
  23.0 1.6 %copy-done.1 = bf16[512,2048]{1,0:T(8,128)(2,1)S(1)} copy-done((bf16[512,2048]{1,0:T(8,128)(2,1)S(1)}, bf16[512,2048]{1,0:T(8,128)(2,1)}, u32[]{:S(2)}) %copy-start.1) | copy-done | bytes 2097176
  24.6 0.6 shard_map.137
  25.2 1.6 %collective-permute-start.5 = (bf16[32,512]{1,0:T(8,128)(2,1)S(1)}, bf16[32,512]{1,0:T(8,128)(2,1)S(1)}, u32[]{:S(2)}, u32[]{:S(2)}) collective-permute-start(bf16[32,512]{1,0:T(8,128)(2,1)S(1)} %get-tuple-element.25), channel_id=1, source_target_pairs={{0,2},{1,3},{2,0},{3,1},{4,6},{5,7},{6,4},{7,5},{8,10},{9,11},{10,... | collective-permute-start | bytes 98312 | tf_op jit(solution)/shard_map/ppermute | solution.py:53
  26.8 0.3 collective-permute-start.6
  27.1 2.1 %collective-permute-done.5.rest_1_ = bf16[32,512]{1,0:T(8,128)(2,1)S(1)} collective-permute-done((bf16[32,512]{1,0:T(8,128)(2,1)S(1)}, bf16[32,512]{1,0:T(8,128)(2,1)S(1)}, u32[]{:S(2)}, u32[]{:S(2)}) %collective-permute-start.5) | collective-permute-done | bytes 32800 | tf_op jit(solution)/shard_map/ppermute | solution.py:53
  29.2 1.0 %collective-permute-done.6.rest_2_ = bf16[32,512]{1,0:T(8,128)(2,1)S(1)} collective-permute-done((bf16[32,512]{1,0:T(8,128)(2,1)S(1)}, bf16[32,512]{1,0:T(8,128)(2,1)S(1)}, u32[]{:S(2)}, u32[]{:S(2)}) %collective-permute-start.6) | collective-permute-done | bytes 32800 | tf_op jit(solution)/shard_map/ppermute | solution.py:53
  30.2 0.4 shard_map.138
  30.6 1.6 %collective-permute-start.7 = (bf16[32,640]{1,0:T(8,128)(2,1)S(1)}, bf16[32,640]{1,0:T(8,128)(2,1)S(1)}, u32[]{:S(2)}, u32[]{:S(2)}) collective-permute-start(bf16[32,640]{1,0:T(8,128)(2,1)S(1)} %get-tuple-element.28.refs_0_), channel_id=1, source_target_pairs={{0,8},{4,12},{8,0},{12,4},{16,24},{20,28},{24,16},{28,20},{1,9},{5... | collective-permute-start | bytes 122888 | tf_op jit(solution)/shard_map/ppermute | solution.py:53
  32.2 2.6 %collective-permute-start.8 = (bf16[32,640]{1,0:T(8,128)(2,1)S(1)}, bf16[32,640]{1,0:T(8,128)(2,1)S(1)}, u32[]{:S(2)}, u32[]{:S(2)}) collective-permute-start(bf16[32,640]{1,0:T(8,128)(2,1)S(1)} %get-tuple-element.28.refs_0_), channel_id=1, source_target_pairs={{0,16},{4,20},{8,24},{12,28},{16,0},{20,4},{24,8},{28,12},{1,17},{... | collective-permute-start | bytes 122888 | tf_op jit(solution)/shard_map/ppermute | solution.py:53
  34.8 0.2 collective-permute-start.9
  35.0 2.9 %collective-permute-done.8.refs_2_ = bf16[32,640]{1,0:T(8,128)(2,1)S(1)} collective-permute-done((bf16[32,640]{1,0:T(8,128)(2,1)S(1)}, bf16[32,640]{1,0:T(8,128)(2,1)S(1)}, u32[]{:S(2)}, u32[]{:S(2)}) %collective-permute-start.8) | collective-permute-done | bytes 40992 | tf_op jit(solution)/shard_map/ppermute | solution.py:53
  37.9 2.7 %collective-permute-done.9.refs_3_ = bf16[32,640]{1,0:T(8,128)(2,1)S(1)} collective-permute-done((bf16[32,640]{1,0:T(8,128)(2,1)S(1)}, bf16[32,640]{1,0:T(8,128)(2,1)S(1)}, u32[]{:S(2)}, u32[]{:S(2)}) %collective-permute-start.9) | collective-permute-done | bytes 40992 | tf_op jit(solution)/shard_map/ppermute | solution.py:53
  40.6 0.4 shard_map.139
  41.0 3.4 %shard_map.142 = bf16[48,2816]{1,0:T(8,128)(2,1)S(1)} custom-call(bf16[192,512]{1,0:T(8,128)(2,1)S(1)} %get-tuple-element.29.picked, bf16[8,512,2816]{2,1,0:T(8,128)(2,1)} %weights.10), custom_call_target="tpu_custom_call" | custom-call | flops 138412032 | bytes 5767168 | tf_op jit(solution)/shard_map/pallas_call | solution.py:57
  44.5 3.4 %shard_map.140 = bf16[48,2816]{1,0:T(8,128)(2,1)S(1)} custom-call(bf16[192,512]{1,0:T(8,128)(2,1)S(1)} %get-tuple-element.29.picked, bf16[8,512,2816]{2,1,0:T(8,128)(2,1)} %weights.10), custom_call_target="tpu_custom_call" | custom-call | flops 138412032 | bytes 5767168 | tf_op jit(solution)/shard_map/pallas_call | solution.py:57
  47.8 0.6 collective-permute-start.10
  48.4 3.4 %shard_map.143 = bf16[48,2816]{1,0:T(8,128)(2,1)S(1)} custom-call(bf16[192,512]{1,0:T(8,128)(2,1)S(1)} %get-tuple-element.29.picked, bf16[8,512,2816]{2,1,0:T(8,128)(2,1)} %weights.10, bf16[48,2816]{1,0:T(8,128)(2,1)S(1)} %collective-permute-done.11.refs_0_), custom_call_target="tpu_custom_call" | custom-call | flops 138412032 | bytes 5767168 | tf_op jit(solution)/shard_map/pallas_call | solution.py:57
  51.8 0.9 %collective-permute-start.12 = (bf16[48,2816]{1,0:T(8,128)(2,1)S(1)}, bf16[48,2816]{1,0:T(8,128)(2,1)S(1)}, u32[]{:S(2)}, u32[]{:S(2)}) collective-permute-start(bf16[48,2816]{1,0:T(8,128)(2,1)S(1)} %shard_map.143), channel_id=1, source_target_pairs={{0,2},{1,3},{2,0},{3,1},{4,6},{5,7},{6,4},{7,5},{8,10},{9,11},{10,... | collective-permute-start | bytes 811016 | tf_op jit(solution)/shard_map/ppermute | solution.py:53
  52.7 1.2 %collective-permute-start.14 = (f32[8,128]{1,0:T(8,128)S(1)}, f32[8,128]{1,0:T(8,128)S(1)}, u32[]{:S(2)}, u32[]{:S(2)}) collective-permute-start(f32[8,128]{1,0:T(8,128)S(1)} %get-tuple-element.31.stat0), channel_id=1, source_target_pairs={{0,2},{1,3},{2,0},{3,1},{4,6},{5,7},{6,4},{7,5},{8,10},{9,11},{10,... | collective-permute-start | bytes 12296 | tf_op jit(solution)/shard_map/ppermute | solution.py:53
  54.0 0.6 collective-permute-start.15
  54.6 4.1 %shard_map.141.near = f32[48,2816]{1,0:T(8,128)S(1)} custom-call(bf16[192,512]{1,0:T(8,128)(2,1)S(1)} %get-tuple-element.29.picked, bf16[8,512,2816]{2,1,0:T(8,128)(2,1)} %weights.10, bf16[48,2816]{1,0:T(8,128)(2,1)S(1)} %collective-permute-done.10.refs_0_), custom_call_target="tpu_custom_call" | custom-call | flops 138412032 | bytes 5767168 | tf_op jit(solution)/shard_map/pallas_call | solution.py:57
  58.7 1.7 %collective-permute-done.14.stat2 = f32[8,128]{1,0:T(8,128)S(1)} collective-permute-done((f32[8,128]{1,0:T(8,128)S(1)}, f32[8,128]{1,0:T(8,128)S(1)}, u32[]{:S(2)}, u32[]{:S(2)}) %collective-permute-start.14) | collective-permute-done | bytes 4128 | tf_op jit(solution)/shard_map/ppermute | solution.py:53
  60.4 0.3 shard_map.144
  60.7 0.9 %collective-permute-start.16 = (bf16[48,1408]{1,0:T(8,128)(2,1)S(1)}, bf16[48,1408]{1,0:T(8,128)(2,1)S(1)}, u32[]{:S(2)}, u32[]{:S(2)}) collective-permute-start(bf16[48,1408]{1,0:T(8,128)(2,1)S(1)} %get-tuple-element.34.refs_0_), channel_id=1, source_target_pairs={{0,2},{1,3},{2,0},{3,1},{4,6},{5,7},{6,4},{7,5},{8,10},{9,11},{10,... | collective-permute-start | bytes 405512 | tf_op jit(solution)/shard_map/ppermute | solution.py:53
  61.6 4.7 %collective-permute-done.16.refs_0_ = bf16[48,1408]{1,0:T(8,128)(2,1)S(1)} collective-permute-done((bf16[48,1408]{1,0:T(8,128)(2,1)S(1)}, bf16[48,1408]{1,0:T(8,128)(2,1)S(1)}, u32[]{:S(2)}, u32[]{:S(2)}) %collective-permute-start.16) | collective-permute-done | bytes 135200 | tf_op jit(solution)/shard_map/ppermute | solution.py:53
  66.4 3.5 %shard_map.145.refs_1_ = f32[128,512]{1,0:T(8,128)S(1)} custom-call(bf16[8,512,1408]{2,1,0:T(8,128)(2,1)S(1)} %bitcast.20, f32[8,128]{1,0:T(8,128)S(1)} %get-tuple-element.32.stats, f32[8,128]{1,0:T(8,128)S(1)} %get-tuple-element.30.target, f32[8,128]{1,0:T(8,128)S(1)} %get-tuple-element.33.choice, bf16[48,1408]{1,0:T(8,128)(2,1)S(1)} %get-tuple-element.34.refs_0_, ...), custom_call_target="tpu_custom_call" | custom-call | flops 138412032 | bytes 5767168 | tf_op jit(solution)/shard_map/pallas_call | solution.py:57
  69.8 1.9 %shard_map.146.refs_1_ = f32[128,512]{1,0:T(8,128)S(1)} custom-call(bf16[8,512,1408]{2,1,0:T(8,128)(2,1)S(1)} %bitcast.20, f32[8,128]{1,0:T(8,128)S(1)} %get-tuple-element.32.stats, f32[8,128]{1,0:T(8,128)S(1)} %get-tuple-element.30.target, f32[8,128]{1,0:T(8,128)S(1)} %get-tuple-element.33.choice, bf16[48,1408]{1,0:T(8,128)(2,1)S(1)} %collective-permute-done.16.refs_0_, ...), custom_call_target="tpu_custom_call" | custom-call | flops 69206016 | bytes 2883584 | tf_op jit(solution)/shard_map/pallas_call | solution.py:57
  71.7 1.9 %shard_map.147 = (f32[64,512]{1,0:T(8,128)S(1)}, bf16[64,512]{1,0:T(8,128)(2,1)S(1)}) custom-call(bf16[8,512,1408]{2,1,0:T(8,128)(2,1)S(1)} %bitcast.20, f32[8,128]{1,0:T(8,128)S(1)} %get-tuple-element.32.stats, f32[8,128]{1,0:T(8,128)S(1)} %get-tuple-element.30.target, f32[8,128]{1,0:T(8,128)S(1)} %get-tuple-element.33.choice, ...), custom_call_target="tpu_custom_call" | custom-call | flops 69206016 | bytes 2883584 | tf_op jit(solution)/shard_map/pallas_call | solution.py:57
  73.6 0.6 collective-permute-start.19
  74.2 4.0 %collective-permute-done.19.far = bf16[64,512]{1,0:T(8,128)(2,1)S(1)} collective-permute-done((bf16[64,512]{1,0:T(8,128)(2,1)S(1)}, bf16[64,512]{1,0:T(8,128)(2,1)S(1)}, u32[]{:S(2)}, u32[]{:S(2)}) %collective-permute-start.19) | collective-permute-done | bytes 65568 | tf_op jit(solution)/shard_map/ppermute | solution.py:53
  78.2 1.2 %collective-permute-start.21 = (bf16[16,512]{1,0:T(8,128)(2,1)S(1)}, bf16[16,512]{1,0:T(8,128)(2,1)S(1)}, u32[]{:S(2)}, u32[]{:S(2)}) collective-permute-start(bf16[16,512]{1,0:T(8,128)(2,1)S(1)} %get-tuple-element.39), channel_id=1, source_target_pairs={{0,16},{4,20},{8,24},{12,28},{16,0},{20,4},{24,8},{28,12},{1,17},{... | collective-permute-start | bytes 49160 | tf_op jit(solution)/shard_map/ppermute | solution.py:53
  79.5 3.1 %collective-permute-start.22 = (bf16[16,512]{1,0:T(8,128)(2,1)S(1)}, bf16[16,512]{1,0:T(8,128)(2,1)S(1)}, u32[]{:S(2)}, u32[]{:S(2)}) collective-permute-start(bf16[16,512]{1,0:T(8,128)(2,1)S(1)} %get-tuple-element.40), channel_id=1, source_target_pairs={{0,24},{4,28},{8,16},{12,20},{16,8},{20,12},{24,0},{28,4},{1,25},{... | collective-permute-start | bytes 49160 | tf_op jit(solution)/shard_map/ppermute | solution.py:53
  82.6 0.4 collective-permute-done.21.rest_1_
  83.0 2.0 %collective-permute-done.22.rest_2_ = bf16[16,512]{1,0:T(8,128)(2,1)S(1)} collective-permute-done((bf16[16,512]{1,0:T(8,128)(2,1)S(1)}, bf16[16,512]{1,0:T(8,128)(2,1)S(1)}, u32[]{:S(2)}, u32[]{:S(2)}) %collective-permute-start.22) | collective-permute-done | bytes 16416 | tf_op jit(solution)/shard_map/ppermute | solution.py:53
  85.0 0.6 reshape.23
  (42 shorter events, 0.5 us)
Async XLA Ops:
  0.0 30.1 %copy-start.4 = (f32[512]{0:T(512)S(1)}, f32[512]{0:T(512)}, u32[]{:S(2)}) copy-start(f32[512]{0:T(512)} %param.25) | copy-start | bytes 6148
  0.0 10.3 %collective-permute-start = (bf16[4,4,2048]{2,1,0:T(4,128)(2,1)}, bf16[4,4,2048]{2,1,0:T(4,128)(2,1)S(1)}, u32[]{:S(2)}, u32[]{:S(2)}) collective-permute-start(bf16[4,4,2048]{2,1,0:T(4,128)(2,1)} %bitcast.27), channel_id=1, source_target_pairs={{0,4},{4,0},{8,12},{12,8},{16,20},{20,16},{24,28},{28,24},{1,5},{5... | collective-permute-start | bytes 196616 | tf_op jit(solution)/shard_map/ppermute | solution.py:53
  3.7 6.5 %collective-permute-start.2 = (s32[4,4]{0,1:T(4,128)S(1)}, s32[4,4]{0,1:T(4,128)S(1)}, u32[]{:S(2)}, u32[]{:S(2)}) collective-permute-start(s32[4,4]{0,1:T(4,128)S(1)} %copy.27), channel_id=1, source_target_pairs={{0,4},{4,0},{8,12},{12,8},{16,20},{20,16},{24,28},{28,24},{1,5},{5... | collective-permute-start | bytes 200 | tf_op jit(solution)/shard_map/ppermute | solution.py:53
  3.7 14.9 %collective-permute-start.1 = (s32[4,4,6]{2,1,0:T(4,128)}, s32[4,4,6]{2,1,0:T(4,128)S(1)}, u32[]{:S(2)}, u32[]{:S(2)}) collective-permute-start(s32[4,4,6]{2,1,0:T(4,128)} %bitcast.28), channel_id=1, source_target_pairs={{0,4},{4,0},{8,12},{12,8},{16,20},{20,16},{24,28},{28,24},{1,5},{5... | collective-permute-start | bytes 1160 | tf_op jit(solution)/shard_map/ppermute | solution.py:53
  10.4 2.8 %copy-start = (bf16[2048,3,512]{2,0,1:T(8,128)(2,1)S(1)}, bf16[2048,3,512]{2,0,1:T(8,128)(2,1)}, u32[]{:S(2)}) copy-start(bf16[2048,3,512]{2,0,1:T(8,128)(2,1)} %param.17) | copy-start | bytes 18874372
  13.2 1.2 %copy-start.2 = (bf16[1,1024,512]{2,1,0:T(8,128)(2,1)S(1)}, bf16[1,1024,512]{2,1,0:T(8,128)(2,1)}, u32[]{:S(2)}) copy-start(bf16[1,1024,512]{2,1,0:T(8,128)(2,1)} %param.19) | copy-start | bytes 3145732
  14.4 1.2 %copy-start.3 = (bf16[1,1024,512]{2,1,0:T(8,128)(2,1)S(1)}, bf16[1,1024,512]{2,1,0:T(8,128)(2,1)}, u32[]{:S(2)}) copy-start(bf16[1,1024,512]{2,1,0:T(8,128)(2,1)} %param.20) | copy-start | bytes 3145732
  18.5 4.5 %collective-permute-start.3 = (f32[32,640]{1,0:T(8,128)S(1)}, f32[32,640]{1,0:T(8,128)S(1)}, u32[]{:S(2)}, u32[]{:S(2)}) collective-permute-start(f32[32,640]{1,0:T(8,128)S(1)} %shard_map.136.near), channel_id=1, source_target_pairs={{0,4},{4,0},{8,12},{12,8},{16,20},{20,16},{24,28},{28,24},{1,5},{5... | collective-permute-start | bytes 245768 | tf_op jit(solution)/shard_map/ppermute | solution.py:53
  23.0 1.6 %copy-start.1 = (bf16[512,2048]{1,0:T(8,128)(2,1)S(1)}, bf16[512,2048]{1,0:T(8,128)(2,1)}, u32[]{:S(2)}) copy-start(bf16[512,2048]{1,0:T(8,128)(2,1)} %w_out.1) | copy-start | bytes 6291460
  25.2 1.9 %collective-permute-start.4 = (bf16[32,512]{1,0:T(8,128)(2,1)S(1)}, bf16[32,512]{1,0:T(8,128)(2,1)S(1)}, u32[]{:S(2)}, u32[]{:S(2)}) collective-permute-start(bf16[32,512]{1,0:T(8,128)(2,1)S(1)} %get-tuple-element.24), channel_id=1, source_target_pairs={{0,1},{1,0},{2,3},{3,2},{4,5},{5,4},{6,7},{7,6},{8,9},{9,8},{10,11... | collective-permute-start | bytes 98312 | tf_op jit(solution)/shard_map/ppermute | solution.py:53
  25.2 4.0 %collective-permute-start.5 = (bf16[32,512]{1,0:T(8,128)(2,1)S(1)}, bf16[32,512]{1,0:T(8,128)(2,1)S(1)}, u32[]{:S(2)}, u32[]{:S(2)}) collective-permute-start(bf16[32,512]{1,0:T(8,128)(2,1)S(1)} %get-tuple-element.25), channel_id=1, source_target_pairs={{0,2},{1,3},{2,0},{3,1},{4,6},{5,7},{6,4},{7,5},{8,10},{9,11},{10,... | collective-permute-start | bytes 98312 | tf_op jit(solution)/shard_map/ppermute | solution.py:53
  26.8 3.3 %collective-permute-start.6 = (bf16[32,512]{1,0:T(8,128)(2,1)S(1)}, bf16[32,512]{1,0:T(8,128)(2,1)S(1)}, u32[]{:S(2)}, u32[]{:S(2)}) collective-permute-start(bf16[32,512]{1,0:T(8,128)(2,1)S(1)} %get-tuple-element.26), channel_id=1, source_target_pairs={{0,3},{1,2},{2,1},{3,0},{4,7},{5,6},{6,5},{7,4},{8,11},{9,10},{10,... | collective-permute-start | bytes 98312 | tf_op jit(solution)/shard_map/ppermute | solution.py:53
  30.6 4.4 %collective-permute-start.7 = (bf16[32,640]{1,0:T(8,128)(2,1)S(1)}, bf16[32,640]{1,0:T(8,128)(2,1)S(1)}, u32[]{:S(2)}, u32[]{:S(2)}) collective-permute-start(bf16[32,640]{1,0:T(8,128)(2,1)S(1)} %get-tuple-element.28.refs_0_), channel_id=1, source_target_pairs={{0,8},{4,12},{8,0},{12,4},{16,24},{20,28},{24,16},{28,20},{1,9},{5... | collective-permute-start | bytes 122888 | tf_op jit(solution)/shard_map/ppermute | solution.py:53
  32.2 5.7 %collective-permute-start.8 = (bf16[32,640]{1,0:T(8,128)(2,1)S(1)}, bf16[32,640]{1,0:T(8,128)(2,1)S(1)}, u32[]{:S(2)}, u32[]{:S(2)}) collective-permute-start(bf16[32,640]{1,0:T(8,128)(2,1)S(1)} %get-tuple-element.28.refs_0_), channel_id=1, source_target_pairs={{0,16},{4,20},{8,24},{12,28},{16,0},{20,4},{24,8},{28,12},{1,17},{... | collective-permute-start | bytes 122888 | tf_op jit(solution)/shard_map/ppermute | solution.py:53
  34.8 5.8 %collective-permute-start.9 = (bf16[32,640]{1,0:T(8,128)(2,1)S(1)}, bf16[32,640]{1,0:T(8,128)(2,1)S(1)}, u32[]{:S(2)}, u32[]{:S(2)}) collective-permute-start(bf16[32,640]{1,0:T(8,128)(2,1)S(1)} %get-tuple-element.28.refs_0_), channel_id=1, source_target_pairs={{0,24},{4,28},{8,16},{12,20},{16,8},{20,12},{24,0},{28,4},{1,25},{... | collective-permute-start | bytes 122888 | tf_op jit(solution)/shard_map/ppermute | solution.py:53
  44.4 4.0 %collective-permute-start.11 = (bf16[48,2816]{1,0:T(8,128)(2,1)S(1)}, bf16[48,2816]{1,0:T(8,128)(2,1)S(1)}, u32[]{:S(2)}, u32[]{:S(2)}) collective-permute-start(bf16[48,2816]{1,0:T(8,128)(2,1)S(1)} %shard_map.142), channel_id=1, source_target_pairs={{0,1},{1,0},{2,3},{3,2},{4,5},{5,4},{6,7},{7,6},{8,9},{9,8},{10,11... | collective-permute-start | bytes 811016 | tf_op jit(solution)/shard_map/ppermute | solution.py:53
  47.8 6.7 %collective-permute-start.10 = (bf16[48,2816]{1,0:T(8,128)(2,1)S(1)}, bf16[48,2816]{1,0:T(8,128)(2,1)S(1)}, u32[]{:S(2)}, u32[]{:S(2)}) collective-permute-start(bf16[48,2816]{1,0:T(8,128)(2,1)S(1)} %shard_map.140), channel_id=1, source_target_pairs={{0,1},{1,0},{2,3},{3,2},{4,5},{5,4},{6,7},{7,6},{8,9},{9,8},{10,11... | collective-permute-start | bytes 811016 | tf_op jit(solution)/shard_map/ppermute | solution.py:53
  51.8 8.6 %collective-permute-start.12 = (bf16[48,2816]{1,0:T(8,128)(2,1)S(1)}, bf16[48,2816]{1,0:T(8,128)(2,1)S(1)}, u32[]{:S(2)}, u32[]{:S(2)}) collective-permute-start(bf16[48,2816]{1,0:T(8,128)(2,1)S(1)} %shard_map.143), channel_id=1, source_target_pairs={{0,2},{1,3},{2,0},{3,1},{4,6},{5,7},{6,4},{7,5},{8,10},{9,11},{10,... | collective-permute-start | bytes 811016 | tf_op jit(solution)/shard_map/ppermute | solution.py:53
  52.7 13.6 %slice-start = ((s8[11534336]{0:T(1024)(128)(4,1)}), s8[4194304]{0:T(1024)(128)(4,1)S(1)}, s32[]{:S(2)}) async-start(s8[11534336]{0:T(1024)(128)(4,1)} %bitcast.19), calls=%async_computation | async-start | bytes 8388608
  52.7 13.6 %slice-start.1 = ((s8[11534336]{0:T(1024)(128)(4,1)}), s8[4194304]{0:T(1024)(128)(4,1)S(1)}, s32[]{:S(2)}) async-start(s8[11534336]{0:T(1024)(128)(4,1)} %bitcast.19), calls=%async_computation.1 | async-start | bytes 8388608
  52.7 13.6 %slice-start.2 = ((s8[11534336]{0:T(1024)(128)(4,1)}), s8[3145728]{0:T(1024)(128)(4,1)S(1)}, s32[]{:S(2)}) async-start(s8[11534336]{0:T(1024)(128)(4,1)} %bitcast.19), calls=%async_computation.2 | async-start | bytes 6291456
  52.7 6.0 %collective-permute-start.13 = (f32[8,128]{1,0:T(8,128)S(1)}, f32[8,128]{1,0:T(8,128)S(1)}, u32[]{:S(2)}, u32[]{:S(2)}) collective-permute-start(f32[8,128]{1,0:T(8,128)S(1)} %get-tuple-element.31.stat0), channel_id=1, source_target_pairs={{0,1},{1,0},{2,3},{3,2},{4,5},{5,4},{6,7},{7,6},{8,9},{9,8},{10,11... | collective-permute-start | bytes 12296 | tf_op jit(solution)/shard_map/ppermute | solution.py:53
  52.7 7.7 %collective-permute-start.14 = (f32[8,128]{1,0:T(8,128)S(1)}, f32[8,128]{1,0:T(8,128)S(1)}, u32[]{:S(2)}, u32[]{:S(2)}) collective-permute-start(f32[8,128]{1,0:T(8,128)S(1)} %get-tuple-element.31.stat0), channel_id=1, source_target_pairs={{0,2},{1,3},{2,0},{3,1},{4,6},{5,7},{6,4},{7,5},{8,10},{9,11},{10,... | collective-permute-start | bytes 12296 | tf_op jit(solution)/shard_map/ppermute | solution.py:53
  54.0 6.4 %collective-permute-start.15 = (f32[8,128]{1,0:T(8,128)S(1)}, f32[8,128]{1,0:T(8,128)S(1)}, u32[]{:S(2)}, u32[]{:S(2)}) collective-permute-start(f32[8,128]{1,0:T(8,128)S(1)} %get-tuple-element.31.stat0), channel_id=1, source_target_pairs={{0,3},{1,2},{2,1},{3,0},{4,7},{5,6},{6,5},{7,4},{8,11},{9,10},{10,... | collective-permute-start | bytes 12296 | tf_op jit(solution)/shard_map/ppermute | solution.py:53
  60.7 5.7 %collective-permute-start.16 = (bf16[48,1408]{1,0:T(8,128)(2,1)S(1)}, bf16[48,1408]{1,0:T(8,128)(2,1)S(1)}, u32[]{:S(2)}, u32[]{:S(2)}) collective-permute-start(bf16[48,1408]{1,0:T(8,128)(2,1)S(1)} %get-tuple-element.34.refs_0_), channel_id=1, source_target_pairs={{0,2},{1,3},{2,0},{3,1},{4,6},{5,7},{6,4},{7,5},{8,10},{9,11},{10,... | collective-permute-start | bytes 405512 | tf_op jit(solution)/shard_map/ppermute | solution.py:53
  61.6 4.7 %collective-permute-start.18 = (bf16[48,1408]{1,0:T(8,128)(2,1)S(1)}, bf16[48,1408]{1,0:T(8,128)(2,1)S(1)}, u32[]{:S(2)}, u32[]{:S(2)}) collective-permute-start(bf16[48,1408]{1,0:T(8,128)(2,1)S(1)} %get-tuple-element.34.refs_0_), channel_id=1, source_target_pairs={{0,1},{1,0},{2,3},{3,2},{4,5},{5,4},{6,7},{7,6},{8,9},{9,8},{10,11... | collective-permute-start | bytes 405512 | tf_op jit(solution)/shard_map/ppermute | solution.py:53
  66.3 5.4 %collective-permute-start.17 = (bf16[48,1408]{1,0:T(8,128)(2,1)S(1)}, bf16[48,1408]{1,0:T(8,128)(2,1)S(1)}, u32[]{:S(2)}, u32[]{:S(2)}) collective-permute-start(bf16[48,1408]{1,0:T(8,128)(2,1)S(1)} %collective-permute-done.16.refs_0_), channel_id=1, source_target_pairs={{0,1},{1,0},{2,3},{3,2},{4,5},{5,4},{6,7},{7,6},{8,9},{9,8},{10,11... | collective-permute-start | bytes 405512 | tf_op jit(solution)/shard_map/ppermute | solution.py:53
  73.6 4.6 %collective-permute-start.19 = (bf16[64,512]{1,0:T(8,128)(2,1)S(1)}, bf16[64,512]{1,0:T(8,128)(2,1)S(1)}, u32[]{:S(2)}, u32[]{:S(2)}) collective-permute-start(bf16[64,512]{1,0:T(8,128)(2,1)S(1)} %get-tuple-element.36), channel_id=1, source_target_pairs={{0,4},{4,0},{8,12},{12,8},{16,20},{20,16},{24,28},{28,24},{1,5},{5... | collective-permute-start | bytes 196616 | tf_op jit(solution)/shard_map/ppermute | solution.py:53
  78.2 4.5 %collective-permute-start.20 = (bf16[16,512]{1,0:T(8,128)(2,1)S(1)}, bf16[16,512]{1,0:T(8,128)(2,1)S(1)}, u32[]{:S(2)}, u32[]{:S(2)}) collective-permute-start(bf16[16,512]{1,0:T(8,128)(2,1)S(1)} %get-tuple-element.38), channel_id=1, source_target_pairs={{0,8},{4,12},{8,0},{12,4},{16,24},{20,28},{24,16},{28,20},{1,9},{5... | collective-permute-start | bytes 49160 | tf_op jit(solution)/shard_map/ppermute | solution.py:53
  78.2 4.7 %collective-permute-start.21 = (bf16[16,512]{1,0:T(8,128)(2,1)S(1)}, bf16[16,512]{1,0:T(8,128)(2,1)S(1)}, u32[]{:S(2)}, u32[]{:S(2)}) collective-permute-start(bf16[16,512]{1,0:T(8,128)(2,1)S(1)} %get-tuple-element.39), channel_id=1, source_target_pairs={{0,16},{4,20},{8,24},{12,28},{16,0},{20,4},{24,8},{28,12},{1,17},{... | collective-permute-start | bytes 49160 | tf_op jit(solution)/shard_map/ppermute | solution.py:53
  79.5 5.5 %collective-permute-start.22 = (bf16[16,512]{1,0:T(8,128)(2,1)S(1)}, bf16[16,512]{1,0:T(8,128)(2,1)S(1)}, u32[]{:S(2)}, u32[]{:S(2)}) collective-permute-start(bf16[16,512]{1,0:T(8,128)(2,1)S(1)} %get-tuple-element.40), channel_id=1, source_target_pairs={{0,24},{4,28},{8,16},{12,20},{16,8},{20,12},{24,0},{28,4},{1,25},{... | collective-permute-start | bytes 49160 | tf_op jit(solution)/shard_map/ppermute | solution.py:53

commit v2 on v1

v2 whole, which is shorter than its diff:
```python
import functools

import jax
import jax.numpy as jnp
from jax import lax
from jax.experimental import pallas as pl
from jax.experimental.pallas import tpu as pltpu
from jax.sharding import PartitionSpec as P

HDIM = 128
EXPERTS = 64
FFE = 1408
TOPK = 6
BEAMS = 8
STEPS = 4
CAP_E = 3
HALF = 4
PREV = 60
LANES = 128
MODEL = 2048
ROWS = STEPS * HALF
PAIR = 2 * ROWS
STATS = 1 + TOPK

NEGATIVE = -1e30
EPSILON = 1e-06
MIB = 1024 * 1024
BF = jnp.bfloat16
HINT = 10**10
F32 = jnp.float32

VMEM = pl.BlockSpec(memory_space=pltpu.VMEM)
SMEM = pl.BlockSpec(memory_space=pltpu.SMEM)
ANY = pl.BlockSpec(memory_space=pl.ANY)


def iota(shape, dim):
    return lax.broadcasted_iota(jnp.int32, shape, dim)


def dot(a, b):
    return jnp.dot(a, b, preferred_element_type=F32)


def dot_t(a, b):
    return lax.dot_general(a, b, (((1,), (1,)), ((), ())), preferred_element_type=F32)


def t_dot(a, b):
    return lax.dot_general(a, b, (((0,), (0,)), ((), ())), preferred_element_type=F32)


def exchanged(value, axis, mask):
    pairs = [(source, source ^ mask) for source in range(lax.axis_size(axis))]
    return lax.ppermute(value, axis, pairs)


def call(body, outs, in_specs, *args, after=(), scratch=(), limit=8, flops=0, nbytes=0):
    count = len(args)

    def ordered(*refs):
        body(*refs[:count], *refs[count + len(after) :])

    return pl.pallas_call(
        ordered if after else body,
        out_shape=outs,
        in_specs=list(in_specs) + [ANY] * len(after),
        out_specs=jax.tree.map(lambda _: VMEM, outs),
        scratch_shapes=list(scratch),
        compiler_params=pltpu.CompilerParams(vmem_limit_bytes=limit * MIB),
        cost_estimate=pl.CostEstimate(flops=flops, bytes_accessed=nbytes, transcendentals=0),
    )(*args, *after)


def shape(dims, dtype):
    return jax.ShapeDtypeStruct(tuple(dims), dtype)


def columns_kernel(order, tail_at, new_at):
    half = lax.axis_index("grp") % 2
    to_row = iota(order.shape, 0)
    wanted = (to_row % ROWS // HALF) * BEAMS + (to_row // ROWS) * HALF + to_row % HALF
    order[...] = (iota(order.shape, 1) == wanted).astype(BF)
    column = iota(tail_at.shape, 1)
    tail_at[...] = (iota(tail_at.shape, 0) == half * HALF + column % HALF).astype(BF)
    column = iota(new_at.shape, 1)
    beam = (column // ROWS) * HALF + column % HALF
    place = BEAMS + BEAMS * (column % ROWS // HALF) + beam
    here = (iota(new_at.shape, 0) == place) & (column // ROWS == half)
    new_at[...] = here.astype(BF)


def slot_rows(source):
    return jnp.concatenate([source[step].astype(F32) for step in range(STEPS)], axis=0)


def in_order(first, own, far):
    return jnp.concatenate([jnp.where(first, own, far), jnp.where(first, far, own)], axis=0)


def pieces(value, count):
    out = []
    for _ in range(count - 1):
        out.append(value.astype(BF).astype(F32))
        value = value - out[-1]
    return out + [value]


def attend_kernel(
    parts,
    order,
    tail_at,
    new_at,
    par_own,
    par_far,
    routes,
    x_own,
    x_far,
    wqkv,
    kp,
    vp,
    tk_raw,
    tv_raw,
    out,
    x_out,
):
    half = lax.axis_index("grp") % 2
    width = wqkv.shape[2]
    heads = width // HDIM
    x_all = in_order(half == 0, slot_rows(x_own), slot_rows(x_far))
    rows = x_all.astype(BF)
    features = x_out.shape[1]
    me = lax.axis_index("exp")
    mine = jnp.zeros((PAIR, features), F32)
    for k in range(x_all.shape[1] // features):
        mine = jnp.where(me == k, x_all[:, k * features : (k + 1) * features], mine)
    x_out[...] = mine
    query = dot(rows, wqkv[0]).astype(BF)
    key_new = dot(rows, wqkv[1]).astype(BF)
    value_new = dot(rows, wqkv[2]).astype(BF)
    lane = iota((BEAMS, LANES), 1)
    beam = iota((BEAMS, LANES), 0)
    state = (lane == beam).astype(F32)
    states = []
    same = iota((HALF, HALF), 0) == iota((HALF, HALF), 1)
    for step in range(STEPS):
        columns = [
            jnp.sum(
                jnp.where(same, source[step : step + 1, :].astype(F32), 0.0),
                axis=1,
                keepdims=True,
            )
            for source in (par_own, par_far)
        ]
        parent = in_order(half == 0, *columns)
        taken = jnp.zeros((BEAMS, LANES), F32)
        for j in range(BEAMS):
            taken = taken + jnp.where(parent == float(j), state[j : j + 1, :], 0.0)
        state = jnp.where(lane == BEAMS + BEAMS * step + beam, 1.0, taken)
        states.append(state)
    held = jnp.concatenate(states, axis=0).astype(BF)
    held = dot(order[...], held).astype(BF)
    tail_mask = dot(held, tail_at[...]) > 0.5
    new_mask = dot(held, new_at[...]) > 0.5
    tk = tk_raw[...].reshape(PREV * HALF, width)
    tv = tv_raw[...].reshape(PREV * HALF, width)
    cap = kp.shape[0]
    live = iota((PAIR, cap), 1) < parts[0]
    scale = HDIM ** (-0.5)
    info = jnp.zeros((PAIR, LANES), F32)
    info_lane = iota((PAIR, LANES), 1)
    own_rows = iota((PAIR, LANES), 0) // ROWS == half
    named = slot_rows(routes)
    named = jnp.concatenate([named, named], axis=0)
    for k in range(TOPK):
        info = jnp.where((info_lane == 5 * heads + k) & own_rows, named[:, k : k + 1], info)
    for head in range(heads):
        at = slice(head * HDIM, (head + 1) * HDIM)
        q = query[:, at]
        s_p = jnp.where(live, dot_t(q, kp[:, at]) * scale, NEGATIVE)
        s_t = jnp.where(tail_mask, dot_t(q, tk[:, at]) * scale, NEGATIVE)
        s_n = jnp.where(new_mask, dot_t(q, key_new[:, at]) * scale, NEGATIVE)
        top = jnp.maximum(
            jnp.max(s_p, axis=1, keepdims=True),
            jnp.maximum(
                jnp.max(s_t, axis=1, keepdims=True), jnp.max(s_n, axis=1, keepdims=True)
            ),
        )
        p_p = jnp.exp(s_p - top)
        p_t = jnp.exp(s_t - top)
        p_n = jnp.exp(s_n - top)
        total = (
            jnp.sum(p_p, axis=1, keepdims=True)
            + jnp.sum(p_t, axis=1, keepdims=True)
            + jnp.sum(p_n, axis=1, keepdims=True)
        )
        mix = (
            dot(p_p.astype(BF), vp[:, at])
            + dot(p_t.astype(BF), tv[:, at])
            + dot(p_n.astype(BF), value_new[:, at])
        )
        out[:, at] = mix.astype(BF)
        for k, column in enumerate(pieces(top, 3) + pieces(total, 2)):
            info = jnp.where(info_lane == k * heads + head, column, info)
    out[:, width:] = info.astype(BF)


def project_kernel(near, far, w_out, *outs):
    me = lax.axis_index("exp")
    width = w_out.shape[0]
    heads = width // HDIM
    parts = []
    infos = [side[:, width:].astype(F32) for side in (near, far)]
    for head in range(heads):
        at = slice(head * HDIM, (head + 1) * HDIM)
        columns = [
            [info[:, k * heads + head : k * heads + head + 1] for k in range(5)] for info in infos
        ]
        (m_near, l_near), (m_far, l_far) = [
            ((c[0] + c[1]) + c[2], c[3] + c[4]) for c in columns
        ]
        top = jnp.maximum(m_near, m_far)
        f_near = jnp.exp(m_near - top)
        f_far = jnp.exp(m_far - top)
        total = l_near * f_near + l_far * f_far
        mix = near[:, at].astype(F32) * f_near + far[:, at].astype(F32) * f_far
        parts.append((mix / total).astype(BF))
    attention = jnp.concatenate(parts, axis=1)
    features = outs[0].shape[1]
    for k, out in enumerate(outs):
        start = pl.multiple_of((me ^ k) * features, LANES)
        out[...] = dot(attention, w_out[:, pl.ds(start, features)]).astype(out.dtype)


def residual_kernel(x, gain, w_router, near, far, own, *rest):
    others, (residual_out, message) = rest[:-2], rest[-2:]
    features = own.shape[1]
    width = near.shape[1] - LANES
    named = near[:, width:].astype(F32) + far[:, width:].astype(F32)
    routes_at = 5 * (width // HDIM)
    residual = x[...] + own[...]
    for other in others:
        residual = residual + other[...].astype(F32)
    residual_out[...] = residual
    rows = (residual * gain[...]).astype(BF)
    message[:, :features] = rows
    logits = dot_t(rows, w_router[...])
    expert = iota(logits.shape, 1).astype(F32)
    lane = iota((PAIR, LANES), 1)
    info = jnp.zeros((PAIR, LANES), F32)
    columns = [jnp.sum(residual * residual, axis=1, keepdims=True)]
    for k in range(TOPK):
        route = named[:, routes_at + k : routes_at + k + 1]
        columns.append(jnp.sum(jnp.where(expert == route, logits, 0.0), axis=1, keepdims=True))
        info = jnp.where(lane == 2 * STATS + k, route, info)
    for at, column in enumerate(columns):
        high = column.astype(BF).astype(F32)
        info = jnp.where(lane == at, high, info)
        info = jnp.where(lane == STATS + at, column - high, info)
    message[:, features:] = info.astype(BF)


def gather_kernel(local, *refs):
    messages, (picked, stats, target, choice, rows) = refs[:-5], refs[-5:]
    blocks = len(messages)
    tokens = blocks * PAIR
    features = rows.shape[1]
    infos = []
    for k, message in enumerate(messages):
        rows[k * PAIR : (k + 1) * PAIR, :] = message[:, :features]
        infos.append(message[:, features:].astype(F32))
    info = jnp.concatenate(infos, axis=0).T
    stats[...] = jnp.concatenate(
        [info[:STATS] + info[STATS : 2 * STATS], jnp.zeros((8 - STATS, tokens), F32)], axis=0
    )
    first = (lax.axis_index("grp") * local).astype(F32)
    expert = iota((8, tokens), 0).astype(F32)
    chosen = jnp.full((8, tokens), -1.0, F32)
    for k in range(TOPK):
        route = info[2 * STATS + k : 2 * STATS + k + 1] - first
        chosen = jnp.where((route == expert) & (expert < local), float(k), chosen)
    choice[...] = chosen
    named = chosen >= 0.0
    before = iota((tokens, tokens), 0)
    after = iota((tokens, tokens), 1)
    earlier = ((before < after) & (before // ROWS == after // ROWS)).astype(BF)
    rank = dot(named.astype(BF), earlier)
    slot = (iota((8, tokens), 1) // ROWS).astype(F32)
    goal = jnp.where(named, slot * CAP_E + rank, -1.0)
    target[...] = goal
    capacity = picked.shape[1]
    row = iota((capacity, tokens), 0).astype(F32)
    places = [(row == goal[e : e + 1]).astype(F32) for e in range(local)]
    result = dot(jnp.concatenate(places, axis=0).astype(BF), rows[...])
    for e in range(local):
        picked[e] = result[e * capacity : (e + 1) * capacity].astype(BF)


def split_rows(value, rows):
    high = value[:STATS].astype(BF).astype(F32)
    low = value[:STATS] - high
    rest = jnp.zeros((rows - 2 * STATS, value.shape[1]), F32)
    return jnp.concatenate([high, low, rest], axis=0).astype(BF)


def joined_rows(value):
    value = value.astype(F32)
    high, low = value[:STATS], value[STATS : 2 * STATS]
    return jnp.concatenate([high + low, jnp.zeros((8 - STATS, value.shape[1]), F32)], axis=0)


def gate_kernel(places, block, with_stats, count, weights, picked, *refs):
    if with_stats:
        stats, refs = refs[0], refs[1:]
    far, outs = refs[:count], refs[count:]
    me = lax.axis_index("exp")
    width = weights.shape[2]
    for i, (mask, pick) in enumerate(places):
        at = (me ^ mask) * block + pick
        result = dot(picked[at], weights[at])
        if far:
            result = result + far[i][:, :width].astype(F32)
        outs[i][:, :width] = result.astype(outs[i].dtype)
    if with_stats:
        value = stats[...]
        if far:
            value = value + joined_rows(far[0][:, width:])
            outs[-1][...] = value
        outs[0][:, width:] = split_rows(value, outs[0].shape[0])


def gate_block(places, weights, picked, block, stats=(), far=(), dtypes=(BF,), after=(), flops=0):
    capacity, depth = picked.shape[1:]
    width = weights.shape[2]
    outs = [shape((capacity, width), dtype) for dtype in dtypes]
    if stats:
        outs[0] = shape((capacity, width + stats[0].shape[1]), BF)
        if far:
            outs.append(shape(stats[0].shape, F32))
    return call(
        functools.partial(gate_kernel, places, block, bool(stats), len(far)),
        tuple(outs),
        [VMEM] * (2 + len(stats) + len(far)),
        weights,
        picked,
        *stats,
        *far,
        after=after,
        flops=flops,
    )


def place_kernel(local, target, choice, stats, far, high, low):
    stats = stats[...] + joined_rows(far[:, far.shape[1] - target.shape[1] :])
    inverse = lax.rsqrt(stats[0:1] / MODEL + EPSILON)
    logits = [stats[1 + k : 2 + k] * inverse for k in range(TOPK)]
    top = functools.reduce(jnp.maximum, logits)
    weights = [jnp.exp(logit - top) for logit in logits]
    whole = functools.reduce(lambda a, b: a + b, weights)
    chosen = choice[...]
    share = jnp.zeros(chosen.shape, F32)
    for k in range(TOPK):
        share = jnp.where(chosen == float(k), weights[k] / whole, share)
    row = iota(high.shape[1:], 0).astype(F32)
    for e in range(local):
        place = jnp.where(row == target[e : e + 1, :], share[e : e + 1], 0.0)
        rounded = place.astype(BF)
        high[e] = rounded
        low[e] = (place - rounded.astype(F32)).astype(BF)


def hidden_kernel(block, pick, near, mid, far, target, stats, far_stats, hidden):
    capacity = near.shape[0]
    stats = stats[...] + joined_rows(far_stats[:, far_stats.shape[1] - target.shape[1] :])
    inverse = lax.rsqrt(stats[0:1] / MODEL + EPSILON)
    goal = target[pl.ds(lax.axis_index("exp") * block + pick, 1), :]
    row = iota((capacity, target.shape[1]), 0).astype(F32)
    scale = jnp.sum(jnp.where(row == goal, inverse, 0.0), axis=1, keepdims=True)
    half = near.shape[1] // 2
    gate = near[:, :half] + mid[:, :half].astype(F32) + far[:, :half].astype(F32)
    up = near[:, half:] + mid[:, half:].astype(F32) + far[:, half : 2 * half].astype(F32)
    gate, up = gate * scale, up * scale
    hidden[...] = (gate / (1.0 + jnp.exp(-gate)) * up).astype(BF)


def down_kernel(places, block, last, count, weights, high, low, *refs):
    hiddens, refs = refs[: len(places)], refs[len(places) :]
    before, refs = refs[:count], refs[count:]
    me = lax.axis_index("exp")
    mixed = before[0][...] if before else 0.0
    for hidden, (mask, pick) in zip(hiddens, places):
        at = (me ^ mask) * block + pick
        result = dot_t(hidden[...], weights[at]).astype(BF)
        mixed = mixed + (t_dot(high[at], result) + t_dot(low[at], result))
    if not last:
        refs[0][...] = mixed
        return
    send, rows = refs
    rows[...] = mixed
    request = lax.axis_index("grp") // 2
    for group in range(send.shape[0]):
        start = ((group // 2) ^ request) * PAIR + group % 2 * ROWS
        send[group] = rows[pl.ds(pl.multiple_of(start, ROWS), ROWS), :].astype(BF)


def down_blocks(places, hiddens, weights, high, low, block, before=(), last=False, after=()):
    features, width = weights.shape[1:]
    tokens = high.shape[2]
    if last:
        out = shape((tokens // ROWS, ROWS, features), BF)
    else:
        out = shape((tokens, features), F32)
    return call(
        functools.partial(down_kernel, places, block, last, len(before)),
        out,
        [VMEM] * (3 + len(hiddens) + len(before)),
        weights,
        high,
        low,
        *hiddens,
        *before,
        after=after,
        scratch=[pltpu.VMEM((tokens, features), F32)] if last else [],
    )


def finish_kernel(residual, back, out):
    half = lax.axis_index("grp") % 2
    value = residual[pl.ds(pl.multiple_of(half * ROWS, ROWS), ROWS), :]
    for group in range(back.shape[0]):
        value = value + back[group].astype(F32)
    out[...] = value.astype(out.dtype)


def on_device(
    step_inputs,
    parents,
    routes,
    w_qkv,
    w_out,
    prompt_keys,
    prompt_values,
    prompt_parts,
    tail_keys,
    tail_values,
    w_router,
    norm_gain,
    w_gate_up,
    w_down,
):
    groups = lax.axis_size("grp")
    splits = lax.axis_size("exp")
    requests = groups // 2
    model = w_qkv.shape[0]
    width = w_qkv.shape[2]
    features = norm_gain.shape[0]
    local = w_gate_up.shape[0]
    tokens = requests * PAIR

    columns = call(
        columns_kernel,
        (
            shape((PAIR, PAIR), BF),
            shape((LANES, PREV * HALF), BF),
            shape((LANES, PAIR), BF),
        ),
        [],
        flops=HINT,
    )
    own_inputs, own_parents, columns = lax.optimization_barrier(
        (step_inputs[0], parents[0], columns)
    )
    far_inputs, far_parents = exchanged((own_inputs, own_parents), "grp", 1)
    near, x = call(
        attend_kernel,
        (shape((PAIR, width + LANES), BF), shape((PAIR, features), F32)),
        [SMEM] + [VMEM] * 13,
        prompt_parts,
        *columns,
        parents[0],
        far_parents,
        routes[0],
        step_inputs[0],
        far_inputs,
        w_qkv.transpose(1, 0, 2),
        prompt_keys[0],
        prompt_values[0],
        tail_keys[0].transpose(1, 0, 2),
        tail_values[0].transpose(1, 0, 2),
        flops=HINT,
    )
    far = exchanged(near, "grp", 1)
    terms = call(
        project_kernel,
        tuple(shape((PAIR, features), F32 if k == 0 else BF) for k in range(splits)),
        [VMEM] * 3,
        near,
        far,
        w_out,
        flops=HINT,
    )
    arrived = [exchanged(terms[k], "exp", k) for k in range(1, splits)]
    residual, message = call(
        residual_kernel,
        (shape((PAIR, features), F32), shape((PAIR, features + LANES), BF)),
        [VMEM] * (6 + len(arrived)),
        x,
        norm_gain.reshape(1, features),
        w_router.T,
        near,
        far,
        terms[0],
        *arrived,
        flops=HINT,
    )
    messages = [message] + [exchanged(message, "grp", 2 * k) for k in range(1, requests)]
    picked, stats, target, choice = call(
        functools.partial(gather_kernel, local),
        (
            shape((local, EXPERTS * CAP_E // local, features), BF),
            shape((8, tokens), F32),
            shape((8, tokens), F32),
            shape((8, tokens), F32),
        ),
        [VMEM] * requests,
        *messages,
        scratch=[pltpu.VMEM((tokens, features), BF)],
        flops=HINT,
    )
    if splits == 4 and local == 2 * splits:
        gate = functools.partial(gate_block, weights=w_gate_up, picked=picked, block=2)
        (a0,) = gate(((3, 0),), stats=(stats,))
        far_a0 = exchanged(a0, "exp", 1)
        (a1,) = gate(((3, 1),), after=(a0,))
        far_a1 = exchanged(a1, "exp", 1)
        c0, stats = gate(((2, 0),), stats=(stats,), far=(far_a0,), after=(a1,))
        far_c0 = exchanged(c0, "exp", 2)
        (c1,) = gate(((2, 1),), far=(far_a1,), after=(c0,))
        far_c1 = exchanged(c1, "exp", 2)
        b0, b1, d0, d1 = gate(
            ((1, 0), (1, 1), (0, 0), (0, 1)), dtypes=(BF, BF, F32, F32), after=(c1,), flops=HINT // 2
        )
        far_b0, far_b1 = exchanged((b0, b1), "exp", 1)

        def hidden_of(pick, near, mid, far, after=()):
            return call(
                functools.partial(hidden_kernel, 2, pick),
                shape((near.shape[0], FFE), BF),
                [VMEM] * 6,
                near,
                mid,
                far,
                target,
                stats,
                far_c0,
                after=after,
                flops=HINT // 2,
            )

        own0 = hidden_of(0, d0, far_b0, far_c0)
        core0 = exchanged(own0, "exp", 1)
        y0 = exchanged(own0, "exp", 2)
        place = shape((local, picked.shape[1], tokens), BF)
        high, low = call(
            functools.partial(place_kernel, local),
            (place, place),
            [VMEM] * 4,
            target,
            choice,
            stats,
            far_c0,
            after=(own0,),
        )
        down = functools.partial(down_blocks, weights=w_down, high=high, low=low, block=2)
        mixed = down(((0, 0), (1, 0)), (own0, core0))
        own1 = hidden_of(1, d1, far_b1, far_c1, after=(mixed,))
        core1 = exchanged(own1, "exp", 1)
        y1 = exchanged(own1, "exp", 2)
        mixed = down(((0, 1), (1, 1)), (own1, core1), before=(mixed,))
        far0 = exchanged(y0, "exp", 1)
        mixed = down(((2, 0),), (y0,), before=(mixed,))
        y1, mixed = lax.optimization_barrier((y1, mixed))
        far1 = exchanged(y1, "exp", 1)
        mixed = down(((2, 1), (3, 0)), (y1, far0), before=(mixed,))
        send = down(((3, 1),), (far1,), before=(mixed,), last=True)
    else:
        stats = lax.psum(stats, "exp")
        sums = jnp.einsum("lcd,ldf->lcf", picked, w_gate_up, preferred_element_type=F32)
        sums = lax.psum(sums.astype(BF), "exp").astype(F32)
        inverse = lax.rsqrt(stats[0] / model + EPSILON)
        goal, pick = target[:local], choice[:local]
        place = goal[:, None, :] == jnp.arange(picked.shape[1], dtype=F32)[None, :, None]
        sums = sums * jnp.sum(jnp.where(place, inverse, 0.0), axis=2, keepdims=True)
        hidden = (jax.nn.silu(sums[..., :FFE]) * sums[..., FFE:]).astype(BF)
        result = jnp.einsum("lcf,ldf->lcd", hidden, w_down, preferred_element_type=F32)
        share = jax.nn.softmax(stats[1:STATS] * inverse, axis=0)
        ids = jnp.arange(TOPK, dtype=F32)[None, :, None]
        weight = jnp.sum(jnp.where(pick[:, None, :] == ids, share[None], 0.0), axis=1)
        mixed = jnp.einsum(
            "lct,lcd->td",
            jnp.where(place, weight[:, None, :], 0.0),
            result.astype(BF).astype(F32),
            precision=lax.Precision.HIGHEST,
        ).reshape(requests, 2 * ROWS, features)
        order = jnp.arange(requests) ^ (lax.axis_index("grp") // 2)
        send = mixed[order].reshape(groups, ROWS, features).astype(BF)
    back = lax.all_to_all(send, "grp", split_axis=0, concat_axis=0, tiled=True)
    result = call(
        finish_kernel, shape((ROWS, features), BF), [VMEM] * 2, residual, back
    )
    return result.reshape(1, STEPS, HALF, features)


def solution(mesh):
    placed = (
        P("grp", None, None, None),
        P("grp", None, None),
        P("grp", None, None, None),
        P(None, None, "exp"),
        P("exp", None),
        P("grp", None, "exp"),
        P("grp", None, "exp"),
        P("grp"),
        P("grp", None, None, "exp"),
        P("grp", None, None, "exp"),
        P("exp", None),
        P("exp"),
        P("grp", "exp", None),
        P("grp", "exp", None),
    )
    return jax.shard_map(
        on_device,
        mesh=mesh,
        in_specs=placed,
        out_specs=P("grp", None, None, "exp"),
        check_vma=False,
    )
```

time: 86.1 us -> 61.6 us (0.72)
  Pallas kernels: 26 us -> 14.6 us
  blocking collectives: 0 us -> 10.3 us
  local copies, waits for them, and re-layouts: 12.1 us -> 1.87 us
  waiting for transfers between devices: 25.1 us -> 18.3 us
  starting transfers between devices: 20.8 us -> 15.4 us
    pallas_call x14 -> x19, Pallas kernels: 26 us -> 14.6 us  [call(): pl.pallas_call(ordered if after else body, out_shape=outs, in_specs=list(...]
    all_to_all x0 -> x1, blocking collectives: none -> 10.3 us  [on_device(): back = lax.all_to_all(send, 'grp', split_axis=0, concat_axis=0, tiled=True)]
    ppermute x23 -> x21, waiting for transfers between devices: 25.1 us -> 18.3 us  [exchanged(): return lax.ppermute(value, axis, pairs)]
    unnamed x17 -> x40, local copies, waits for them, and re-layouts: 7.79 us -> 1.25 us
    ppermute x23 -> x21, starting transfers between devices: 20.8 us -> 15.4 us  [exchanged(): return lax.ppermute(value, axis, pairs)]
    reshape x3 -> x0, local copies, waits for them, and re-layouts: 2.04 us -> none  [the longest x1 1.01 us: on_device(): tail_k = tail_keys[0].transpose(1, 0, 2).reshape(PREV * HALF, width)]
  transfers between devices with their start and end apart: 23 -> 21, of which waited for: 10 -> 11; matrix products, arithmetic and copies ran while one was open for 6% -> 0% of each run, Pallas kernels for 22% -> 15%
where the time goes in v2:
time: 61.6 us; the launch traced here: 61.4 us
  waiting for transfers between devices  18.3 us (30%)
  starting transfers between devices  15.4 us (25%)
  Pallas kernels  14.6 us (24%)
  blocking collectives  10.3 us (17%)
  local copies, waits for them, and re-layouts  1.87 us (3%)
  between operations  1 us (2%)
    ppermute x21, waiting for transfers between devices, exchanged(): return lax.ppermute(value, axis, pairs)  18.3 us
    ppermute x21, starting transfers between devices, exchanged(): return lax.ppermute(value, axis, pairs)  15.4 us
    pallas_call x19, Pallas kernels, call(): pl.pallas_call(ordered if after else body, out_shape=outs, in_specs=list(...  14.6 us
    all_to_all x1, blocking collectives, on_device(): back = lax.all_to_all(send, 'grp', split_axis=0, concat_axis=0, tiled=True)  10.3 us
    unnamed x40, local copies, waits for them, and re-layouts  1.25 us
  transfers between devices with their start and end apart: 21, of which 11 were waited for; matrix products, arithmetic and copies ran while one was open for 0% of the time, Pallas kernels for 15%

profile of v2, /device:TPU:0, one launch (start us, length us, event | category | flops | bytes accessed | tf_op | source)
XLA Modules:
  0.0 61.4 jit_solution(10429229636525915589)
XLA Ops:
  0.1 0.8 %copy-done.6 = bf16[1,4,4,2048]{3,2,1,0:T(4,128)(2,1)S(1)} copy-done((bf16[1,4,4,2048]{3,2,1,0:T(4,128)(2,1)S(1)}, bf16[1,4,4,2048]{3,2,1,0:T(4,128)(2,1)}, u32[]{:S(2)}) %copy-start.6) | copy-done | bytes 65560
  0.8 2.9 %collective-permute-start.1 = (bf16[4,4,2048]{2,1,0:T(4,128)(2,1)S(1)}, bf16[4,4,2048]{2,1,0:T(4,128)(2,1)S(1)}, u32[]{:S(2)}, u32[]{:S(2)}) collective-permute-start(bf16[4,4,2048]{2,1,0:T(4,128)(2,1)S(1)} %bitcast.23), channel_id=1, source_target_pairs={{0,4},{4,0},{8,12},{12,8},{16,20},{20,16},{24,28},{28,24},{1,5},{5... | collective-permute-start | bytes 196616 | tf_op jit(solution)/shard_map/ppermute | solution.py:55
  4.5 2.9 %collective-permute-done.par_far = s32[4,4]{1,0:T(4,128)S(1)} collective-permute-done((s32[4,4]{1,0:T(4,128)S(1)}, s32[4,4]{1,0:T(4,128)S(1)}, u32[]{:S(2)}, u32[]{:S(2)}) %collective-permute-start) | collective-permute-done | bytes 96 | tf_op jit(solution)/shard_map/ppermute | solution.py:55
  7.4 2.9 %shard_map.137 = (bf16[32,640]{1,0:T(8,128)(2,1)S(1)}, f32[32,512]{1,0:T(8,128)S(1)}) custom-call(s32[1]{0:T(128)S(6)} %copy.15.parts, bf16[32,32]{1,0:T(8,128)(2,1)S(1)} %get-tuple-element.38.order, bf16[128,240]{1,0:T(8,128)(2,1)S(1)} %get-tuple-element.39.tail_at, bf16[128,32]{1,0:T(8,128)(2,1)S(1)} %get-tuple-element.40.new_at, s32[4,4]{1,0:T(4,128)S(1)} %bitcast.28, ...), custom_call_target="tpu_custom_call" | custom-call | flops 10000000000 | tf_op jit(solution)/shard_map/pallas_call | solution.py:64
  10.3 0.8 %collective-permute-start.2 = (bf16[32,640]{1,0:T(8,128)(2,1)S(1)}, bf16[32,640]{1,0:T(8,128)(2,1)S(1)}, u32[]{:S(2)}, u32[]{:S(2)}) collective-permute-start(bf16[32,640]{1,0:T(8,128)(2,1)S(1)} %get-tuple-element.44.near), channel_id=1, source_target_pairs={{0,4},{4,0},{8,12},{12,8},{16,20},{20,16},{24,28},{28,24},{1,5},{5... | collective-permute-start | bytes 122888 | tf_op jit(solution)/shard_map/ppermute | solution.py:55
  11.1 3.3 %collective-permute-done.2.far = bf16[32,640]{1,0:T(8,128)(2,1)S(1)} collective-permute-done((bf16[32,640]{1,0:T(8,128)(2,1)S(1)}, bf16[32,640]{1,0:T(8,128)(2,1)S(1)}, u32[]{:S(2)}, u32[]{:S(2)}) %collective-permute-start.2) | collective-permute-done | bytes 40992 | tf_op jit(solution)/shard_map/ppermute | solution.py:55
  14.4 0.6 %shard_map.138 = (f32[32,512]{1,0:T(8,128)S(1)}, bf16[32,512]{1,0:T(8,128)(2,1)S(1)}, bf16[32,512]{1,0:T(8,128)(2,1)S(1)}, bf16[32,512]{1,0:T(8,128)(2,1)S(1)}) custom-call(bf16[32,640]{1,0:T(8,128)(2,1)S(1)} %get-tuple-element.44.near, bf16[32,640]{1,0:T(8,128)(2,1)S(1)} %collective-permute-done.2.far, bf16[512,2048]{1,0:T(8,128)(2,1)S(1)} %copy-done.1), custom_call_target="tpu_custom_call" | custom-call | flops 10000000000 | tf_op jit(solution)/shard_map/pallas_call | solution.py:64
  15.1 1.6 %collective-permute-start.4 = (bf16[32,512]{1,0:T(8,128)(2,1)S(1)}, bf16[32,512]{1,0:T(8,128)(2,1)S(1)}, u32[]{:S(2)}, u32[]{:S(2)}) collective-permute-start(bf16[32,512]{1,0:T(8,128)(2,1)S(1)} %get-tuple-element.47), channel_id=1, source_target_pairs={{0,2},{1,3},{2,0},{3,1},{4,6},{5,7},{6,4},{7,5},{8,10},{9,11},{10,... | collective-permute-start | bytes 98312 | tf_op jit(solution)/shard_map/ppermute | solution.py:55
  16.7 0.3 collective-permute-start.5
  17.0 2.1 %collective-permute-done.4.rest_1_ = bf16[32,512]{1,0:T(8,128)(2,1)S(1)} collective-permute-done((bf16[32,512]{1,0:T(8,128)(2,1)S(1)}, bf16[32,512]{1,0:T(8,128)(2,1)S(1)}, u32[]{:S(2)}, u32[]{:S(2)}) %collective-permute-start.4) | collective-permute-done | bytes 32800 | tf_op jit(solution)/shard_map/ppermute | solution.py:55
  19.1 0.9 %collective-permute-done.5.rest_2_ = bf16[32,512]{1,0:T(8,128)(2,1)S(1)} collective-permute-done((bf16[32,512]{1,0:T(8,128)(2,1)S(1)}, bf16[32,512]{1,0:T(8,128)(2,1)S(1)}, u32[]{:S(2)}, u32[]{:S(2)}) %collective-permute-start.5) | collective-permute-done | bytes 32800 | tf_op jit(solution)/shard_map/ppermute | solution.py:55
  20.1 0.4 shard_map.139
  20.4 1.6 %collective-permute-start.6 = (bf16[32,640]{1,0:T(8,128)(2,1)S(1)}, bf16[32,640]{1,0:T(8,128)(2,1)S(1)}, u32[]{:S(2)}, u32[]{:S(2)}) collective-permute-start(bf16[32,640]{1,0:T(8,128)(2,1)S(1)} %get-tuple-element.50.refs_0_), channel_id=1, source_target_pairs={{0,8},{4,12},{8,0},{12,4},{16,24},{20,28},{24,16},{28,20},{1,9},{5... | collective-permute-start | bytes 122888 | tf_op jit(solution)/shard_map/ppermute | solution.py:55
  22.1 2.6 %collective-permute-start.7 = (bf16[32,640]{1,0:T(8,128)(2,1)S(1)}, bf16[32,640]{1,0:T(8,128)(2,1)S(1)}, u32[]{:S(2)}, u32[]{:S(2)}) collective-permute-start(bf16[32,640]{1,0:T(8,128)(2,1)S(1)} %get-tuple-element.50.refs_0_), channel_id=1, source_target_pairs={{0,16},{4,20},{8,24},{12,28},{16,0},{20,4},{24,8},{28,12},{1,17},{... | collective-permute-start | bytes 122888 | tf_op jit(solution)/shard_map/ppermute | solution.py:55
  24.7 0.2 collective-permute-start.8
  24.9 2.9 %collective-permute-done.7.refs_2_ = bf16[32,640]{1,0:T(8,128)(2,1)S(1)} collective-permute-done((bf16[32,640]{1,0:T(8,128)(2,1)S(1)}, bf16[32,640]{1,0:T(8,128)(2,1)S(1)}, u32[]{:S(2)}, u32[]{:S(2)}) %collective-permute-start.7) | collective-permute-done | bytes 40992 | tf_op jit(solution)/shard_map/ppermute | solution.py:55
  27.8 2.7 %collective-permute-done.8.refs_3_ = bf16[32,640]{1,0:T(8,128)(2,1)S(1)} collective-permute-done((bf16[32,640]{1,0:T(8,128)(2,1)S(1)}, bf16[32,640]{1,0:T(8,128)(2,1)S(1)}, u32[]{:S(2)}, u32[]{:S(2)}) %collective-permute-start.8) | collective-permute-done | bytes 40992 | tf_op jit(solution)/shard_map/ppermute | solution.py:55
  30.5 0.4 shard_map.140
  30.9 0.6 shard_map.141.refs_2_
  31.5 0.6 shard_map.142.refs_4_
  32.1 0.5 collective-permute-start.11
  32.6 0.2 collective-permute-done.9.refs_3_
  32.9 0.6 shard_map.143
  33.5 0.9 %collective-permute-start.10 = (bf16[24,2944]{1,0:T(8,128)(2,1)S(1)}, bf16[24,2944]{1,0:T(8,128)(2,1)S(1)}, u32[]{:S(2)}, u32[]{:S(2)}) collective-permute-start(bf16[24,2944]{1,0:T(8,128)(2,1)S(1)} %get-tuple-element.56.refs_3_), channel_id=1, source_target_pairs={{0,2},{1,3},{2,0},{3,1},{4,6},{5,7},{6,4},{7,5},{8,10},{9,11},{10,... | collective-permute-start | bytes 423944 | tf_op jit(solution)/shard_map/ppermute | solution.py:55
  34.4 0.6 shard_map.144.refs_2_
  35.0 2.1 %shard_map.145 = (bf16[24,2816]{1,0:T(8,128)(2,1)S(1)}, bf16[24,2816]{1,0:T(8,128)(2,1)S(1)}, f32[24,2816]{1,0:T(8,128)S(1)}, f32[24,2816]{1,0:T(8,128)S(1)}) custom-call(bf16[8,512,2816]{2,1,0:T(8,128)(2,1)S(1)} %bitcast.15, bf16[8,24,512]{2,1,0:T(8,128)(2,1)S(1)} %get-tuple-element.53.picked.refs_1_, bf16[24,2816]{1,0:T(8,128)(2,1)S(1)} %shard_map.144.refs_2_), custom_call_target="tpu_custom_call" | custom-call | flops 5000000000 | tf_op jit(solution)/shard_map/pallas_call | solution.py:64
  37.1 1.2 %collective-permute-start.14 = (bf16[24,2816]{1,0:T(8,128)(2,1)S(1)}, bf16[24,2816]{1,0:T(8,128)(2,1)S(1)}, u32[]{:S(2)}, u32[]{:S(2)}) collective-permute-start(bf16[24,2816]{1,0:T(8,128)(2,1)S(1)} %shard_map.144.refs_2_), channel_id=1, source_target_pairs={{0,2},{1,3},{2,0},{3,1},{4,6},{5,7},{6,4},{7,5},{8,10},{9,11},{10,... | collective-permute-start | bytes 405512 | tf_op jit(solution)/shard_map/ppermute | solution.py:55
  38.3 0.2 collective-permute-start.13
  38.5 0.8 %collective-permute-done.10.far.far_stats.refs_3_.refs_5_ = bf16[24,2944]{1,0:T(8,128)(2,1)S(1)} collective-permute-done((bf16[24,2944]{1,0:T(8,128)(2,1)S(1)}, bf16[24,2944]{1,0:T(8,128)(2,1)S(1)}, u32[]{:S(2)}, u32[]{:S(2)}) %collective-permute-start.10) | collective-permute-done | bytes 141344 | tf_op jit(solution)/shard_map/ppermute | solution.py:55
  39.3 0.1 shard_map.146.refs_4_.refs_0_
  39.4 0.1 collective-permute-start.15
  39.5 0.9 %collective-permute-start.17 = (bf16[24,1408]{1,0:T(8,128)(2,1)S(1)}, bf16[24,1408]{1,0:T(8,128)(2,1)S(1)}, u32[]{:S(2)}, u32[]{:S(2)}) collective-permute-start(bf16[24,1408]{1,0:T(8,128)(2,1)S(1)} %shard_map.146.refs_4_.refs_0_), channel_id=1, source_target_pairs={{0,2},{1,3},{2,0},{3,1},{4,6},{5,7},{6,4},{7,5},{8,10},{9,11},{10,... | collective-permute-start | bytes 202760 | tf_op jit(solution)/shard_map/ppermute | solution.py:55
  40.5 0.1 shard_map.147
  40.5 0.2 collective-permute-done.15.refs_1_
  40.8 0.4 slice-done.8
  41.2 1.3 %shard_map.148.refs_6_.refs_2_ = f32[128,512]{1,0:T(8,128)S(1)} custom-call(bf16[8,512,1408]{2,1,0:T(8,128)(2,1)S(1)} %bitcast.17, bf16[8,24,128]{2,1,0:T(8,128)(2,1)S(1)} %get-tuple-element.59.high, bf16[8,24,128]{2,1,0:T(8,128)(2,1)S(1)} %get-tuple-element.60.low, bf16[24,1408]{1,0:T(8,128)(2,1)S(1)} %shard_map.146.refs_4_.refs_0_, ...), custom_call_target="tpu_custom_call" | custom-call | tf_op jit(solution)/shard_map/pallas_call | solution.py:64
  42.5 1.1 %collective-permute-done.14.refs_2_ = bf16[24,2816]{1,0:T(8,128)(2,1)S(1)} collective-permute-done((bf16[24,2816]{1,0:T(8,128)(2,1)S(1)}, bf16[24,2816]{1,0:T(8,128)(2,1)S(1)}, u32[]{:S(2)}, u32[]{:S(2)}) %collective-permute-start.14) | collective-permute-done | bytes 135200 | tf_op jit(solution)/shard_map/ppermute | solution.py:55
  43.6 0.1 shard_map.149.refs_0_
  43.7 0.1 collective-permute-start.18
  43.8 1.2 %collective-permute-start.16 = (bf16[24,1408]{1,0:T(8,128)(2,1)S(1)}, bf16[24,1408]{1,0:T(8,128)(2,1)S(1)}, u32[]{:S(2)}, u32[]{:S(2)}) collective-permute-start(bf16[24,1408]{1,0:T(8,128)(2,1)S(1)} %shard_map.149.refs_0_), channel_id=1, source_target_pairs={{0,2},{1,3},{2,0},{3,1},{4,6},{5,7},{6,4},{7,5},{8,10},{9,11},{10,... | collective-permute-start | bytes 202760 | tf_op jit(solution)/shard_map/ppermute | solution.py:55
  45.0 0.2 collective-permute-start.20
  45.2 1.3 %shard_map.150.refs_1_ = f32[128,512]{1,0:T(8,128)S(1)} custom-call(bf16[8,512,1408]{2,1,0:T(8,128)(2,1)S(1)} %bitcast.17, bf16[8,24,128]{2,1,0:T(8,128)(2,1)S(1)} %get-tuple-element.59.high, bf16[8,24,128]{2,1,0:T(8,128)(2,1)S(1)} %get-tuple-element.60.low, bf16[24,1408]{1,0:T(8,128)(2,1)S(1)} %shard_map.149.refs_0_, ...), custom_call_target="tpu_custom_call" | custom-call | tf_op jit(solution)/shard_map/pallas_call | solution.py:64
  46.5 0.7 %shard_map.151.refs_2_ = f32[128,512]{1,0:T(8,128)S(1)} custom-call(bf16[8,512,1408]{2,1,0:T(8,128)(2,1)S(1)} %bitcast.17, bf16[8,24,128]{2,1,0:T(8,128)(2,1)S(1)} %get-tuple-element.59.high, bf16[8,24,128]{2,1,0:T(8,128)(2,1)S(1)} %get-tuple-element.60.low, bf16[24,1408]{1,0:T(8,128)(2,1)S(1)} %collective-permute-done.17.refs_0_, ...), custom_call_target="tpu_custom_call" | custom-call | tf_op jit(solution)/shard_map/pallas_call | solution.py:64
  47.3 1.1 %collective-permute-done.16.refs_0_ = bf16[24,1408]{1,0:T(8,128)(2,1)S(1)} collective-permute-done((bf16[24,1408]{1,0:T(8,128)(2,1)S(1)}, bf16[24,1408]{1,0:T(8,128)(2,1)S(1)}, u32[]{:S(2)}, u32[]{:S(2)}) %collective-permute-start.16) | collective-permute-done | bytes 67616 | tf_op jit(solution)/shard_map/ppermute | solution.py:55
  48.4 1.3 %shard_map.152.refs_1_ = f32[128,512]{1,0:T(8,128)S(1)} custom-call(bf16[8,512,1408]{2,1,0:T(8,128)(2,1)S(1)} %bitcast.17, bf16[8,24,128]{2,1,0:T(8,128)(2,1)S(1)} %get-tuple-element.59.high, bf16[8,24,128]{2,1,0:T(8,128)(2,1)S(1)} %get-tuple-element.60.low, bf16[24,1408]{1,0:T(8,128)(2,1)S(1)} %collective-permute-done.16.refs_0_, ...), custom_call_target="tpu_custom_call" | custom-call | tf_op jit(solution)/shard_map/pallas_call | solution.py:64
  49.7 0.8 %shard_map.153 = bf16[8,16,512]{2,1,0:T(8,128)(2,1)S(1)} custom-call(bf16[8,512,1408]{2,1,0:T(8,128)(2,1)S(1)} %bitcast.17, bf16[8,24,128]{2,1,0:T(8,128)(2,1)S(1)} %get-tuple-element.59.high, bf16[8,24,128]{2,1,0:T(8,128)(2,1)S(1)} %get-tuple-element.60.low, bf16[24,1408]{1,0:T(8,128)(2,1)S(1)} %collective-permute-done.19.refs_0_, ...), custom_call_target="tpu_custom_call" | custom-call | tf_op jit(solution)/shard_map/pallas_call | solution.py:64
  50.5 10.3 %all_to_all.5.back = bf16[8,16,512]{2,1,0:T(8,128)(2,1)S(1)} all-to-all(bf16[8,16,512]{2,1,0:T(8,128)(2,1)S(1)} %shard_map.153), channel_id=1, replica_groups=mesh['grp'=8,'exp'=4] {'grp'}, dimensions={0} | all-to-all | bytes 262144 | tf_op jit(solution)/shard_map/all_to_all | solution.py:607
  60.8 0.6 %reshape.7 = bf16[1,4,4,512]{3,2,1,0:T(4,128)(2,1)} reshape(bf16[16,512]{1,0:T(8,128)(2,1)S(1)} %shard_map.154) | data formatting | bytes 32768 | tf_op jit(solution)/shard_map/reshape | solution.py:611
  (57 shorter events, 0.3 us)
Async XLA Ops:
  0.0 0.8 %copy-start.6 = (bf16[1,4,4,2048]{3,2,1,0:T(4,128)(2,1)S(1)}, bf16[1,4,4,2048]{3,2,1,0:T(4,128)(2,1)}, u32[]{:S(2)}) copy-start(bf16[1,4,4,2048]{3,2,1,0:T(4,128)(2,1)} %param.14) | copy-start | bytes 196612
  0.0 3.8 %copy-start.9 = (s32[1,4,4]{2,1,0:T(4,128)S(1)}, s32[1,4,4]{2,1,0:T(4,128)}, u32[]{:S(2)}) copy-start(s32[1,4,4]{2,1,0:T(4,128)} %param.15) | copy-start | bytes 196
  0.0 7.4 %copy-start.8 = (s32[1,4,4,6]{3,2,1,0:T(4,128)S(1)}, s32[1,4,4,6]{3,2,1,0:T(4,128)}, u32[]{:S(2)}) copy-start(s32[1,4,4,6]{3,2,1,0:T(4,128)} %param.16) | copy-start | bytes 1156
  0.0 7.4 %copy-start = (bf16[2048,3,512]{2,0,1:T(8,128)(2,1)S(1)}, bf16[2048,3,512]{2,0,1:T(8,128)(2,1)}, u32[]{:S(2)}) copy-start(bf16[2048,3,512]{2,0,1:T(8,128)(2,1)} %param.17) | copy-start | bytes 18874372
  0.0 7.4 %copy-start.2 = (bf16[1,1024,512]{2,1,0:T(8,128)(2,1)S(1)}, bf16[1,1024,512]{2,1,0:T(8,128)(2,1)}, u32[]{:S(2)}) copy-start(bf16[1,1024,512]{2,1,0:T(8,128)(2,1)} %param.19) | copy-start | bytes 3145732
  0.0 7.4 %copy-start.3 = (bf16[1,1024,512]{2,1,0:T(8,128)(2,1)S(1)}, bf16[1,1024,512]{2,1,0:T(8,128)(2,1)}, u32[]{:S(2)}) copy-start(bf16[1,1024,512]{2,1,0:T(8,128)(2,1)} %param.20) | copy-start | bytes 3145732
  0.0 7.4 %copy-start.4 = (bf16[1,4,60,512]{3,1,2,0:T(4,128)(2,1)S(1)}, bf16[1,4,60,512]{3,1,2,0:T(4,128)(2,1)}, u32[]{:S(2)}) copy-start(bf16[1,4,60,512]{3,1,2,0:T(4,128)(2,1)} %param.22) | copy-start | bytes 737284
  0.0 7.4 %copy-start.5 = (bf16[1,4,60,512]{3,1,2,0:T(4,128)(2,1)S(1)}, bf16[1,4,60,512]{3,1,2,0:T(4,128)(2,1)}, u32[]{:S(2)}) copy-start(bf16[1,4,60,512]{3,1,2,0:T(4,128)(2,1)} %param.23) | copy-start | bytes 737284
  0.8 6.5 %collective-permute-start.1 = (bf16[4,4,2048]{2,1,0:T(4,128)(2,1)S(1)}, bf16[4,4,2048]{2,1,0:T(4,128)(2,1)S(1)}, u32[]{:S(2)}, u32[]{:S(2)}) collective-permute-start(bf16[4,4,2048]{2,1,0:T(4,128)(2,1)S(1)} %bitcast.23), channel_id=1, source_target_pairs={{0,4},{4,0},{8,12},{12,8},{16,20},{20,16},{24,28},{28,24},{1,5},{5... | collective-permute-start | bytes 196616 | tf_op jit(solution)/shard_map/ppermute | solution.py:55
  3.8 3.6 %collective-permute-start = (s32[4,4]{1,0:T(4,128)S(1)}, s32[4,4]{1,0:T(4,128)S(1)}, u32[]{:S(2)}, u32[]{:S(2)}) collective-permute-start(s32[4,4]{1,0:T(4,128)S(1)} %bitcast.27), channel_id=1, source_target_pairs={{0,4},{4,0},{8,12},{12,8},{16,20},{20,16},{24,28},{28,24},{1,5},{5... | collective-permute-start | bytes 200 | tf_op jit(solution)/shard_map/ppermute | solution.py:55
  7.4 7.0 %copy-start.1 = (bf16[512,2048]{1,0:T(8,128)(2,1)S(1)}, bf16[512,2048]{1,0:T(8,128)(2,1)}, u32[]{:S(2)}) copy-start(bf16[512,2048]{1,0:T(8,128)(2,1)} %w_out.1) | copy-start | bytes 6291460
  10.3 9.7 %copy-start.7 = (bf16[512,64]{0,1:T(8,128)(2,1)S(1)}, bf16[512,64]{0,1:T(8,128)(2,1)}, u32[]{:S(2)}) copy-start(bf16[512,64]{0,1:T(8,128)(2,1)} %param.24) | copy-start | bytes 196612
  10.3 9.7 %copy-start.10 = (f32[512]{0:T(512)S(1)}, f32[512]{0:T(512)}, u32[]{:S(2)}) copy-start(f32[512]{0:T(512)} %param.25) | copy-start | bytes 6148
  10.3 4.1 %collective-permute-start.2 = (bf16[32,640]{1,0:T(8,128)(2,1)S(1)}, bf16[32,640]{1,0:T(8,128)(2,1)S(1)}, u32[]{:S(2)}, u32[]{:S(2)}) collective-permute-start(bf16[32,640]{1,0:T(8,128)(2,1)S(1)} %get-tuple-element.44.near), channel_id=1, source_target_pairs={{0,4},{4,0},{8,12},{12,8},{16,20},{20,16},{24,28},{28,24},{1,5},{5... | collective-permute-start | bytes 122888 | tf_op jit(solution)/shard_map/ppermute | solution.py:55
  15.1 1.9 %collective-permute-start.3 = (bf16[32,512]{1,0:T(8,128)(2,1)S(1)}, bf16[32,512]{1,0:T(8,128)(2,1)S(1)}, u32[]{:S(2)}, u32[]{:S(2)}) collective-permute-start(bf16[32,512]{1,0:T(8,128)(2,1)S(1)} %get-tuple-element.46), channel_id=1, source_target_pairs={{0,1},{1,0},{2,3},{3,2},{4,5},{5,4},{6,7},{7,6},{8,9},{9,8},{10,11... | collective-permute-start | bytes 98312 | tf_op jit(solution)/shard_map/ppermute | solution.py:55
  15.1 4.0 %collective-permute-start.4 = (bf16[32,512]{1,0:T(8,128)(2,1)S(1)}, bf16[32,512]{1,0:T(8,128)(2,1)S(1)}, u32[]{:S(2)}, u32[]{:S(2)}) collective-permute-start(bf16[32,512]{1,0:T(8,128)(2,1)S(1)} %get-tuple-element.47), channel_id=1, source_target_pairs={{0,2},{1,3},{2,0},{3,1},{4,6},{5,7},{6,4},{7,5},{8,10},{9,11},{10,... | collective-permute-start | bytes 98312 | tf_op jit(solution)/shard_map/ppermute | solution.py:55
  16.7 3.3 %collective-permute-start.5 = (bf16[32,512]{1,0:T(8,128)(2,1)S(1)}, bf16[32,512]{1,0:T(8,128)(2,1)S(1)}, u32[]{:S(2)}, u32[]{:S(2)}) collective-permute-start(bf16[32,512]{1,0:T(8,128)(2,1)S(1)} %get-tuple-element.48), channel_id=1, source_target_pairs={{0,3},{1,2},{2,1},{3,0},{4,7},{5,6},{6,5},{7,4},{8,11},{9,10},{10,... | collective-permute-start | bytes 98312 | tf_op jit(solution)/shard_map/ppermute | solution.py:55
  20.0 10.8 %slice-start = ((s8[23068672]{0:T(1024)(128)(4,1)}), s8[4194304]{0:T(1024)(128)(4,1)S(1)}, s32[]{:S(2)}) async-start(s8[23068672]{0:T(1024)(128)(4,1)} %bitcast.14), calls=%async_computation.1 | async-start | bytes 8388608
  20.0 10.8 %slice-start.1 = ((s8[23068672]{0:T(1024)(128)(4,1)}), s8[4194304]{0:T(1024)(128)(4,1)S(1)}, s32[]{:S(2)}) async-start(s8[23068672]{0:T(1024)(128)(4,1)} %bitcast.14), calls=%async_computation.2 | async-start | bytes 8388608
  20.1 10.8 %slice-start.2 = ((s8[23068672]{0:T(1024)(128)(4,1)}), s8[4194304]{0:T(1024)(128)(4,1)S(1)}, s32[]{:S(2)}) async-start(s8[23068672]{0:T(1024)(128)(4,1)} %bitcast.14), calls=%async_computation.3 | async-start | bytes 8388608
  20.4 10.5 %slice-start.3 = ((s8[23068672]{0:T(1024)(128)(4,1)}), s8[4194304]{0:T(1024)(128)(4,1)S(1)}, s32[]{:S(2)}) async-start(s8[23068672]{0:T(1024)(128)(4,1)} %bitcast.14), calls=%async_computation.4 | async-start | bytes 8388608
  20.4 10.5 %slice-start.4 = ((s8[23068672]{0:T(1024)(128)(4,1)}), s8[4194304]{0:T(1024)(128)(4,1)S(1)}, s32[]{:S(2)}) async-start(s8[23068672]{0:T(1024)(128)(4,1)} %bitcast.14), calls=%async_computation.5 | async-start | bytes 8388608
  20.4 10.5 %slice-start.5 = ((s8[23068672]{0:T(1024)(128)(4,1)}), s8[2097152]{0:T(1024)(128)(4,1)S(1)}, s32[]{:S(2)}) async-start(s8[23068672]{0:T(1024)(128)(4,1)} %bitcast.14), calls=%async_computation.6 | async-start | bytes 4194304
  20.4 4.5 %collective-permute-start.6 = (bf16[32,640]{1,0:T(8,128)(2,1)S(1)}, bf16[32,640]{1,0:T(8,128)(2,1)S(1)}, u32[]{:S(2)}, u32[]{:S(2)}) collective-permute-start(bf16[32,640]{1,0:T(8,128)(2,1)S(1)} %get-tuple-element.50.refs_0_), channel_id=1, source_target_pairs={{0,8},{4,12},{8,0},{12,4},{16,24},{20,28},{24,16},{28,20},{1,9},{5... | collective-permute-start | bytes 122888 | tf_op jit(solution)/shard_map/ppermute | solution.py:55
  22.1 5.7 %collective-permute-start.7 = (bf16[32,640]{1,0:T(8,128)(2,1)S(1)}, bf16[32,640]{1,0:T(8,128)(2,1)S(1)}, u32[]{:S(2)}, u32[]{:S(2)}) collective-permute-start(bf16[32,640]{1,0:T(8,128)(2,1)S(1)} %get-tuple-element.50.refs_0_), channel_id=1, source_target_pairs={{0,16},{4,20},{8,24},{12,28},{16,0},{20,4},{24,8},{28,12},{1,17},{... | collective-permute-start | bytes 122888 | tf_op jit(solution)/shard_map/ppermute | solution.py:55
  24.7 5.8 %collective-permute-start.8 = (bf16[32,640]{1,0:T(8,128)(2,1)S(1)}, bf16[32,640]{1,0:T(8,128)(2,1)S(1)}, u32[]{:S(2)}, u32[]{:S(2)}) collective-permute-start(bf16[32,640]{1,0:T(8,128)(2,1)S(1)} %get-tuple-element.50.refs_0_), channel_id=1, source_target_pairs={{0,24},{4,28},{8,16},{12,20},{16,8},{20,12},{24,0},{28,4},{1,25},{... | collective-permute-start | bytes 122888 | tf_op jit(solution)/shard_map/ppermute | solution.py:55
  31.5 1.4 %collective-permute-start.9 = (bf16[24,2944]{1,0:T(8,128)(2,1)S(1)}, bf16[24,2944]{1,0:T(8,128)(2,1)S(1)}, u32[]{:S(2)}, u32[]{:S(2)}) collective-permute-start(bf16[24,2944]{1,0:T(8,128)(2,1)S(1)} %shard_map.141.refs_2_), channel_id=1, source_target_pairs={{0,1},{1,0},{2,3},{3,2},{4,5},{5,4},{6,7},{7,6},{8,9},{9,8},{10,11... | collective-permute-start | bytes 423944 | tf_op jit(solution)/shard_map/ppermute | solution.py:55
  32.1 2.3 %collective-permute-start.11 = (bf16[24,2816]{1,0:T(8,128)(2,1)S(1)}, bf16[24,2816]{1,0:T(8,128)(2,1)S(1)}, u32[]{:S(2)}, u32[]{:S(2)}) collective-permute-start(bf16[24,2816]{1,0:T(8,128)(2,1)S(1)} %shard_map.142.refs_4_), channel_id=1, source_target_pairs={{0,1},{1,0},{2,3},{3,2},{4,5},{5,4},{6,7},{7,6},{8,9},{9,8},{10,11... | collective-permute-start | bytes 405512 | tf_op jit(solution)/shard_map/ppermute | solution.py:55
  33.5 5.8 %collective-permute-start.10 = (bf16[24,2944]{1,0:T(8,128)(2,1)S(1)}, bf16[24,2944]{1,0:T(8,128)(2,1)S(1)}, u32[]{:S(2)}, u32[]{:S(2)}) collective-permute-start(bf16[24,2944]{1,0:T(8,128)(2,1)S(1)} %get-tuple-element.56.refs_3_), channel_id=1, source_target_pairs={{0,2},{1,3},{2,0},{3,1},{4,6},{5,7},{6,4},{7,5},{8,10},{9,11},{10,... | collective-permute-start | bytes 423944 | tf_op jit(solution)/shard_map/ppermute | solution.py:55
  35.0 5.8 %slice-start.6 = ((s8[11534336]{0:T(1024)(128)(4,1)}), s8[4194304]{0:T(1024)(128)(4,1)S(1)}, s32[]{:S(2)}) async-start(s8[11534336]{0:T(1024)(128)(4,1)} %bitcast.16), calls=%async_computation.7 | async-start | bytes 8388608
  35.0 5.8 %slice-start.7 = ((s8[11534336]{0:T(1024)(128)(4,1)}), s8[4194304]{0:T(1024)(128)(4,1)S(1)}, s32[]{:S(2)}) async-start(s8[11534336]{0:T(1024)(128)(4,1)} %bitcast.16), calls=%async_computation.8 | async-start | bytes 8388608
  37.1 1.4 %collective-permute-start.12 = (bf16[24,2816]{1,0:T(8,128)(2,1)S(1)}, bf16[24,2816]{1,0:T(8,128)(2,1)S(1)}, u32[]{:S(2)}, u32[]{:S(2)}) collective-permute-start(bf16[24,2816]{1,0:T(8,128)(2,1)S(1)} %get-tuple-element.58), channel_id=1, source_target_pairs={{0,1},{1,0},{2,3},{3,2},{4,5},{5,4},{6,7},{7,6},{8,9},{9,8},{10,11... | collective-permute-start | bytes 405512 | tf_op jit(solution)/shard_map/ppermute | solution.py:55
  37.1 6.5 %collective-permute-start.14 = (bf16[24,2816]{1,0:T(8,128)(2,1)S(1)}, bf16[24,2816]{1,0:T(8,128)(2,1)S(1)}, u32[]{:S(2)}, u32[]{:S(2)}) collective-permute-start(bf16[24,2816]{1,0:T(8,128)(2,1)S(1)} %shard_map.144.refs_2_), channel_id=1, source_target_pairs={{0,2},{1,3},{2,0},{3,1},{4,6},{5,7},{6,4},{7,5},{8,10},{9,11},{10,... | collective-permute-start | bytes 405512 | tf_op jit(solution)/shard_map/ppermute | solution.py:55
  38.3 4.2 %collective-permute-start.13 = (bf16[24,2816]{1,0:T(8,128)(2,1)S(1)}, bf16[24,2816]{1,0:T(8,128)(2,1)S(1)}, u32[]{:S(2)}, u32[]{:S(2)}) collective-permute-start(bf16[24,2816]{1,0:T(8,128)(2,1)S(1)} %get-tuple-element.62), channel_id=1, source_target_pairs={{0,1},{1,0},{2,3},{3,2},{4,5},{5,4},{6,7},{7,6},{8,9},{9,8},{10,11... | collective-permute-start | bytes 405512 | tf_op jit(solution)/shard_map/ppermute | solution.py:55
  39.3 1.9 %slice-start.8 = ((s8[11534336]{0:T(1024)(128)(4,1)}), s8[3145728]{0:T(1024)(128)(4,1)S(1)}, s32[]{:S(2)}) async-start(s8[11534336]{0:T(1024)(128)(4,1)} %bitcast.16), calls=%async_computation.9 | async-start | bytes 6291456
  39.4 1.3 %collective-permute-start.15 = (bf16[24,1408]{1,0:T(8,128)(2,1)S(1)}, bf16[24,1408]{1,0:T(8,128)(2,1)S(1)}, u32[]{:S(2)}, u32[]{:S(2)}) collective-permute-start(bf16[24,1408]{1,0:T(8,128)(2,1)S(1)} %shard_map.146.refs_4_.refs_0_), channel_id=1, source_target_pairs={{0,1},{1,0},{2,3},{3,2},{4,5},{5,4},{6,7},{7,6},{8,9},{9,8},{10,11... | collective-permute-start | bytes 202760 | tf_op jit(solution)/shard_map/ppermute | solution.py:55
  39.5 5.5 %collective-permute-start.17 = (bf16[24,1408]{1,0:T(8,128)(2,1)S(1)}, bf16[24,1408]{1,0:T(8,128)(2,1)S(1)}, u32[]{:S(2)}, u32[]{:S(2)}) collective-permute-start(bf16[24,1408]{1,0:T(8,128)(2,1)S(1)} %shard_map.146.refs_4_.refs_0_), channel_id=1, source_target_pairs={{0,2},{1,3},{2,0},{3,1},{4,6},{5,7},{6,4},{7,5},{8,10},{9,11},{10,... | collective-permute-start | bytes 202760 | tf_op jit(solution)/shard_map/ppermute | solution.py:55
  43.7 1.5 %collective-permute-start.18 = (bf16[24,1408]{1,0:T(8,128)(2,1)S(1)}, bf16[24,1408]{1,0:T(8,128)(2,1)S(1)}, u32[]{:S(2)}, u32[]{:S(2)}) collective-permute-start(bf16[24,1408]{1,0:T(8,128)(2,1)S(1)} %shard_map.149.refs_0_), channel_id=1, source_target_pairs={{0,1},{1,0},{2,3},{3,2},{4,5},{5,4},{6,7},{7,6},{8,9},{9,8},{10,11... | collective-permute-start | bytes 202760 | tf_op jit(solution)/shard_map/ppermute | solution.py:55
  43.8 4.6 %collective-permute-start.16 = (bf16[24,1408]{1,0:T(8,128)(2,1)S(1)}, bf16[24,1408]{1,0:T(8,128)(2,1)S(1)}, u32[]{:S(2)}, u32[]{:S(2)}) collective-permute-start(bf16[24,1408]{1,0:T(8,128)(2,1)S(1)} %shard_map.149.refs_0_), channel_id=1, source_target_pairs={{0,2},{1,3},{2,0},{3,1},{4,6},{5,7},{6,4},{7,5},{8,10},{9,11},{10,... | collective-permute-start | bytes 202760 | tf_op jit(solution)/shard_map/ppermute | solution.py:55
  45.0 3.3 %collective-permute-start.20 = (bf16[24,1408]{1,0:T(8,128)(2,1)S(1)}, bf16[24,1408]{1,0:T(8,128)(2,1)S(1)}, u32[]{:S(2)}, u32[]{:S(2)}) collective-permute-start(bf16[24,1408]{1,0:T(8,128)(2,1)S(1)} %collective-permute-done.17.refs_0_), channel_id=1, source_target_pairs={{0,1},{1,0},{2,3},{3,2},{4,5},{5,4},{6,7},{7,6},{8,9},{9,8},{10,11... | collective-permute-start | bytes 202760 | tf_op jit(solution)/shard_map/ppermute | solution.py:55
  48.4 1.3 %collective-permute-start.19 = (bf16[24,1408]{1,0:T(8,128)(2,1)S(1)}, bf16[24,1408]{1,0:T(8,128)(2,1)S(1)}, u32[]{:S(2)}, u32[]{:S(2)}) collective-permute-start(bf16[24,1408]{1,0:T(8,128)(2,1)S(1)} %collective-permute-done.16.refs_0_), channel_id=1, source_target_pairs={{0,1},{1,0},{2,3},{3,2},{4,5},{5,4},{6,7},{7,6},{8,9},{9,8},{10,11... | collective-permute-start | bytes 202760 | tf_op jit(solution)/shard_map/ppermute | solution.py:55

commit v3 on v2

--- a/solution.py
+++ b/solution.py
@@ -81,17 +81,31 @@
     to_row = iota(order.shape, 0)
     wanted = (to_row % ROWS // HALF) * BEAMS + (to_row // ROWS) * HALF + to_row % HALF
     order[...] = (iota(order.shape, 1) == wanted).astype(BF)
-    column = iota(tail_at.shape, 1)
-    tail_at[...] = (iota(tail_at.shape, 0) == half * HALF + column % HALF).astype(BF)
-    column = iota(new_at.shape, 1)
-    beam = (column // ROWS) * HALF + column % HALF
-    place = BEAMS + BEAMS * (column % ROWS // HALF) + beam
-    here = (iota(new_at.shape, 0) == place) & (column // ROWS == half)
-    new_at[...] = here.astype(BF)
+    column = iota(tail_at.shape, 0)
+    tail_at[...] = (iota(tail_at.shape, 1) == half * HALF + column % HALF).astype(BF)
+    column = iota(new_at.shape, 0)
+    place = BEAMS + BEAMS * (column // HALF) + half * HALF + column % HALF
+    new_at[...] = (iota(new_at.shape, 1) == place).astype(BF)
 
 
 def slot_rows(source):
     return jnp.concatenate([source[step].astype(F32) for step in range(STEPS)], axis=0)
+
+
+def feature_part(rows, features):
+    me = lax.axis_index("exp")
+    mine = rows[:, :features]
+    for k in range(1, rows.shape[1] // features):
+        mine = jnp.where(me == k, rows[:, k * features : (k + 1) * features], mine)
+    return mine
+
+
+def own_kernel(x_own, wqkv, query, keys, values, part):
+    rows = slot_rows(x_own)
+    part[...] = feature_part(rows, part.shape[1])
+    rows = rows.astype(BF)
+    for k, out in enumerate((query, keys, values)):
+        out[...] = dot(rows, wqkv[k]).astype(BF)
 
 
 def in_order(first, own, far):
@@ -114,9 +128,12 @@
     par_own,
     par_far,
     routes,
-    x_own,
     x_far,
+    query_own,
+    part_own,
     wqkv,
+    key_new,
+    value_new,
     kp,
     vp,
     tk_raw,
@@ -125,19 +142,13 @@
     x_out,
 ):
     half = lax.axis_index("grp") % 2
-    width = wqkv.shape[2]
+    first = half == 0
+    width = kp.shape[1]
     heads = width // HDIM
-    x_all = in_order(half == 0, slot_rows(x_own), slot_rows(x_far))
-    rows = x_all.astype(BF)
-    features = x_out.shape[1]
-    me = lax.axis_index("exp")
-    mine = jnp.zeros((PAIR, features), F32)
-    for k in range(x_all.shape[1] // features):
-        mine = jnp.where(me == k, x_all[:, k * features : (k + 1) * features], mine)
-    x_out[...] = mine
-    query = dot(rows, wqkv[0]).astype(BF)
-    key_new = dot(rows, wqkv[1]).astype(BF)
-    value_new = dot(rows, wqkv[2]).astype(BF)
+    far_rows = slot_rows(x_far)
+    x_out[...] = in_order(first, part_own[...], feature_part(far_rows, part_own.shape[1]))
+    query_far = dot(far_rows.astype(BF), wqkv[0]).astype(BF)
+    query = in_order(first, query_own[...], query_far)
     lane = iota((BEAMS, LANES), 1)
     beam = iota((BEAMS, LANES), 0)
     state = (lane == beam).astype(F32)
@@ -152,7 +163,7 @@
             )
             for source in (par_own, par_far)
         ]
-        parent = in_order(half == 0, *columns)
+        parent = in_order(first, *columns)
         taken = jnp.zeros((BEAMS, LANES), F32)
         for j in range(BEAMS):
             taken = taken + jnp.where(parent == float(j), state[j : j + 1, :], 0.0)
@@ -160,47 +171,49 @@
         states.append(state)
     held = jnp.concatenate(states, axis=0).astype(BF)
     held = dot(order[...], held).astype(BF)
-    tail_mask = dot(held, tail_at[...]) > 0.5
-    new_mask = dot(held, new_at[...]) > 0.5
+    held = jnp.concatenate([held] * heads, axis=0)
+    spread = jnp.concatenate([query] * heads, axis=0)
+    lanes = heads * PAIR
+    owner = iota((lanes, width), 0) // PAIR == iota((lanes, width), 1) // HDIM
+    spread = jnp.where(owner, spread.astype(F32), 0.0).astype(BF)
     tk = tk_raw[...].reshape(PREV * HALF, width)
     tv = tv_raw[...].reshape(PREV * HALF, width)
     cap = kp.shape[0]
-    live = iota((PAIR, cap), 1) < parts[0]
     scale = HDIM ** (-0.5)
+    live = iota((cap, lanes), 0) < parts[0]
+    s_p = jnp.where(live, dot_t(kp[...], spread) * scale, NEGATIVE)
+    s_t = jnp.where(dot_t(tail_at[...], held) > 0.5, dot_t(tk, spread) * scale, NEGATIVE)
+    s_n = jnp.where(
+        dot_t(new_at[...], held) > 0.5, dot_t(key_new[...], spread) * scale, NEGATIVE
+    )
+    top = jnp.maximum(
+        jnp.max(s_p, axis=0, keepdims=True),
+        jnp.maximum(jnp.max(s_t, axis=0, keepdims=True), jnp.max(s_n, axis=0, keepdims=True)),
+    )
+    p_p, p_t, p_n = [jnp.exp(part - top) for part in (s_p, s_t, s_n)]
+    total = (
+        jnp.sum(p_p, axis=0, keepdims=True)
+        + jnp.sum(p_t, axis=0, keepdims=True)
+        + jnp.sum(p_n, axis=0, keepdims=True)
+    )
+    mix = (
+        t_dot(p_p.astype(BF), vp[...])
+        + t_dot(p_t.astype(BF), tv)
+        + t_dot(p_n.astype(BF), value_new[...])
+    )
+    columns = jnp.concatenate([top, total, jnp.zeros((6, lanes), F32)], axis=0).T
     info = jnp.zeros((PAIR, LANES), F32)
     info_lane = iota((PAIR, LANES), 1)
-    own_rows = iota((PAIR, LANES), 0) // ROWS == half
     named = slot_rows(routes)
-    named = jnp.concatenate([named, named], axis=0)
+    named = in_order(first, named, jnp.zeros_like(named))
     for k in range(TOPK):
-        info = jnp.where((info_lane == 5 * heads + k) & own_rows, named[:, k : k + 1], info)
+        info = jnp.where(info_lane == 5 * heads + k, named[:, k : k + 1], info)
     for head in range(heads):
         at = slice(head * HDIM, (head + 1) * HDIM)
-        q = query[:, at]
-        s_p = jnp.where(live, dot_t(q, kp[:, at]) * scale, NEGATIVE)
-        s_t = jnp.where(tail_mask, dot_t(q, tk[:, at]) * scale, NEGATIVE)
-        s_n = jnp.where(new_mask, dot_t(q, key_new[:, at]) * scale, NEGATIVE)
-        top = jnp.maximum(
-            jnp.max(s_p, axis=1, keepdims=True),
-            jnp.maximum(
-                jnp.max(s_t, axis=1, keepdims=True), jnp.max(s_n, axis=1, keepdims=True)
-            ),
-        )
-        p_p = jnp.exp(s_p - top)
-        p_t = jnp.exp(s_t - top)
-        p_n = jnp.exp(s_n - top)
-        total = (
-            jnp.sum(p_p, axis=1, keepdims=True)
-            + jnp.sum(p_t, axis=1, keepdims=True)
-            + jnp.sum(p_n, axis=1, keepdims=True)
-        )
-        mix = (
-            dot(p_p.astype(BF), vp[:, at])
-            + dot(p_t.astype(BF), tv[:, at])
-            + dot(p_n.astype(BF), value_new[:, at])
-        )
-        out[:, at] = mix.astype(BF)
-        for k, column in enumerate(pieces(top, 3) + pieces(total, 2)):
+        these = slice(head * PAIR, (head + 1) * PAIR)
+        out[:, at] = mix[these, at].astype(BF)
+        parts_of = pieces(columns[these, 0:1], 3) + pieces(columns[these, 1:2], 2)
+        for k, column in enumerate(parts_of):
             info = jnp.where(info_lane == k * heads + head, column, info)
     out[:, width:] = info.astype(BF)
 
@@ -261,7 +274,7 @@
 
 
 def gather_kernel(local, *refs):
-    messages, (picked, stats, target, choice, rows) = refs[:-5], refs[-5:]
+    messages, (picked, stats, target, choice, rows) = refs[:-5][::-1], refs[-5:]
     blocks = len(messages)
     tokens = blocks * PAIR
     features = rows.shape[1]
@@ -457,12 +470,13 @@
     local = w_gate_up.shape[0]
     tokens = requests * PAIR
 
+    w_all = w_qkv.transpose(1, 0, 2)
     columns = call(
         columns_kernel,
         (
             shape((PAIR, PAIR), BF),
-            shape((LANES, PREV * HALF), BF),
-            shape((LANES, PAIR), BF),
+            shape((PREV * HALF, LANES), BF),
+            shape((ROWS, LANES), BF),
         ),
         [],
         flops=HINT,
@@ -471,18 +485,30 @@
         (step_inputs[0], parents[0], columns)
     )
     far_inputs, far_parents = exchanged((own_inputs, own_parents), "grp", 1)
+    query, keys_new, values_new, part = call(
+        own_kernel,
+        (shape((ROWS, width), BF),) * 3 + (shape((ROWS, features), F32),),
+        [VMEM] * 2,
+        step_inputs[0],
+        w_all,
+        after=columns[:1],
+        flops=HINT // 4,
+    )
     near, x = call(
         attend_kernel,
         (shape((PAIR, width + LANES), BF), shape((PAIR, features), F32)),
-        [SMEM] + [VMEM] * 13,
+        [SMEM] + [VMEM] * 16,
         prompt_parts,
         *columns,
         parents[0],
         far_parents,
         routes[0],
-        step_inputs[0],
         far_inputs,
-        w_qkv.transpose(1, 0, 2),
+        query,
+        part,
+        w_all,
+        keys_new,
+        values_new,
         prompt_keys[0],
         prompt_values[0],
         tail_keys[0].transpose(1, 0, 2),
@@ -513,7 +539,8 @@
         *arrived,
         flops=HINT,
     )
-    messages = [message] + [exchanged(message, "grp", 2 * k) for k in range(1, requests)]
+    messages = [exchanged(message, "grp", 2 * k) for k in range(1, requests)]
+    messages = [message] + messages
     picked, stats, target, choice = call(
         functools.partial(gather_kernel, local),
         (
@@ -523,7 +550,7 @@
             shape((8, tokens), F32),
         ),
         [VMEM] * requests,
-        *messages,
+        *messages[::-1],
         scratch=[pltpu.VMEM((tokens, features), BF)],
         flops=HINT,
     )
@@ -538,7 +565,10 @@
         (c1,) = gate(((2, 1),), far=(far_a1,), after=(c0,))
         far_c1 = exchanged(c1, "exp", 2)
         b0, b1, d0, d1 = gate(
-            ((1, 0), (1, 1), (0, 0), (0, 1)), dtypes=(BF, BF, F32, F32), after=(c1,), flops=HINT // 2
+            ((1, 0), (1, 1), (0, 0), (0, 1)),
+            dtypes=(BF, BF, F32, F32),
+            after=(c1,),
+            flops=5000000000,
         )
         far_b0, far_b1 = exchanged((b0, b1), "exp", 1)
 
@@ -554,7 +584,7 @@
                 stats,
                 far_c0,
                 after=after,
-                flops=HINT // 2,
+                flops=2000000000,
             )
 
         own0 = hidden_of(0, d0, far_b0, far_c0)
@@ -570,6 +600,7 @@
             stats,
             far_c0,
             after=(own0,),
+            flops=2000000000,
         )
         down = functools.partial(down_blocks, weights=w_down, high=high, low=low, block=2)
         mixed = down(((0, 0), (1, 0)), (own0, core0))

time: 61.6 us -> 60.1 us (0.976)
  waiting for transfers between devices: 18.3 us -> 17.1 us
    ppermute x21, waiting for transfers between devices: 18.3 us -> 17.1 us  [exchanged(): return lax.ppermute(value, axis, pairs)]
    pallas_call x19 -> x20, Pallas kernels: 14.6 us -> 14.5 us  [call(): pl.pallas_call(ordered if after else body, out_shape=outs, in_specs=list(...]
  transfers between devices with their start and end apart: 21 -> 21, of which waited for: 11 -> 11; matrix products, arithmetic and copies ran while one was open for 0% -> 0% of each run, Pallas kernels for 15% -> 16%
where the time goes in v3:
time: 60.1 us; the launch traced here: 59.9 us
  waiting for transfers between devices  17.1 us (28%)
  starting transfers between devices  14.9 us (25%)
  Pallas kernels  14.5 us (24%)
  blocking collectives  10.7 us (18%)
  local copies, waits for them, and re-layouts  1.74 us (3%)
  between operations  1.01 us (2%)
    ppermute x21, waiting for transfers between devices, exchanged(): return lax.ppermute(value, axis, pairs)  17.1 us
    ppermute x21, starting transfers between devices, exchanged(): return lax.ppermute(value, axis, pairs)  14.9 us
    pallas_call x20, Pallas kernels, call(): pl.pallas_call(ordered if after else body, out_shape=outs, in_specs=list(...  14.5 us
    all_to_all x1, blocking collectives, on_device(): back = lax.all_to_all(send, 'grp', split_axis=0, concat_axis=0, tiled=True)  10.7 us
  transfers between devices with their start and end apart: 21, of which 11 were waited for; matrix products, arithmetic and copies ran while one was open for 0% of the time, Pallas kernels for 16%

profile of v3, /device:TPU:0, one launch (start us, length us, event | category | flops | bytes accessed | tf_op | source)
XLA Modules:
  0.0 59.9 jit_solution(17855993078235474)
XLA Ops:
  0.1 0.6 %copy-done.9 = s32[1,4,4]{2,1,0:T(4,128)S(1)} copy-done((s32[1,4,4]{2,1,0:T(4,128)S(1)}, s32[1,4,4]{2,1,0:T(4,128)}, u32[]{:S(2)}) %copy-start.9) | copy-done | bytes 88
  0.7 2.9 %collective-permute-start = (s32[4,4]{1,0:T(4,128)S(1)}, s32[4,4]{1,0:T(4,128)S(1)}, u32[]{:S(2)}, u32[]{:S(2)}) collective-permute-start(s32[4,4]{1,0:T(4,128)S(1)} %bitcast.28), channel_id=1, source_target_pairs={{0,4},{4,0},{8,12},{12,8},{16,20},{20,16},{24,28},{28,24},{1,5},{5... | collective-permute-start | bytes 200 | tf_op jit(solution)/shard_map/ppermute | solution.py:55
  3.7 0.1 collective-permute-start.1
  3.8 0.9 %shard_map.137 = (bf16[16,512]{1,0:T(8,128)(2,1)S(1)}, bf16[16,512]{1,0:T(8,128)(2,1)S(1)}, bf16[16,512]{1,0:T(8,128)(2,1)S(1)}, f32[16,512]{1,0:T(8,128)S(1)}) custom-call(bf16[4,4,2048]{2,1,0:T(4,128)(2,1)S(1)} %bitcast.25, bf16[3,2048,512]{2,1,0:T(8,128)(2,1)S(1)} %bitcast.18, bf16[32,32]{1,0:T(8,128)(2,1)S(1)} %get-tuple-element.42.refs_2_.order), custom_call_target="tpu_custom_call" | custom-call | flops 2500000000 | tf_op jit(solution)/shard_map/pallas_call | solution.py:64
  5.4 2.5 %collective-permute-done.1.x_far = bf16[4,4,2048]{2,1,0:T(4,128)(2,1)S(1)} collective-permute-done((bf16[4,4,2048]{2,1,0:T(4,128)(2,1)S(1)}, bf16[4,4,2048]{2,1,0:T(4,128)(2,1)S(1)}, u32[]{:S(2)}, u32[]{:S(2)}) %collective-permute-start.1) | collective-permute-done | bytes 65568 | tf_op jit(solution)/shard_map/ppermute | solution.py:55
  8.0 1.9 %shard_map.138 = (bf16[32,640]{1,0:T(8,128)(2,1)S(1)}, f32[32,512]{1,0:T(8,128)S(1)}) custom-call(s32[1]{0:T(128)S(6)} %copy.15.parts, bf16[32,32]{1,0:T(8,128)(2,1)S(1)} %get-tuple-element.42.refs_2_.order, bf16[240,128]{1,0:T(8,128)(2,1)S(1)} %get-tuple-element.43.tail_at, bf16[16,128]{1,0:T(8,128)(2,1)S(1)} %get-tuple-element.44.new_at, ...), custom_call_target="tpu_custom_call" | custom-call | flops 10000000000 | tf_op jit(solution)/shard_map/pallas_call | solution.py:64
  9.9 0.2 collective-permute-start.2
  10.1 3.9 %collective-permute-done.2.far = bf16[32,640]{1,0:T(8,128)(2,1)S(1)} collective-permute-done((bf16[32,640]{1,0:T(8,128)(2,1)S(1)}, bf16[32,640]{1,0:T(8,128)(2,1)S(1)}, u32[]{:S(2)}, u32[]{:S(2)}) %collective-permute-start.2) | collective-permute-done | bytes 40992 | tf_op jit(solution)/shard_map/ppermute | solution.py:55
  14.0 0.6 %shard_map.139 = (f32[32,512]{1,0:T(8,128)S(1)}, bf16[32,512]{1,0:T(8,128)(2,1)S(1)}, bf16[32,512]{1,0:T(8,128)(2,1)S(1)}, bf16[32,512]{1,0:T(8,128)(2,1)S(1)}) custom-call(bf16[32,640]{1,0:T(8,128)(2,1)S(1)} %get-tuple-element.52.near, bf16[32,640]{1,0:T(8,128)(2,1)S(1)} %collective-permute-done.2.far, bf16[512,2048]{1,0:T(8,128)(2,1)S(1)} %copy-done.1), custom_call_target="tpu_custom_call" | custom-call | flops 10000000000 | tf_op jit(solution)/shard_map/pallas_call | solution.py:64
  14.7 1.6 %collective-permute-start.4 = (bf16[32,512]{1,0:T(8,128)(2,1)S(1)}, bf16[32,512]{1,0:T(8,128)(2,1)S(1)}, u32[]{:S(2)}, u32[]{:S(2)}) collective-permute-start(bf16[32,512]{1,0:T(8,128)(2,1)S(1)} %get-tuple-element.55), channel_id=1, source_target_pairs={{0,2},{1,3},{2,0},{3,1},{4,6},{5,7},{6,4},{7,5},{8,10},{9,11},{10,... | collective-permute-start | bytes 98312 | tf_op jit(solution)/shard_map/ppermute | solution.py:55
  16.2 0.3 collective-permute-start.5
  16.5 2.1 %collective-permute-done.4.rest_1_ = bf16[32,512]{1,0:T(8,128)(2,1)S(1)} collective-permute-done((bf16[32,512]{1,0:T(8,128)(2,1)S(1)}, bf16[32,512]{1,0:T(8,128)(2,1)S(1)}, u32[]{:S(2)}, u32[]{:S(2)}) %collective-permute-start.4) | collective-permute-done | bytes 32800 | tf_op jit(solution)/shard_map/ppermute | solution.py:55
  18.6 0.9 %collective-permute-done.5.rest_2_ = bf16[32,512]{1,0:T(8,128)(2,1)S(1)} collective-permute-done((bf16[32,512]{1,0:T(8,128)(2,1)S(1)}, bf16[32,512]{1,0:T(8,128)(2,1)S(1)}, u32[]{:S(2)}, u32[]{:S(2)}) %collective-permute-start.5) | collective-permute-done | bytes 32800 | tf_op jit(solution)/shard_map/ppermute | solution.py:55
  19.6 0.4 shard_map.140
  20.0 3.7 %collective-permute-start.6 = (bf16[32,640]{1,0:T(8,128)(2,1)S(1)}, bf16[32,640]{1,0:T(8,128)(2,1)S(1)}, u32[]{:S(2)}, u32[]{:S(2)}) collective-permute-start(bf16[32,640]{1,0:T(8,128)(2,1)S(1)} %get-tuple-element.58.refs_3_), channel_id=1, source_target_pairs={{0,24},{4,28},{8,16},{12,20},{16,8},{20,12},{24,0},{28,4},{1,25},{... | collective-permute-start | bytes 122888 | tf_op jit(solution)/shard_map/ppermute | solution.py:55
  23.7 0.8 %collective-permute-start.8 = (bf16[32,640]{1,0:T(8,128)(2,1)S(1)}, bf16[32,640]{1,0:T(8,128)(2,1)S(1)}, u32[]{:S(2)}, u32[]{:S(2)}) collective-permute-start(bf16[32,640]{1,0:T(8,128)(2,1)S(1)} %get-tuple-element.58.refs_3_), channel_id=1, source_target_pairs={{0,8},{4,12},{8,0},{12,4},{16,24},{20,28},{24,16},{28,20},{1,9},{5... | collective-permute-start | bytes 122888 | tf_op jit(solution)/shard_map/ppermute | solution.py:55
  24.4 1.5 %collective-permute-done.6.refs_0_ = bf16[32,640]{1,0:T(8,128)(2,1)S(1)} collective-permute-done((bf16[32,640]{1,0:T(8,128)(2,1)S(1)}, bf16[32,640]{1,0:T(8,128)(2,1)S(1)}, u32[]{:S(2)}, u32[]{:S(2)}) %collective-permute-start.6) | collective-permute-done | bytes 40992 | tf_op jit(solution)/shard_map/ppermute | solution.py:55
  25.9 2.7 %collective-permute-done.7.refs_1_ = bf16[32,640]{1,0:T(8,128)(2,1)S(1)} collective-permute-done((bf16[32,640]{1,0:T(8,128)(2,1)S(1)}, bf16[32,640]{1,0:T(8,128)(2,1)S(1)}, u32[]{:S(2)}, u32[]{:S(2)}) %collective-permute-start.7) | collective-permute-done | bytes 40992 | tf_op jit(solution)/shard_map/ppermute | solution.py:55
  28.6 0.4 shard_map.141
  29.0 0.6 %shard_map.142.refs_2_ = bf16[24,2944]{1,0:T(8,128)(2,1)S(1)} custom-call(bf16[8,512,2816]{2,1,0:T(8,128)(2,1)S(1)} %bitcast.15, bf16[8,24,512]{2,1,0:T(8,128)(2,1)S(1)} %get-tuple-element.61.picked.refs_1_, f32[8,128]{1,0:T(8,128)S(1)} %get-tuple-element.62.refs_0_.refs_2_), custom_call_target="tpu_custom_call" | custom-call | tf_op jit(solution)/shard_map/pallas_call | solution.py:64
  29.6 0.6 %shard_map.143.refs_4_ = bf16[24,2816]{1,0:T(8,128)(2,1)S(1)} custom-call(bf16[8,512,2816]{2,1,0:T(8,128)(2,1)S(1)} %bitcast.15, bf16[8,24,512]{2,1,0:T(8,128)(2,1)S(1)} %get-tuple-element.61.picked.refs_1_, bf16[24,2944]{1,0:T(8,128)(2,1)S(1)} %shard_map.142.refs_2_), custom_call_target="tpu_custom_call" | custom-call | tf_op jit(solution)/shard_map/pallas_call | solution.py:64
  30.2 0.5 collective-permute-start.11
  30.7 0.2 collective-permute-done.9.refs_3_
  31.0 0.6 shard_map.144
  31.6 0.9 %collective-permute-start.10 = (bf16[24,2944]{1,0:T(8,128)(2,1)S(1)}, bf16[24,2944]{1,0:T(8,128)(2,1)S(1)}, u32[]{:S(2)}, u32[]{:S(2)}) collective-permute-start(bf16[24,2944]{1,0:T(8,128)(2,1)S(1)} %get-tuple-element.64.refs_3_), channel_id=1, source_target_pairs={{0,2},{1,3},{2,0},{3,1},{4,6},{5,7},{6,4},{7,5},{8,10},{9,11},{10,... | collective-permute-start | bytes 423944 | tf_op jit(solution)/shard_map/ppermute | solution.py:55
  32.5 0.6 shard_map.145.refs_2_
  33.1 2.1 %shard_map.146 = (bf16[24,2816]{1,0:T(8,128)(2,1)S(1)}, bf16[24,2816]{1,0:T(8,128)(2,1)S(1)}, f32[24,2816]{1,0:T(8,128)S(1)}, f32[24,2816]{1,0:T(8,128)S(1)}) custom-call(bf16[8,512,2816]{2,1,0:T(8,128)(2,1)S(1)} %bitcast.15, bf16[8,24,512]{2,1,0:T(8,128)(2,1)S(1)} %get-tuple-element.61.picked.refs_1_, bf16[24,2816]{1,0:T(8,128)(2,1)S(1)} %shard_map.145.refs_2_), custom_call_target="tpu_custom_call" | custom-call | flops 5000000000 | tf_op jit(solution)/shard_map/pallas_call | solution.py:64
  35.2 1.2 %collective-permute-start.14 = (bf16[24,2816]{1,0:T(8,128)(2,1)S(1)}, bf16[24,2816]{1,0:T(8,128)(2,1)S(1)}, u32[]{:S(2)}, u32[]{:S(2)}) collective-permute-start(bf16[24,2816]{1,0:T(8,128)(2,1)S(1)} %shard_map.145.refs_2_), channel_id=1, source_target_pairs={{0,2},{1,3},{2,0},{3,1},{4,6},{5,7},{6,4},{7,5},{8,10},{9,11},{10,... | collective-permute-start | bytes 405512 | tf_op jit(solution)/shard_map/ppermute | solution.py:55
  36.4 0.2 collective-permute-start.13
  36.6 0.8 %collective-permute-done.10.far.far_stats.refs_3_.refs_5_ = bf16[24,2944]{1,0:T(8,128)(2,1)S(1)} collective-permute-done((bf16[24,2944]{1,0:T(8,128)(2,1)S(1)}, bf16[24,2944]{1,0:T(8,128)(2,1)S(1)}, u32[]{:S(2)}, u32[]{:S(2)}) %collective-permute-start.10) | collective-permute-done | bytes 141344 | tf_op jit(solution)/shard_map/ppermute | solution.py:55
  37.4 0.1 shard_map.147.refs_4_.refs_0_
  37.5 0.1 collective-permute-start.15
  37.6 0.9 %collective-permute-start.17 = (bf16[24,1408]{1,0:T(8,128)(2,1)S(1)}, bf16[24,1408]{1,0:T(8,128)(2,1)S(1)}, u32[]{:S(2)}, u32[]{:S(2)}) collective-permute-start(bf16[24,1408]{1,0:T(8,128)(2,1)S(1)} %shard_map.147.refs_4_.refs_0_), channel_id=1, source_target_pairs={{0,2},{1,3},{2,0},{3,1},{4,6},{5,7},{6,4},{7,5},{8,10},{9,11},{10,... | collective-permute-start | bytes 202760 | tf_op jit(solution)/shard_map/ppermute | solution.py:55
  38.6 0.2 collective-permute-done.15.refs_1_
  38.9 0.4 slice-done.8
  39.3 1.3 %shard_map.149.refs_6_.refs_2_ = f32[128,512]{1,0:T(8,128)S(1)} custom-call(bf16[8,512,1408]{2,1,0:T(8,128)(2,1)S(1)} %bitcast.17, bf16[8,24,128]{2,1,0:T(8,128)(2,1)S(1)} %get-tuple-element.67.high, bf16[8,24,128]{2,1,0:T(8,128)(2,1)S(1)} %get-tuple-element.68.low, bf16[24,1408]{1,0:T(8,128)(2,1)S(1)} %shard_map.147.refs_4_.refs_0_, ...), custom_call_target="tpu_custom_call" | custom-call | tf_op jit(solution)/shard_map/pallas_call | solution.py:64
  40.6 1.0 %collective-permute-done.14.refs_2_ = bf16[24,2816]{1,0:T(8,128)(2,1)S(1)} collective-permute-done((bf16[24,2816]{1,0:T(8,128)(2,1)S(1)}, bf16[24,2816]{1,0:T(8,128)(2,1)S(1)}, u32[]{:S(2)}, u32[]{:S(2)}) %collective-permute-start.14) | collective-permute-done | bytes 135200 | tf_op jit(solution)/shard_map/ppermute | solution.py:55
  41.7 0.1 shard_map.150.refs_0_
  41.8 0.1 collective-permute-start.18
  41.9 1.2 %collective-permute-start.16 = (bf16[24,1408]{1,0:T(8,128)(2,1)S(1)}, bf16[24,1408]{1,0:T(8,128)(2,1)S(1)}, u32[]{:S(2)}, u32[]{:S(2)}) collective-permute-start(bf16[24,1408]{1,0:T(8,128)(2,1)S(1)} %shard_map.150.refs_0_), channel_id=1, source_target_pairs={{0,2},{1,3},{2,0},{3,1},{4,6},{5,7},{6,4},{7,5},{8,10},{9,11},{10,... | collective-permute-start | bytes 202760 | tf_op jit(solution)/shard_map/ppermute | solution.py:55
  43.1 0.2 collective-permute-start.20
  43.3 1.3 %shard_map.151.refs_1_ = f32[128,512]{1,0:T(8,128)S(1)} custom-call(bf16[8,512,1408]{2,1,0:T(8,128)(2,1)S(1)} %bitcast.17, bf16[8,24,128]{2,1,0:T(8,128)(2,1)S(1)} %get-tuple-element.67.high, bf16[8,24,128]{2,1,0:T(8,128)(2,1)S(1)} %get-tuple-element.68.low, bf16[24,1408]{1,0:T(8,128)(2,1)S(1)} %shard_map.150.refs_0_, ...), custom_call_target="tpu_custom_call" | custom-call | tf_op jit(solution)/shard_map/pallas_call | solution.py:64
  44.6 0.7 %shard_map.152.refs_2_ = f32[128,512]{1,0:T(8,128)S(1)} custom-call(bf16[8,512,1408]{2,1,0:T(8,128)(2,1)S(1)} %bitcast.17, bf16[8,24,128]{2,1,0:T(8,128)(2,1)S(1)} %get-tuple-element.67.high, bf16[8,24,128]{2,1,0:T(8,128)(2,1)S(1)} %get-tuple-element.68.low, bf16[24,1408]{1,0:T(8,128)(2,1)S(1)} %collective-permute-done.17.refs_0_, ...), custom_call_target="tpu_custom_call" | custom-call | tf_op jit(solution)/shard_map/pallas_call | solution.py:64
  45.3 1.1 %collective-permute-done.16.refs_0_ = bf16[24,1408]{1,0:T(8,128)(2,1)S(1)} collective-permute-done((bf16[24,1408]{1,0:T(8,128)(2,1)S(1)}, bf16[24,1408]{1,0:T(8,128)(2,1)S(1)}, u32[]{:S(2)}, u32[]{:S(2)}) %collective-permute-start.16) | collective-permute-done | bytes 67616 | tf_op jit(solution)/shard_map/ppermute | solution.py:55
  46.4 1.3 %shard_map.153.refs_1_ = f32[128,512]{1,0:T(8,128)S(1)} custom-call(bf16[8,512,1408]{2,1,0:T(8,128)(2,1)S(1)} %bitcast.17, bf16[8,24,128]{2,1,0:T(8,128)(2,1)S(1)} %get-tuple-element.67.high, bf16[8,24,128]{2,1,0:T(8,128)(2,1)S(1)} %get-tuple-element.68.low, bf16[24,1408]{1,0:T(8,128)(2,1)S(1)} %collective-permute-done.16.refs_0_, ...), custom_call_target="tpu_custom_call" | custom-call | tf_op jit(solution)/shard_map/pallas_call | solution.py:64
  47.8 0.8 %shard_map.154 = bf16[8,16,512]{2,1,0:T(8,128)(2,1)S(1)} custom-call(bf16[8,512,1408]{2,1,0:T(8,128)(2,1)S(1)} %bitcast.17, bf16[8,24,128]{2,1,0:T(8,128)(2,1)S(1)} %get-tuple-element.67.high, bf16[8,24,128]{2,1,0:T(8,128)(2,1)S(1)} %get-tuple-element.68.low, bf16[24,1408]{1,0:T(8,128)(2,1)S(1)} %collective-permute-done.19.refs_0_, ...), custom_call_target="tpu_custom_call" | custom-call | tf_op jit(solution)/shard_map/pallas_call | solution.py:64
  48.5 10.7 %all_to_all.5.back = bf16[8,16,512]{2,1,0:T(8,128)(2,1)S(1)} all-to-all(bf16[8,16,512]{2,1,0:T(8,128)(2,1)S(1)} %shard_map.154), channel_id=1, replica_groups=mesh['grp'=8,'exp'=4] {'grp'}, dimensions={0} | all-to-all | bytes 262144 | tf_op jit(solution)/shard_map/all_to_all | solution.py:638
  59.3 0.6 %reshape.7 = bf16[1,4,4,512]{3,2,1,0:T(4,128)(2,1)} reshape(bf16[16,512]{1,0:T(8,128)(2,1)S(1)} %shard_map.155) | data formatting | bytes 32768 | tf_op jit(solution)/shard_map/reshape | solution.py:642
  (58 shorter events, 0.3 us)
Async XLA Ops:
  0.0 3.7 %copy-start.6 = (bf16[1,4,4,2048]{3,2,1,0:T(4,128)(2,1)S(1)}, bf16[1,4,4,2048]{3,2,1,0:T(4,128)(2,1)}, u32[]{:S(2)}) copy-start(bf16[1,4,4,2048]{3,2,1,0:T(4,128)(2,1)} %param.14) | copy-start | bytes 196612
  0.0 0.7 %copy-start.9 = (s32[1,4,4]{2,1,0:T(4,128)S(1)}, s32[1,4,4]{2,1,0:T(4,128)}, u32[]{:S(2)}) copy-start(s32[1,4,4]{2,1,0:T(4,128)} %param.15) | copy-start | bytes 196
  0.0 3.8 %copy-start = (bf16[2048,3,512]{2,0,1:T(8,128)(2,1)S(1)}, bf16[2048,3,512]{2,0,1:T(8,128)(2,1)}, u32[]{:S(2)}) copy-start(bf16[2048,3,512]{2,0,1:T(8,128)(2,1)} %param.17) | copy-start | bytes 18874372
  0.0 7.9 %copy-start.8 = (s32[1,4,4,6]{3,2,1,0:T(4,128)S(1)}, s32[1,4,4,6]{3,2,1,0:T(4,128)}, u32[]{:S(2)}) copy-start(s32[1,4,4,6]{3,2,1,0:T(4,128)} %param.16) | copy-start | bytes 1156
  0.0 7.9 %copy-start.2 = (bf16[1,1024,512]{2,1,0:T(8,128)(2,1)S(1)}, bf16[1,1024,512]{2,1,0:T(8,128)(2,1)}, u32[]{:S(2)}) copy-start(bf16[1,1024,512]{2,1,0:T(8,128)(2,1)} %param.19) | copy-start | bytes 3145732
  0.0 7.9 %copy-start.3 = (bf16[1,1024,512]{2,1,0:T(8,128)(2,1)S(1)}, bf16[1,1024,512]{2,1,0:T(8,128)(2,1)}, u32[]{:S(2)}) copy-start(bf16[1,1024,512]{2,1,0:T(8,128)(2,1)} %param.20) | copy-start | bytes 3145732
  0.0 7.9 %copy-start.4 = (bf16[1,4,60,512]{3,1,2,0:T(4,128)(2,1)S(1)}, bf16[1,4,60,512]{3,1,2,0:T(4,128)(2,1)}, u32[]{:S(2)}) copy-start(bf16[1,4,60,512]{3,1,2,0:T(4,128)(2,1)} %param.22) | copy-start | bytes 737284
  0.0 7.9 %copy-start.5 = (bf16[1,4,60,512]{3,1,2,0:T(4,128)(2,1)S(1)}, bf16[1,4,60,512]{3,1,2,0:T(4,128)(2,1)}, u32[]{:S(2)}) copy-start(bf16[1,4,60,512]{3,1,2,0:T(4,128)(2,1)} %param.23) | copy-start | bytes 737284
  0.7 4.6 %collective-permute-start = (s32[4,4]{1,0:T(4,128)S(1)}, s32[4,4]{1,0:T(4,128)S(1)}, u32[]{:S(2)}, u32[]{:S(2)}) collective-permute-start(s32[4,4]{1,0:T(4,128)S(1)} %bitcast.28), channel_id=1, source_target_pairs={{0,4},{4,0},{8,12},{12,8},{16,20},{20,16},{24,28},{28,24},{1,5},{5... | collective-permute-start | bytes 200 | tf_op jit(solution)/shard_map/ppermute | solution.py:55
  3.7 4.3 %collective-permute-start.1 = (bf16[4,4,2048]{2,1,0:T(4,128)(2,1)S(1)}, bf16[4,4,2048]{2,1,0:T(4,128)(2,1)S(1)}, u32[]{:S(2)}, u32[]{:S(2)}) collective-permute-start(bf16[4,4,2048]{2,1,0:T(4,128)(2,1)S(1)} %bitcast.24), channel_id=1, source_target_pairs={{0,4},{4,0},{8,12},{12,8},{16,20},{20,16},{24,28},{28,24},{1,5},{5... | collective-permute-start | bytes 196616 | tf_op jit(solution)/shard_map/ppermute | solution.py:55
  8.0 6.0 %copy-start.1 = (bf16[512,2048]{1,0:T(8,128)(2,1)S(1)}, bf16[512,2048]{1,0:T(8,128)(2,1)}, u32[]{:S(2)}) copy-start(bf16[512,2048]{1,0:T(8,128)(2,1)} %w_out.1) | copy-start | bytes 6291460
  9.9 9.7 %copy-start.7 = (bf16[512,64]{0,1:T(8,128)(2,1)S(1)}, bf16[512,64]{0,1:T(8,128)(2,1)}, u32[]{:S(2)}) copy-start(bf16[512,64]{0,1:T(8,128)(2,1)} %param.24) | copy-start | bytes 196612
  9.9 9.7 %copy-start.10 = (f32[512]{0:T(512)S(1)}, f32[512]{0:T(512)}, u32[]{:S(2)}) copy-start(f32[512]{0:T(512)} %param.25) | copy-start | bytes 6148
  9.9 4.1 %collective-permute-start.2 = (bf16[32,640]{1,0:T(8,128)(2,1)S(1)}, bf16[32,640]{1,0:T(8,128)(2,1)S(1)}, u32[]{:S(2)}, u32[]{:S(2)}) collective-permute-start(bf16[32,640]{1,0:T(8,128)(2,1)S(1)} %get-tuple-element.52.near), channel_id=1, source_target_pairs={{0,4},{4,0},{8,12},{12,8},{16,20},{20,16},{24,28},{28,24},{1,5},{5... | collective-permute-start | bytes 122888 | tf_op jit(solution)/shard_map/ppermute | solution.py:55
  14.6 1.9 %collective-permute-start.3 = (bf16[32,512]{1,0:T(8,128)(2,1)S(1)}, bf16[32,512]{1,0:T(8,128)(2,1)S(1)}, u32[]{:S(2)}, u32[]{:S(2)}) collective-permute-start(bf16[32,512]{1,0:T(8,128)(2,1)S(1)} %get-tuple-element.54), channel_id=1, source_target_pairs={{0,1},{1,0},{2,3},{3,2},{4,5},{5,4},{6,7},{7,6},{8,9},{9,8},{10,11... | collective-permute-start | bytes 98312 | tf_op jit(solution)/shard_map/ppermute | solution.py:55
  14.7 4.0 %collective-permute-start.4 = (bf16[32,512]{1,0:T(8,128)(2,1)S(1)}, bf16[32,512]{1,0:T(8,128)(2,1)S(1)}, u32[]{:S(2)}, u32[]{:S(2)}) collective-permute-start(bf16[32,512]{1,0:T(8,128)(2,1)S(1)} %get-tuple-element.55), channel_id=1, source_target_pairs={{0,2},{1,3},{2,0},{3,1},{4,6},{5,7},{6,4},{7,5},{8,10},{9,11},{10,... | collective-permute-start | bytes 98312 | tf_op jit(solution)/shard_map/ppermute | solution.py:55
  16.2 3.3 %collective-permute-start.5 = (bf16[32,512]{1,0:T(8,128)(2,1)S(1)}, bf16[32,512]{1,0:T(8,128)(2,1)S(1)}, u32[]{:S(2)}, u32[]{:S(2)}) collective-permute-start(bf16[32,512]{1,0:T(8,128)(2,1)S(1)} %get-tuple-element.56), channel_id=1, source_target_pairs={{0,3},{1,2},{2,1},{3,0},{4,7},{5,6},{6,5},{7,4},{8,11},{9,10},{10,... | collective-permute-start | bytes 98312 | tf_op jit(solution)/shard_map/ppermute | solution.py:55
  19.6 9.4 %slice-start = ((s8[23068672]{0:T(1024)(128)(4,1)}), s8[4194304]{0:T(1024)(128)(4,1)S(1)}, s32[]{:S(2)}) async-start(s8[23068672]{0:T(1024)(128)(4,1)} %bitcast.14), calls=%async_computation.1 | async-start | bytes 8388608
  19.6 9.4 %slice-start.1 = ((s8[23068672]{0:T(1024)(128)(4,1)}), s8[4194304]{0:T(1024)(128)(4,1)S(1)}, s32[]{:S(2)}) async-start(s8[23068672]{0:T(1024)(128)(4,1)} %bitcast.14), calls=%async_computation.2 | async-start | bytes 8388608
  19.6 9.4 %slice-start.2 = ((s8[23068672]{0:T(1024)(128)(4,1)}), s8[4194304]{0:T(1024)(128)(4,1)S(1)}, s32[]{:S(2)}) async-start(s8[23068672]{0:T(1024)(128)(4,1)} %bitcast.14), calls=%async_computation.3 | async-start | bytes 8388608
  20.0 9.0 %slice-start.3 = ((s8[23068672]{0:T(1024)(128)(4,1)}), s8[4194304]{0:T(1024)(128)(4,1)S(1)}, s32[]{:S(2)}) async-start(s8[23068672]{0:T(1024)(128)(4,1)} %bitcast.14), calls=%async_computation.4 | async-start | bytes 8388608
  20.0 9.0 %slice-start.4 = ((s8[23068672]{0:T(1024)(128)(4,1)}), s8[4194304]{0:T(1024)(128)(4,1)S(1)}, s32[]{:S(2)}) async-start(s8[23068672]{0:T(1024)(128)(4,1)} %bitcast.14), calls=%async_computation.5 | async-start | bytes 8388608
  20.0 9.0 %slice-start.5 = ((s8[23068672]{0:T(1024)(128)(4,1)}), s8[2097152]{0:T(1024)(128)(4,1)S(1)}, s32[]{:S(2)}) async-start(s8[23068672]{0:T(1024)(128)(4,1)} %bitcast.14), calls=%async_computation.6 | async-start | bytes 4194304
  20.0 5.9 %collective-permute-start.6 = (bf16[32,640]{1,0:T(8,128)(2,1)S(1)}, bf16[32,640]{1,0:T(8,128)(2,1)S(1)}, u32[]{:S(2)}, u32[]{:S(2)}) collective-permute-start(bf16[32,640]{1,0:T(8,128)(2,1)S(1)} %get-tuple-element.58.refs_3_), channel_id=1, source_target_pairs={{0,24},{4,28},{8,16},{12,20},{16,8},{20,12},{24,0},{28,4},{1,25},{... | collective-permute-start | bytes 122888 | tf_op jit(solution)/shard_map/ppermute | solution.py:55
  23.6 4.9 %collective-permute-start.7 = (bf16[32,640]{1,0:T(8,128)(2,1)S(1)}, bf16[32,640]{1,0:T(8,128)(2,1)S(1)}, u32[]{:S(2)}, u32[]{:S(2)}) collective-permute-start(bf16[32,640]{1,0:T(8,128)(2,1)S(1)} %get-tuple-element.58.refs_3_), channel_id=1, source_target_pairs={{0,16},{4,20},{8,24},{12,28},{16,0},{20,4},{24,8},{28,12},{1,17},{... | collective-permute-start | bytes 122888 | tf_op jit(solution)/shard_map/ppermute | solution.py:55
  23.7 4.9 %collective-permute-start.8 = (bf16[32,640]{1,0:T(8,128)(2,1)S(1)}, bf16[32,640]{1,0:T(8,128)(2,1)S(1)}, u32[]{:S(2)}, u32[]{:S(2)}) collective-permute-start(bf16[32,640]{1,0:T(8,128)(2,1)S(1)} %get-tuple-element.58.refs_3_), channel_id=1, source_target_pairs={{0,8},{4,12},{8,0},{12,4},{16,24},{20,28},{24,16},{28,20},{1,9},{5... | collective-permute-start | bytes 122888 | tf_op jit(solution)/shard_map/ppermute | solution.py:55
  29.6 1.4 %collective-permute-start.9 = (bf16[24,2944]{1,0:T(8,128)(2,1)S(1)}, bf16[24,2944]{1,0:T(8,128)(2,1)S(1)}, u32[]{:S(2)}, u32[]{:S(2)}) collective-permute-start(bf16[24,2944]{1,0:T(8,128)(2,1)S(1)} %shard_map.142.refs_2_), channel_id=1, source_target_pairs={{0,1},{1,0},{2,3},{3,2},{4,5},{5,4},{6,7},{7,6},{8,9},{9,8},{10,11... | collective-permute-start | bytes 423944 | tf_op jit(solution)/shard_map/ppermute | solution.py:55
  30.2 2.3 %collective-permute-start.11 = (bf16[24,2816]{1,0:T(8,128)(2,1)S(1)}, bf16[24,2816]{1,0:T(8,128)(2,1)S(1)}, u32[]{:S(2)}, u32[]{:S(2)}) collective-permute-start(bf16[24,2816]{1,0:T(8,128)(2,1)S(1)} %shard_map.143.refs_4_), channel_id=1, source_target_pairs={{0,1},{1,0},{2,3},{3,2},{4,5},{5,4},{6,7},{7,6},{8,9},{9,8},{10,11... | collective-permute-start | bytes 405512 | tf_op jit(solution)/shard_map/ppermute | solution.py:55
  31.6 5.8 %collective-permute-start.10 = (bf16[24,2944]{1,0:T(8,128)(2,1)S(1)}, bf16[24,2944]{1,0:T(8,128)(2,1)S(1)}, u32[]{:S(2)}, u32[]{:S(2)}) collective-permute-start(bf16[24,2944]{1,0:T(8,128)(2,1)S(1)} %get-tuple-element.64.refs_3_), channel_id=1, source_target_pairs={{0,2},{1,3},{2,0},{3,1},{4,6},{5,7},{6,4},{7,5},{8,10},{9,11},{10,... | collective-permute-start | bytes 423944 | tf_op jit(solution)/shard_map/ppermute | solution.py:55
  33.1 5.8 %slice-start.6 = ((s8[11534336]{0:T(1024)(128)(4,1)}), s8[4194304]{0:T(1024)(128)(4,1)S(1)}, s32[]{:S(2)}) async-start(s8[11534336]{0:T(1024)(128)(4,1)} %bitcast.16), calls=%async_computation.7 | async-start | bytes 8388608
  33.1 5.8 %slice-start.7 = ((s8[11534336]{0:T(1024)(128)(4,1)}), s8[4194304]{0:T(1024)(128)(4,1)S(1)}, s32[]{:S(2)}) async-start(s8[11534336]{0:T(1024)(128)(4,1)} %bitcast.16), calls=%async_computation.8 | async-start | bytes 8388608
  35.2 1.4 %collective-permute-start.12 = (bf16[24,2816]{1,0:T(8,128)(2,1)S(1)}, bf16[24,2816]{1,0:T(8,128)(2,1)S(1)}, u32[]{:S(2)}, u32[]{:S(2)}) collective-permute-start(bf16[24,2816]{1,0:T(8,128)(2,1)S(1)} %get-tuple-element.66), channel_id=1, source_target_pairs={{0,1},{1,0},{2,3},{3,2},{4,5},{5,4},{6,7},{7,6},{8,9},{9,8},{10,11... | collective-permute-start | bytes 405512 | tf_op jit(solution)/shard_map/ppermute | solution.py:55
  35.2 6.5 %collective-permute-start.14 = (bf16[24,2816]{1,0:T(8,128)(2,1)S(1)}, bf16[24,2816]{1,0:T(8,128)(2,1)S(1)}, u32[]{:S(2)}, u32[]{:S(2)}) collective-permute-start(bf16[24,2816]{1,0:T(8,128)(2,1)S(1)} %shard_map.145.refs_2_), channel_id=1, source_target_pairs={{0,2},{1,3},{2,0},{3,1},{4,6},{5,7},{6,4},{7,5},{8,10},{9,11},{10,... | collective-permute-start | bytes 405512 | tf_op jit(solution)/shard_map/ppermute | solution.py:55
  36.4 4.2 %collective-permute-start.13 = (bf16[24,2816]{1,0:T(8,128)(2,1)S(1)}, bf16[24,2816]{1,0:T(8,128)(2,1)S(1)}, u32[]{:S(2)}, u32[]{:S(2)}) collective-permute-start(bf16[24,2816]{1,0:T(8,128)(2,1)S(1)} %get-tuple-element.70), channel_id=1, source_target_pairs={{0,1},{1,0},{2,3},{3,2},{4,5},{5,4},{6,7},{7,6},{8,9},{9,8},{10,11... | collective-permute-start | bytes 405512 | tf_op jit(solution)/shard_map/ppermute | solution.py:55
  37.4 1.9 %slice-start.8 = ((s8[11534336]{0:T(1024)(128)(4,1)}), s8[3145728]{0:T(1024)(128)(4,1)S(1)}, s32[]{:S(2)}) async-start(s8[11534336]{0:T(1024)(128)(4,1)} %bitcast.16), calls=%async_computation.9 | async-start | bytes 6291456
  37.5 1.3 %collective-permute-start.15 = (bf16[24,1408]{1,0:T(8,128)(2,1)S(1)}, bf16[24,1408]{1,0:T(8,128)(2,1)S(1)}, u32[]{:S(2)}, u32[]{:S(2)}) collective-permute-start(bf16[24,1408]{1,0:T(8,128)(2,1)S(1)} %shard_map.147.refs_4_.refs_0_), channel_id=1, source_target_pairs={{0,1},{1,0},{2,3},{3,2},{4,5},{5,4},{6,7},{7,6},{8,9},{9,8},{10,11... | collective-permute-start | bytes 202760 | tf_op jit(solution)/shard_map/ppermute | solution.py:55
  37.6 5.5 %collective-permute-start.17 = (bf16[24,1408]{1,0:T(8,128)(2,1)S(1)}, bf16[24,1408]{1,0:T(8,128)(2,1)S(1)}, u32[]{:S(2)}, u32[]{:S(2)}) collective-permute-start(bf16[24,1408]{1,0:T(8,128)(2,1)S(1)} %shard_map.147.refs_4_.refs_0_), channel_id=1, source_target_pairs={{0,2},{1,3},{2,0},{3,1},{4,6},{5,7},{6,4},{7,5},{8,10},{9,11},{10,... | collective-permute-start | bytes 202760 | tf_op jit(solution)/shard_map/ppermute | solution.py:55
  41.8 1.5 %collective-permute-start.18 = (bf16[24,1408]{1,0:T(8,128)(2,1)S(1)}, bf16[24,1408]{1,0:T(8,128)(2,1)S(1)}, u32[]{:S(2)}, u32[]{:S(2)}) collective-permute-start(bf16[24,1408]{1,0:T(8,128)(2,1)S(1)} %shard_map.150.refs_0_), channel_id=1, source_target_pairs={{0,1},{1,0},{2,3},{3,2},{4,5},{5,4},{6,7},{7,6},{8,9},{9,8},{10,11... | collective-permute-start | bytes 202760 | tf_op jit(solution)/shard_map/ppermute | solution.py:55
  41.9 4.6 %collective-permute-start.16 = (bf16[24,1408]{1,0:T(8,128)(2,1)S(1)}, bf16[24,1408]{1,0:T(8,128)(2,1)S(1)}, u32[]{:S(2)}, u32[]{:S(2)}) collective-permute-start(bf16[24,1408]{1,0:T(8,128)(2,1)S(1)} %shard_map.150.refs_0_), channel_id=1, source_target_pairs={{0,2},{1,3},{2,0},{3,1},{4,6},{5,7},{6,4},{7,5},{8,10},{9,11},{10,... | collective-permute-start | bytes 202760 | tf_op jit(solution)/shard_map/ppermute | solution.py:55
  43.1 3.3 %collective-permute-start.20 = (bf16[24,1408]{1,0:T(8,128)(2,1)S(1)}, bf16[24,1408]{1,0:T(8,128)(2,1)S(1)}, u32[]{:S(2)}, u32[]{:S(2)}) collective-permute-start(bf16[24,1408]{1,0:T(8,128)(2,1)S(1)} %collective-permute-done.17.refs_0_), channel_id=1, source_target_pairs={{0,1},{1,0},{2,3},{3,2},{4,5},{5,4},{6,7},{7,6},{8,9},{9,8},{10,11... | collective-permute-start | bytes 202760 | tf_op jit(solution)/shard_map/ppermute | solution.py:55
  46.4 1.3 %collective-permute-start.19 = (bf16[24,1408]{1,0:T(8,128)(2,1)S(1)}, bf16[24,1408]{1,0:T(8,128)(2,1)S(1)}, u32[]{:S(2)}, u32[]{:S(2)}) collective-permute-start(bf16[24,1408]{1,0:T(8,128)(2,1)S(1)} %collective-permute-done.16.refs_0_), channel_id=1, source_target_pairs={{0,1},{1,0},{2,3},{3,2},{4,5},{5,4},{6,7},{7,6},{8,9},{9,8},{10,11... | collective-permute-start | bytes 202760 | tf_op jit(solution)/shard_map/ppermute | solution.py:55

commit v4 on v3

--- a/solution.py
+++ b/solution.py
@@ -100,12 +100,33 @@
     return mine
 
 
-def own_kernel(x_own, wqkv, query, keys, values, part):
+def send_kernel(x_own, parents, routes, out):
     rows = slot_rows(x_own)
-    part[...] = feature_part(rows, part.shape[1])
-    rows = rows.astype(BF)
+    depth = rows.shape[1]
+    out[:, :depth] = rows.astype(BF)
+    lane = iota((ROWS, LANES), 1)
+    info = jnp.zeros((ROWS, LANES), F32)
+    named = slot_rows(routes)
+    for k in range(TOPK):
+        info = jnp.where(lane == k, named[:, k : k + 1], info)
+    same = iota((HALF, HALF), 0) == iota((HALF, HALF), 1)
+    columns = [
+        jnp.sum(
+            jnp.where(same, parents[step : step + 1, :].astype(F32), 0.0), axis=1, keepdims=True
+        )
+        for step in range(STEPS)
+    ]
+    info = jnp.where(lane == TOPK, jnp.concatenate(columns, axis=0), info)
+    out[:, depth:] = info.astype(BF)
+
+
+def own_kernel(sent, wqkv, tk_raw, tv_raw, query, keys, values, part, tk, tv):
+    rows = sent[:, : wqkv.shape[1]]
+    part[...] = feature_part(rows.astype(F32), part.shape[1])
     for k, out in enumerate((query, keys, values)):
         out[...] = dot(rows, wqkv[k]).astype(BF)
+    tk[...] = tk_raw[...].reshape(tk.shape)
+    tv[...] = tv_raw[...].reshape(tv.shape)
 
 
 def in_order(first, own, far):
@@ -125,10 +146,8 @@
     order,
     tail_at,
     new_at,
-    par_own,
-    par_far,
-    routes,
-    x_far,
+    sent,
+    came,
     query_own,
     part_own,
     wqkv,
@@ -136,34 +155,34 @@
     value_new,
     kp,
     vp,
-    tk_raw,
-    tv_raw,
+    tk,
+    tv,
     out,
     x_out,
+    named,
 ):
     half = lax.axis_index("grp") % 2
     first = half == 0
     width = kp.shape[1]
     heads = width // HDIM
-    far_rows = slot_rows(x_far)
-    x_out[...] = in_order(first, part_own[...], feature_part(far_rows, part_own.shape[1]))
-    query_far = dot(far_rows.astype(BF), wqkv[0]).astype(BF)
+    depth = wqkv.shape[1]
+    far_rows = came[:, :depth]
+    part_far = feature_part(far_rows.astype(F32), part_own.shape[1])
+    x_out[...] = in_order(first, part_own[...], part_far)
+    names = in_order(first, sent[:, depth:].astype(F32), came[:, depth:].astype(F32))
+    named[...] = names
+    parents = names[:, TOPK : TOPK + 1]
+    query_far = dot(far_rows, wqkv[0]).astype(BF)
     query = in_order(first, query_own[...], query_far)
     lane = iota((BEAMS, LANES), 1)
     beam = iota((BEAMS, LANES), 0)
     state = (lane == beam).astype(F32)
     states = []
-    same = iota((HALF, HALF), 0) == iota((HALF, HALF), 1)
     for step in range(STEPS):
-        columns = [
-            jnp.sum(
-                jnp.where(same, source[step : step + 1, :].astype(F32), 0.0),
-                axis=1,
-                keepdims=True,
-            )
-            for source in (par_own, par_far)
-        ]
-        parent = in_order(first, *columns)
+        at = step * HALF
+        parent = jnp.concatenate(
+            [parents[at : at + HALF], parents[ROWS + at : ROWS + at + HALF]], axis=0
+        )
         taken = jnp.zeros((BEAMS, LANES), F32)
         for j in range(BEAMS):
             taken = taken + jnp.where(parent == float(j), state[j : j + 1, :], 0.0)
@@ -176,13 +195,11 @@
     lanes = heads * PAIR
     owner = iota((lanes, width), 0) // PAIR == iota((lanes, width), 1) // HDIM
     spread = jnp.where(owner, spread.astype(F32), 0.0).astype(BF)
-    tk = tk_raw[...].reshape(PREV * HALF, width)
-    tv = tv_raw[...].reshape(PREV * HALF, width)
     cap = kp.shape[0]
     scale = HDIM ** (-0.5)
     live = iota((cap, lanes), 0) < parts[0]
     s_p = jnp.where(live, dot_t(kp[...], spread) * scale, NEGATIVE)
-    s_t = jnp.where(dot_t(tail_at[...], held) > 0.5, dot_t(tk, spread) * scale, NEGATIVE)
+    s_t = jnp.where(dot_t(tail_at[...], held) > 0.5, dot_t(tk[...], spread) * scale, NEGATIVE)
     s_n = jnp.where(
         dot_t(new_at[...], held) > 0.5, dot_t(key_new[...], spread) * scale, NEGATIVE
     )
@@ -198,16 +215,12 @@
     )
     mix = (
         t_dot(p_p.astype(BF), vp[...])
-        + t_dot(p_t.astype(BF), tv)
+        + t_dot(p_t.astype(BF), tv[...])
         + t_dot(p_n.astype(BF), value_new[...])
     )
     columns = jnp.concatenate([top, total, jnp.zeros((6, lanes), F32)], axis=0).T
     info = jnp.zeros((PAIR, LANES), F32)
     info_lane = iota((PAIR, LANES), 1)
-    named = slot_rows(routes)
-    named = in_order(first, named, jnp.zeros_like(named))
-    for k in range(TOPK):
-        info = jnp.where(info_lane == 5 * heads + k, named[:, k : k + 1], info)
     for head in range(heads):
         at = slice(head * HDIM, (head + 1) * HDIM)
         these = slice(head * PAIR, (head + 1) * PAIR)
@@ -245,12 +258,9 @@
         out[...] = dot(attention, w_out[:, pl.ds(start, features)]).astype(out.dtype)
 
 
-def residual_kernel(x, gain, w_router, near, far, own, *rest):
+def residual_kernel(x, named, gain, w_router, own, *rest):
     others, (residual_out, message) = rest[:-2], rest[-2:]
     features = own.shape[1]
-    width = near.shape[1] - LANES
-    named = near[:, width:].astype(F32) + far[:, width:].astype(F32)
-    routes_at = 5 * (width // HDIM)
     residual = x[...] + own[...]
     for other in others:
         residual = residual + other[...].astype(F32)
@@ -263,7 +273,7 @@
     info = jnp.zeros((PAIR, LANES), F32)
     columns = [jnp.sum(residual * residual, axis=1, keepdims=True)]
     for k in range(TOPK):
-        route = named[:, routes_at + k : routes_at + k + 1]
+        route = named[:, k : k + 1]
         columns.append(jnp.sum(jnp.where(expert == route, logits, 0.0), axis=1, keepdims=True))
         info = jnp.where(lane == 2 * STATS + k, route, info)
     for at, column in enumerate(columns):
@@ -274,15 +284,16 @@
 
 
 def gather_kernel(local, *refs):
-    messages, (picked, stats, target, choice, rows) = refs[:-5][::-1], refs[-5:]
+    messages, (picked, stats, target, choice, rows, infos) = refs[:-6], refs[-6:]
     blocks = len(messages)
     tokens = blocks * PAIR
     features = rows.shape[1]
-    infos = []
+    request = lax.axis_index("grp") // 2
     for k, message in enumerate(messages):
-        rows[k * PAIR : (k + 1) * PAIR, :] = message[:, :features]
-        infos.append(message[:, features:].astype(F32))
-    info = jnp.concatenate(infos, axis=0).T
+        at = pl.ds(pl.multiple_of((request ^ k) * PAIR, PAIR), PAIR)
+        rows[at, :] = message[:, :features]
+        infos[at, :] = message[:, features:].astype(F32)
+    info = infos[...].T
     stats[...] = jnp.concatenate(
         [info[:STATS] + info[STATS : 2 * STATS], jnp.zeros((8 - STATS, tokens), F32)], axis=0
     )
@@ -408,12 +419,7 @@
     if not last:
         refs[0][...] = mixed
         return
-    send, rows = refs
-    rows[...] = mixed
-    request = lax.axis_index("grp") // 2
-    for group in range(send.shape[0]):
-        start = ((group // 2) ^ request) * PAIR + group % 2 * ROWS
-        send[group] = rows[pl.ds(pl.multiple_of(start, ROWS), ROWS), :].astype(BF)
+    refs[0][...] = mixed.astype(BF).reshape(refs[0].shape)
 
 
 def down_blocks(places, hiddens, weights, high, low, block, before=(), last=False, after=()):
@@ -433,7 +439,6 @@
         *hiddens,
         *before,
         after=after,
-        scratch=[pltpu.VMEM((tokens, features), F32)] if last else [],
     )
 
 
@@ -481,29 +486,40 @@
         [],
         flops=HINT,
     )
-    own_inputs, own_parents, columns = lax.optimization_barrier(
-        (step_inputs[0], parents[0], columns)
-    )
-    far_inputs, far_parents = exchanged((own_inputs, own_parents), "grp", 1)
-    query, keys_new, values_new, part = call(
+    sent = call(
+        send_kernel,
+        shape((ROWS, model + LANES), BF),
+        [VMEM] * 3,
+        step_inputs[0],
+        parents[0],
+        routes[0],
+        after=columns[:1],
+    )
+    came = exchanged(sent, "grp", 1)
+    query, keys_new, values_new, part, tail_k, tail_v = call(
         own_kernel,
-        (shape((ROWS, width), BF),) * 3 + (shape((ROWS, features), F32),),
-        [VMEM] * 2,
-        step_inputs[0],
+        (shape((ROWS, width), BF),) * 3
+        + (shape((ROWS, features), F32),)
+        + (shape((PREV * HALF, width), BF),) * 2,
+        [VMEM] * 4,
+        sent,
         w_all,
-        after=columns[:1],
+        tail_keys[0].transpose(1, 0, 2),
+        tail_values[0].transpose(1, 0, 2),
         flops=HINT // 4,
     )
-    near, x = call(
+    near, x, named = call(
         attend_kernel,
-        (shape((PAIR, width + LANES), BF), shape((PAIR, features), F32)),
-        [SMEM] + [VMEM] * 16,
+        (
+            shape((PAIR, width + LANES), BF),
+            shape((PAIR, features), F32),
+            shape((PAIR, LANES), F32),
+        ),
+        [SMEM] + [VMEM] * 14,
         prompt_parts,
         *columns,
-        parents[0],
-        far_parents,
-        routes[0],
-        far_inputs,
+        sent,
+        came,
         query,
         part,
         w_all,
@@ -511,8 +527,8 @@
         values_new,
         prompt_keys[0],
         prompt_values[0],
-        tail_keys[0].transpose(1, 0, 2),
-        tail_values[0].transpose(1, 0, 2),
+        tail_k,
+        tail_v,
         flops=HINT,
     )
     far = exchanged(near, "grp", 1)
@@ -529,12 +545,11 @@
     residual, message = call(
         residual_kernel,
         (shape((PAIR, features), F32), shape((PAIR, features + LANES), BF)),
-        [VMEM] * (6 + len(arrived)),
+        [VMEM] * (5 + len(arrived)),
         x,
+        named,
         norm_gain.reshape(1, features),
         w_router.T,
-        near,
-        far,
         terms[0],
         *arrived,
         flops=HINT,
@@ -550,8 +565,8 @@
             shape((8, tokens), F32),
         ),
         [VMEM] * requests,
-        *messages[::-1],
-        scratch=[pltpu.VMEM((tokens, features), BF)],
+        *messages,
+        scratch=[pltpu.VMEM((tokens, features), BF), pltpu.VMEM((tokens, LANES), F32)],
         flops=HINT,
     )
     if splits == 4 and local == 2 * splits:
@@ -564,13 +579,10 @@
         far_c0 = exchanged(c0, "exp", 2)
         (c1,) = gate(((2, 1),), far=(far_a1,), after=(c0,))
         far_c1 = exchanged(c1, "exp", 2)
-        b0, b1, d0, d1 = gate(
-            ((1, 0), (1, 1), (0, 0), (0, 1)),
-            dtypes=(BF, BF, F32, F32),
-            after=(c1,),
-            flops=5000000000,
-        )
-        far_b0, far_b1 = exchanged((b0, b1), "exp", 1)
+        b0, d0 = gate(((1, 0), (0, 0)), dtypes=(BF, F32), after=(c1,), flops=30 * HINT // 100)
+        far_b0 = exchanged(b0, "exp", 1)
+        b1, d1 = gate(((1, 1), (0, 1)), dtypes=(BF, F32), after=(d0,), flops=30 * HINT // 100)
+        far_b1 = exchanged(b1, "exp", 1)
 
         def hidden_of(pick, near, mid, far, after=()):
             return call(
@@ -584,10 +596,10 @@
                 stats,
                 far_c0,
                 after=after,
-                flops=2000000000,
+                flops=10 * HINT // 100,
             )
 
-        own0 = hidden_of(0, d0, far_b0, far_c0)
+        own0 = hidden_of(0, d0, far_b0, far_c0, after=(d1,))
         core0 = exchanged(own0, "exp", 1)
         y0 = exchanged(own0, "exp", 2)
         place = shape((local, picked.shape[1], tokens), BF)
@@ -600,19 +612,19 @@
             stats,
             far_c0,
             after=(own0,),
-            flops=2000000000,
+            flops=10 * HINT // 100,
         )
         down = functools.partial(down_blocks, weights=w_down, high=high, low=low, block=2)
-        mixed = down(((0, 0), (1, 0)), (own0, core0))
-        own1 = hidden_of(1, d1, far_b1, far_c1, after=(mixed,))
+        own1 = hidden_of(1, d1, far_b1, far_c1, after=(high,))
         core1 = exchanged(own1, "exp", 1)
         y1 = exchanged(own1, "exp", 2)
-        mixed = down(((0, 1), (1, 1)), (own1, core1), before=(mixed,))
+        mixed = down(((0, 0), (1, 0)), (own0, core0), after=(own1,))
+        y0, mixed = lax.optimization_barrier((y0, mixed))
         far0 = exchanged(y0, "exp", 1)
-        mixed = down(((2, 0),), (y0,), before=(mixed,))
+        mixed = down(((0, 1), (1, 1), (2, 0)), (own1, core1, y0), before=(mixed,))
         y1, mixed = lax.optimization_barrier((y1, mixed))
         far1 = exchanged(y1, "exp", 1)
-        mixed = down(((2, 1), (3, 0)), (y1, far0), before=(mixed,))
+        mixed = down(((3, 0), (2, 1)), (far0, y1), before=(mixed,))
         send = down(((3, 1),), (far1,), before=(mixed,), last=True)
     else:
         stats = lax.psum(stats, "exp")
@@ -632,9 +644,8 @@
             jnp.where(place, weight[:, None, :], 0.0),
             result.astype(BF).astype(F32),
             precision=lax.Precision.HIGHEST,
-        ).reshape(requests, 2 * ROWS, features)
-        order = jnp.arange(requests) ^ (lax.axis_index("grp") // 2)
-        send = mixed[order].reshape(groups, ROWS, features).astype(BF)
+        )
+        send = mixed.reshape(groups, ROWS, features).astype(BF)
     back = lax.all_to_all(send, "grp", split_axis=0, concat_axis=0, tiled=True)
     result = call(
         finish_kernel, shape((ROWS, features), BF), [VMEM] * 2, residual, back

time: 60.1 us -> 58.6 us (0.975)
  waiting for transfers between devices: 17.1 us -> 12.6 us
  starting transfers between devices: 14.9 us -> 17.3 us
  blocking collectives: 10.7 us -> 11.4 us
    ppermute x21 -> x20, waiting for transfers between devices: 17.1 us -> 12.6 us  [exchanged(): return lax.ppermute(value, axis, pairs)]
    ppermute x21 -> x20, starting transfers between devices: 14.9 us -> 17.3 us  [exchanged(): return lax.ppermute(value, axis, pairs)]
    all_to_all x1, blocking collectives: 10.7 us -> 11.4 us  [on_device(): back = lax.all_to_all(send, 'grp', split_axis=0, concat_axis=0, tiled=True)]
    pallas_call x20 -> x21, Pallas kernels: 14.5 us -> 14.6 us  [call(): pl.pallas_call(ordered if after else body, out_shape=outs, in_specs=list(...]
  transfers between devices with their start and end apart: 21 -> 20, of which waited for: 11 -> 11; matrix products, arithmetic and copies ran while one was open for 0% -> 0% of each run, Pallas kernels for 16% -> 17%
where the time goes in v4:
time: 58.6 us; the launch traced here: 58.4 us
  starting transfers between devices  17.3 us (30%)
  Pallas kernels  14.6 us (25%)
  waiting for transfers between devices  12.6 us (22%)
  blocking collectives  11.4 us (19%)
  local copies, waits for them, and re-layouts  1.48 us (3%)
  between operations  0.98 us (2%)
    ppermute x20, starting transfers between devices, exchanged(): return lax.ppermute(value, axis, pairs)  17.3 us
    pallas_call x21, Pallas kernels, call(): pl.pallas_call(ordered if after else body, out_shape=outs, in_specs=list(...  14.6 us
    ppermute x20, waiting for transfers between devices, exchanged(): return lax.ppermute(value, axis, pairs)  12.6 us
    all_to_all x1, blocking collectives, on_device(): back = lax.all_to_all(send, 'grp', split_axis=0, concat_axis=0, tiled=True)  11.4 us
  transfers between devices with their start and end apart: 20, of which 11 were waited for; matrix products, arithmetic and copies ran while one was open for 0% of the time, Pallas kernels for 17%

profile of v4, /device:TPU:0, one launch (start us, length us, event | category | flops | bytes accessed | tf_op | source)
XLA Modules:
  0.0 58.4 jit_solution(4235119272699099299)
XLA Ops:
  0.1 0.6 %copy-done.1 = s32[1,4,4,6]{3,2,1,0:T(4,128)S(1)} copy-done((s32[1,4,4,6]{3,2,1,0:T(4,128)S(1)}, s32[1,4,4,6]{3,2,1,0:T(4,128)}, u32[]{:S(2)}) %copy-start.1) | copy-done | bytes 408
  0.7 0.2 copy-done
  0.9 0.2 shard_map.137.sent
  1.0 3.0 %collective-permute-start = (bf16[16,2176]{1,0:T(8,128)(2,1)S(1)}, bf16[16,2176]{1,0:T(8,128)(2,1)S(1)}, u32[]{:S(2)}, u32[]{:S(2)}) collective-permute-start(bf16[16,2176]{1,0:T(8,128)(2,1)S(1)} %shard_map.137.sent), channel_id=1, source_target_pairs={{0,4},{4,0},{8,12},{12,8},{16,20},{20,16},{24,28},{28,24},{1,5},{5... | collective-permute-start | bytes 208904 | tf_op jit(solution)/shard_map/ppermute | solution.py:55
  4.0 0.9 %shard_map.138 = (bf16[16,512]{1,0:T(8,128)(2,1)S(1)}, bf16[16,512]{1,0:T(8,128)(2,1)S(1)}, bf16[16,512]{1,0:T(8,128)(2,1)S(1)}, f32[16,512]{1,0:T(8,128)S(1)}, ...) custom-call(bf16[16,2176]{1,0:T(8,128)(2,1)S(1)} %shard_map.137.sent, bf16[3,2048,512]{2,1,0:T(8,128)(2,1)S(1)} %bitcast.21, ...), custom_call_target="tpu_custom_call" | custom-call | flops 2500000000 | tf_op jit(solution)/shard_map/pallas_call | solution.py:64
  5.6 0.7 %collective-permute-done.came = bf16[16,2176]{1,0:T(8,128)(2,1)S(1)} collective-permute-done((bf16[16,2176]{1,0:T(8,128)(2,1)S(1)}, bf16[16,2176]{1,0:T(8,128)(2,1)S(1)}, u32[]{:S(2)}, u32[]{:S(2)}) %collective-permute-start) | collective-permute-done | bytes 69664 | tf_op jit(solution)/shard_map/ppermute | solution.py:55
  6.3 1.8 %shard_map.139 = (bf16[32,640]{1,0:T(8,128)(2,1)S(1)}, f32[32,512]{1,0:T(8,128)S(1)}, f32[32,128]{1,0:T(8,128)S(1)}) custom-call(s32[1]{0:T(128)S(6)} %copy.15.parts, bf16[32,32]{1,0:T(8,128)(2,1)S(1)} %get-tuple-element.39.refs_3_.order, bf16[240,128]{1,0:T(8,128)(2,1)S(1)} %get-tuple-element.40.tail_at, bf16[16,128]{1,0:T(8,128)(2,1)S(1)} %get-tuple-element.41.new_at, ...), custom_call_target="tpu_custom_call" | custom-call | flops 10000000000 | tf_op jit(solution)/shard_map/pallas_call | solution.py:64
  8.2 2.1 %collective-permute-start.1 = (bf16[32,640]{1,0:T(8,128)(2,1)S(1)}, bf16[32,640]{1,0:T(8,128)(2,1)S(1)}, u32[]{:S(2)}, u32[]{:S(2)}) collective-permute-start(bf16[32,640]{1,0:T(8,128)(2,1)S(1)} %get-tuple-element.50.near), channel_id=1, source_target_pairs={{0,4},{4,0},{8,12},{12,8},{16,20},{20,16},{24,28},{28,24},{1,5},{5... | collective-permute-start | bytes 122888 | tf_op jit(solution)/shard_map/ppermute | solution.py:55
  10.3 2.0 %collective-permute-done.1.far = bf16[32,640]{1,0:T(8,128)(2,1)S(1)} collective-permute-done((bf16[32,640]{1,0:T(8,128)(2,1)S(1)}, bf16[32,640]{1,0:T(8,128)(2,1)S(1)}, u32[]{:S(2)}, u32[]{:S(2)}) %collective-permute-start.1) | collective-permute-done | bytes 40992 | tf_op jit(solution)/shard_map/ppermute | solution.py:55
  12.2 0.6 %shard_map.140 = (f32[32,512]{1,0:T(8,128)S(1)}, bf16[32,512]{1,0:T(8,128)(2,1)S(1)}, bf16[32,512]{1,0:T(8,128)(2,1)S(1)}, bf16[32,512]{1,0:T(8,128)(2,1)S(1)}) custom-call(bf16[32,640]{1,0:T(8,128)(2,1)S(1)} %get-tuple-element.50.near, bf16[32,640]{1,0:T(8,128)(2,1)S(1)} %collective-permute-done.1.far, bf16[512,2048]{1,0:T(8,128)(2,1)S(1)} %copy-done.4), custom_call_target="tpu_custom_call" | custom-call | flops 10000000000 | tf_op jit(solution)/shard_map/pallas_call | solution.py:64
  12.9 2.1 %collective-permute-start.3 = (bf16[32,512]{1,0:T(8,128)(2,1)S(1)}, bf16[32,512]{1,0:T(8,128)(2,1)S(1)}, u32[]{:S(2)}, u32[]{:S(2)}) collective-permute-start(bf16[32,512]{1,0:T(8,128)(2,1)S(1)} %get-tuple-element.53), channel_id=1, source_target_pairs={{0,2},{1,3},{2,0},{3,1},{4,6},{5,7},{6,4},{7,5},{8,10},{9,11},{10,... | collective-permute-start | bytes 98312 | tf_op jit(solution)/shard_map/ppermute | solution.py:55
  15.1 1.9 %collective-permute-done.3.rest_1_ = bf16[32,512]{1,0:T(8,128)(2,1)S(1)} collective-permute-done((bf16[32,512]{1,0:T(8,128)(2,1)S(1)}, bf16[32,512]{1,0:T(8,128)(2,1)S(1)}, u32[]{:S(2)}, u32[]{:S(2)}) %collective-permute-start.3) | collective-permute-done | bytes 32800 | tf_op jit(solution)/shard_map/ppermute | solution.py:55
  17.0 1.4 %collective-permute-done.4.rest_2_ = bf16[32,512]{1,0:T(8,128)(2,1)S(1)} collective-permute-done((bf16[32,512]{1,0:T(8,128)(2,1)S(1)}, bf16[32,512]{1,0:T(8,128)(2,1)S(1)}, u32[]{:S(2)}, u32[]{:S(2)}) %collective-permute-start.4) | collective-permute-done | bytes 32800 | tf_op jit(solution)/shard_map/ppermute | solution.py:55
  18.4 0.4 shard_map.141
  18.8 3.7 %collective-permute-start.7 = (bf16[32,640]{1,0:T(8,128)(2,1)S(1)}, bf16[32,640]{1,0:T(8,128)(2,1)S(1)}, u32[]{:S(2)}, u32[]{:S(2)}) collective-permute-start(bf16[32,640]{1,0:T(8,128)(2,1)S(1)} %get-tuple-element.56.refs_0_), channel_id=1, source_target_pairs={{0,24},{4,28},{8,16},{12,20},{16,8},{20,12},{24,0},{28,4},{1,25},{... | collective-permute-start | bytes 122888 | tf_op jit(solution)/shard_map/ppermute | solution.py:55
  22.5 0.8 %collective-permute-start.5 = (bf16[32,640]{1,0:T(8,128)(2,1)S(1)}, bf16[32,640]{1,0:T(8,128)(2,1)S(1)}, u32[]{:S(2)}, u32[]{:S(2)}) collective-permute-start(bf16[32,640]{1,0:T(8,128)(2,1)S(1)} %get-tuple-element.56.refs_0_), channel_id=1, source_target_pairs={{0,8},{4,12},{8,0},{12,4},{16,24},{20,28},{24,16},{28,20},{1,9},{5... | collective-permute-start | bytes 122888 | tf_op jit(solution)/shard_map/ppermute | solution.py:55
  23.2 1.5 %collective-permute-done.7.refs_3_ = bf16[32,640]{1,0:T(8,128)(2,1)S(1)} collective-permute-done((bf16[32,640]{1,0:T(8,128)(2,1)S(1)}, bf16[32,640]{1,0:T(8,128)(2,1)S(1)}, u32[]{:S(2)}, u32[]{:S(2)}) %collective-permute-start.7) | collective-permute-done | bytes 40992 | tf_op jit(solution)/shard_map/ppermute | solution.py:55
  24.7 2.7 %collective-permute-done.6.refs_2_ = bf16[32,640]{1,0:T(8,128)(2,1)S(1)} collective-permute-done((bf16[32,640]{1,0:T(8,128)(2,1)S(1)}, bf16[32,640]{1,0:T(8,128)(2,1)S(1)}, u32[]{:S(2)}, u32[]{:S(2)}) %collective-permute-start.6) | collective-permute-done | bytes 40992 | tf_op jit(solution)/shard_map/ppermute | solution.py:55
  27.4 0.4 shard_map.142
  27.8 0.6 %shard_map.143.refs_2_ = bf16[24,2944]{1,0:T(8,128)(2,1)S(1)} custom-call(bf16[8,512,2816]{2,1,0:T(8,128)(2,1)S(1)} %bitcast.15, bf16[8,24,512]{2,1,0:T(8,128)(2,1)S(1)} %get-tuple-element.59.picked.refs_1_, f32[8,128]{1,0:T(8,128)S(1)} %get-tuple-element.60.refs_0_.refs_2_), custom_call_target="tpu_custom_call" | custom-call | tf_op jit(solution)/shard_map/pallas_call | solution.py:64
  28.5 0.6 %shard_map.144.refs_4_ = bf16[24,2816]{1,0:T(8,128)(2,1)S(1)} custom-call(bf16[8,512,2816]{2,1,0:T(8,128)(2,1)S(1)} %bitcast.15, bf16[8,24,512]{2,1,0:T(8,128)(2,1)S(1)} %get-tuple-element.59.picked.refs_1_, bf16[24,2944]{1,0:T(8,128)(2,1)S(1)} %shard_map.143.refs_2_), custom_call_target="tpu_custom_call" | custom-call | tf_op jit(solution)/shard_map/pallas_call | solution.py:64
  29.1 0.5 collective-permute-start.10
  29.6 0.2 collective-permute-done.8.refs_3_
  29.8 0.6 %shard_map.145 = (bf16[24,2944]{1,0:T(8,128)(2,1)S(1)}, f32[8,128]{1,0:T(8,128)S(1)}) custom-call(bf16[8,512,2816]{2,1,0:T(8,128)(2,1)S(1)} %bitcast.15, bf16[8,24,512]{2,1,0:T(8,128)(2,1)S(1)} %get-tuple-element.59.picked.refs_1_, f32[8,128]{1,0:T(8,128)S(1)} %get-tuple-element.60.refs_0_.refs_2_, bf16[24,2944]{1,0:T(8,128)(2,1)S(1)} %collective-permute-done.8.refs_3_, ...), custom_call_target="tpu_custom_call" | custom-call | tf_op jit(solution)/shard_map/pallas_call | solution.py:64
  30.4 0.9 %collective-permute-start.9 = (bf16[24,2944]{1,0:T(8,128)(2,1)S(1)}, bf16[24,2944]{1,0:T(8,128)(2,1)S(1)}, u32[]{:S(2)}, u32[]{:S(2)}) collective-permute-start(bf16[24,2944]{1,0:T(8,128)(2,1)S(1)} %get-tuple-element.62.refs_3_), channel_id=1, source_target_pairs={{0,2},{1,3},{2,0},{3,1},{4,6},{5,7},{6,4},{7,5},{8,10},{9,11},{10,... | collective-permute-start | bytes 423944 | tf_op jit(solution)/shard_map/ppermute | solution.py:55
  31.3 0.6 %shard_map.146.refs_2_ = bf16[24,2816]{1,0:T(8,128)(2,1)S(1)} custom-call(bf16[8,512,2816]{2,1,0:T(8,128)(2,1)S(1)} %bitcast.15, bf16[8,24,512]{2,1,0:T(8,128)(2,1)S(1)} %get-tuple-element.59.picked.refs_1_, bf16[24,2816]{1,0:T(8,128)(2,1)S(1)} %collective-permute-done.10.refs_2_, bf16[24,2944]{1,0:T(8,128)(2,1)S(1)} %get-tuple-element.62.refs_3_), custom_call_target="tpu_custom_call" | custom-call | tf_op jit(solution)/shard_map/pallas_call | solution.py:64
  31.9 1.2 %collective-permute-start.13 = (bf16[24,2816]{1,0:T(8,128)(2,1)S(1)}, bf16[24,2816]{1,0:T(8,128)(2,1)S(1)}, u32[]{:S(2)}, u32[]{:S(2)}) collective-permute-start(bf16[24,2816]{1,0:T(8,128)(2,1)S(1)} %shard_map.146.refs_2_), channel_id=1, source_target_pairs={{0,2},{1,3},{2,0},{3,1},{4,6},{5,7},{6,4},{7,5},{8,10},{9,11},{10,... | collective-permute-start | bytes 405512 | tf_op jit(solution)/shard_map/ppermute | solution.py:55
  33.1 1.1 %shard_map.147 = (bf16[24,2816]{1,0:T(8,128)(2,1)S(1)}, f32[24,2816]{1,0:T(8,128)S(1)}) custom-call(bf16[8,512,2816]{2,1,0:T(8,128)(2,1)S(1)} %bitcast.15, bf16[8,24,512]{2,1,0:T(8,128)(2,1)S(1)} %get-tuple-element.59.picked.refs_1_, bf16[24,2816]{1,0:T(8,128)(2,1)S(1)} %shard_map.146.refs_2_), custom_call_target="tpu_custom_call" | custom-call | flops 3000000000 | tf_op jit(solution)/shard_map/pallas_call | solution.py:64
  34.2 1.1 %shard_map.148 = (bf16[24,2816]{1,0:T(8,128)(2,1)S(1)}, f32[24,2816]{1,0:T(8,128)S(1)}) custom-call(bf16[8,512,2816]{2,1,0:T(8,128)(2,1)S(1)} %bitcast.15, bf16[8,24,512]{2,1,0:T(8,128)(2,1)S(1)} %get-tuple-element.59.picked.refs_1_, f32[24,2816]{1,0:T(8,128)S(1)} %get-tuple-element.63.refs_2_.refs_0_), custom_call_target="tpu_custom_call" | custom-call | flops 3000000000 | tf_op jit(solution)/shard_map/pallas_call | solution.py:64
  35.3 0.5 collective-permute-start.12
  35.8 1.2 %collective-permute-done.9.refs_2_.refs_5_.refs_3_ = bf16[24,2944]{1,0:T(8,128)(2,1)S(1)} collective-permute-done((bf16[24,2944]{1,0:T(8,128)(2,1)S(1)}, bf16[24,2944]{1,0:T(8,128)(2,1)S(1)}, u32[]{:S(2)}, u32[]{:S(2)}) %collective-permute-start.9) | collective-permute-done | bytes 141344 | tf_op jit(solution)/shard_map/ppermute | solution.py:55
  37.0 0.1 shard_map.149.refs_4_.refs_3_
  37.2 0.1 collective-permute-start.17
  37.2 0.9 %collective-permute-start.16 = (bf16[24,1408]{1,0:T(8,128)(2,1)S(1)}, bf16[24,1408]{1,0:T(8,128)(2,1)S(1)}, u32[]{:S(2)}, u32[]{:S(2)}) collective-permute-start(bf16[24,1408]{1,0:T(8,128)(2,1)S(1)} %shard_map.149.refs_4_.refs_3_), channel_id=1, source_target_pairs={{0,2},{1,3},{2,0},{3,1},{4,6},{5,7},{6,4},{7,5},{8,10},{9,11},{10,... | collective-permute-start | bytes 202760 | tf_op jit(solution)/shard_map/ppermute | solution.py:55
  38.3 0.9 %collective-permute-done.13.refs_2_ = bf16[24,2816]{1,0:T(8,128)(2,1)S(1)} collective-permute-done((bf16[24,2816]{1,0:T(8,128)(2,1)S(1)}, bf16[24,2816]{1,0:T(8,128)(2,1)S(1)}, u32[]{:S(2)}, u32[]{:S(2)}) %collective-permute-start.13) | collective-permute-done | bytes 135200 | tf_op jit(solution)/shard_map/ppermute | solution.py:55
  39.1 0.1 shard_map.151.refs_5_.refs_0_
  39.3 0.1 collective-permute-start.15
  39.3 0.9 %collective-permute-start.14 = (bf16[24,1408]{1,0:T(8,128)(2,1)S(1)}, bf16[24,1408]{1,0:T(8,128)(2,1)S(1)}, u32[]{:S(2)}, u32[]{:S(2)}) collective-permute-start(bf16[24,1408]{1,0:T(8,128)(2,1)S(1)} %shard_map.151.refs_5_.refs_0_), channel_id=1, source_target_pairs={{0,2},{1,3},{2,0},{3,1},{4,6},{5,7},{6,4},{7,5},{8,10},{9,11},{10,... | collective-permute-start | bytes 202760 | tf_op jit(solution)/shard_map/ppermute | solution.py:55
  40.3 1.3 %shard_map.152.refs_3_ = f32[128,512]{1,0:T(8,128)S(1)} custom-call(bf16[8,512,1408]{2,1,0:T(8,128)(2,1)S(1)} %bitcast.17, bf16[8,24,128]{2,1,0:T(8,128)(2,1)S(1)} %get-tuple-element.66.refs_6_.refs_1_.high, bf16[8,24,128]{2,1,0:T(8,128)(2,1)S(1)} %get-tuple-element.67.refs_2_.low, bf16[24,1408]{1,0:T(8,128)(2,1)S(1)} %shard_map.149.refs_4_.refs_3_, ...), custom_call_target="tpu_custom_call" | custom-call | tf_op jit(solution)/shard_map/pallas_call | solution.py:64
  41.6 0.1 collective-permute-done.16.refs_2_
  41.8 0.1 collective-permute-start.19
  41.9 1.9 %shard_map.153.refs_2_ = f32[128,512]{1,0:T(8,128)S(1)} custom-call(bf16[8,512,1408]{2,1,0:T(8,128)(2,1)S(1)} %bitcast.17, bf16[8,24,128]{2,1,0:T(8,128)(2,1)S(1)} %get-tuple-element.66.refs_6_.refs_1_.high, bf16[8,24,128]{2,1,0:T(8,128)(2,1)S(1)} %get-tuple-element.67.refs_2_.low, bf16[24,1408]{1,0:T(8,128)(2,1)S(1)} %shard_map.151.refs_5_.refs_0_, ...), custom_call_target="tpu_custom_call" | custom-call | tf_op jit(solution)/shard_map/pallas_call | solution.py:64
  43.8 0.1 collective-permute-done.14.refs_1_
  43.9 0.4 collective-permute-start.18
  44.3 1.3 %shard_map.154.refs_1_ = f32[128,512]{1,0:T(8,128)S(1)} custom-call(bf16[8,512,1408]{2,1,0:T(8,128)(2,1)S(1)} %bitcast.17, bf16[8,24,128]{2,1,0:T(8,128)(2,1)S(1)} %get-tuple-element.66.refs_6_.refs_1_.high, bf16[8,24,128]{2,1,0:T(8,128)(2,1)S(1)} %get-tuple-element.67.refs_2_.low, bf16[24,1408]{1,0:T(8,128)(2,1)S(1)} %collective-permute-done.19.refs_0_, ...), custom_call_target="tpu_custom_call" | custom-call | tf_op jit(solution)/shard_map/pallas_call | solution.py:64
  45.6 0.7 %shard_map.155 = bf16[8,16,512]{2,1,0:T(8,128)(2,1)S(1)} custom-call(bf16[8,512,1408]{2,1,0:T(8,128)(2,1)S(1)} %bitcast.17, bf16[8,24,128]{2,1,0:T(8,128)(2,1)S(1)} %get-tuple-element.66.refs_6_.refs_1_.high, bf16[8,24,128]{2,1,0:T(8,128)(2,1)S(1)} %get-tuple-element.67.refs_2_.low, bf16[24,1408]{1,0:T(8,128)(2,1)S(1)} %collective-permute-done.18.refs_0_, ...), custom_call_target="tpu_custom_call" | custom-call | tf_op jit(solution)/shard_map/pallas_call | solution.py:64
  46.4 11.4 %all_to_all.5.back = bf16[8,16,512]{2,1,0:T(8,128)(2,1)S(1)} all-to-all(bf16[8,16,512]{2,1,0:T(8,128)(2,1)S(1)} %shard_map.155), channel_id=1, replica_groups=mesh['grp'=8,'exp'=4] {'grp'}, dimensions={0} | all-to-all | bytes 262144 | tf_op jit(solution)/shard_map/all_to_all | solution.py:649
  57.8 0.6 %reshape.7 = bf16[1,4,4,512]{3,2,1,0:T(4,128)(2,1)} reshape(bf16[16,512]{1,0:T(8,128)(2,1)S(1)} %shard_map.156) | data formatting | bytes 32768 | tf_op jit(solution)/shard_map/reshape | solution.py:653
  (57 shorter events, 0.4 us)
Async XLA Ops:
  0.0 0.7 %copy-start.1 = (s32[1,4,4,6]{3,2,1,0:T(4,128)S(1)}, s32[1,4,4,6]{3,2,1,0:T(4,128)}, u32[]{:S(2)}) copy-start(s32[1,4,4,6]{3,2,1,0:T(4,128)} %param.16) | copy-start | bytes 1156
  0.0 0.7 %copy-start.2 = (s32[1,4,4]{2,1,0:T(4,128)S(1)}, s32[1,4,4]{2,1,0:T(4,128)}, u32[]{:S(2)}) copy-start(s32[1,4,4]{2,1,0:T(4,128)} %param.15) | copy-start | bytes 196
  0.0 0.9 %copy-start = (bf16[1,4,4,2048]{3,2,1,0:T(4,128)(2,1)S(1)}, bf16[1,4,4,2048]{3,2,1,0:T(4,128)(2,1)}, u32[]{:S(2)}) copy-start(bf16[1,4,4,2048]{3,2,1,0:T(4,128)(2,1)} %param.14) | copy-start | bytes 196612
  0.0 4.0 %copy-start.8 = (bf16[1,4,60,512]{3,1,2,0:T(4,128)(2,1)S(1)}, bf16[1,4,60,512]{3,1,2,0:T(4,128)(2,1)}, u32[]{:S(2)}) copy-start(bf16[1,4,60,512]{3,1,2,0:T(4,128)(2,1)} %param.23) | copy-start | bytes 737284
  0.0 4.0 %copy-start.7 = (bf16[1,4,60,512]{3,1,2,0:T(4,128)(2,1)S(1)}, bf16[1,4,60,512]{3,1,2,0:T(4,128)(2,1)}, u32[]{:S(2)}) copy-start(bf16[1,4,60,512]{3,1,2,0:T(4,128)(2,1)} %param.22) | copy-start | bytes 737284
  0.0 4.0 %copy-start.3 = (bf16[2048,3,512]{2,0,1:T(8,128)(2,1)S(1)}, bf16[2048,3,512]{2,0,1:T(8,128)(2,1)}, u32[]{:S(2)}) copy-start(bf16[2048,3,512]{2,0,1:T(8,128)(2,1)} %param.17) | copy-start | bytes 18874372
  0.0 6.3 %copy-start.6 = (bf16[1,1024,512]{2,1,0:T(8,128)(2,1)S(1)}, bf16[1,1024,512]{2,1,0:T(8,128)(2,1)}, u32[]{:S(2)}) copy-start(bf16[1,1024,512]{2,1,0:T(8,128)(2,1)} %param.20) | copy-start | bytes 3145732
  0.0 6.3 %copy-start.5 = (bf16[1,1024,512]{2,1,0:T(8,128)(2,1)S(1)}, bf16[1,1024,512]{2,1,0:T(8,128)(2,1)}, u32[]{:S(2)}) copy-start(bf16[1,1024,512]{2,1,0:T(8,128)(2,1)} %param.19) | copy-start | bytes 3145732
  1.0 5.2 %collective-permute-start = (bf16[16,2176]{1,0:T(8,128)(2,1)S(1)}, bf16[16,2176]{1,0:T(8,128)(2,1)S(1)}, u32[]{:S(2)}, u32[]{:S(2)}) collective-permute-start(bf16[16,2176]{1,0:T(8,128)(2,1)S(1)} %shard_map.137.sent), channel_id=1, source_target_pairs={{0,4},{4,0},{8,12},{12,8},{16,20},{20,16},{24,28},{28,24},{1,5},{5... | collective-permute-start | bytes 208904 | tf_op jit(solution)/shard_map/ppermute | solution.py:55
  6.3 5.9 %copy-start.4 = (bf16[512,2048]{1,0:T(8,128)(2,1)S(1)}, bf16[512,2048]{1,0:T(8,128)(2,1)}, u32[]{:S(2)}) copy-start(bf16[512,2048]{1,0:T(8,128)(2,1)} %w_out.1) | copy-start | bytes 6291460
  8.1 10.3 %copy-start.9 = (bf16[512,64]{0,1:T(8,128)(2,1)S(1)}, bf16[512,64]{0,1:T(8,128)(2,1)}, u32[]{:S(2)}) copy-start(bf16[512,64]{0,1:T(8,128)(2,1)} %param.24) | copy-start | bytes 196612
  8.2 10.2 %copy-start.10 = (f32[512]{0:T(512)S(1)}, f32[512]{0:T(512)}, u32[]{:S(2)}) copy-start(f32[512]{0:T(512)} %param.25) | copy-start | bytes 6148
  8.2 4.1 %collective-permute-start.1 = (bf16[32,640]{1,0:T(8,128)(2,1)S(1)}, bf16[32,640]{1,0:T(8,128)(2,1)S(1)}, u32[]{:S(2)}, u32[]{:S(2)}) collective-permute-start(bf16[32,640]{1,0:T(8,128)(2,1)S(1)} %get-tuple-element.50.near), channel_id=1, source_target_pairs={{0,4},{4,0},{8,12},{12,8},{16,20},{20,16},{24,28},{28,24},{1,5},{5... | collective-permute-start | bytes 122888 | tf_op jit(solution)/shard_map/ppermute | solution.py:55
  12.9 2.2 %collective-permute-start.2 = (bf16[32,512]{1,0:T(8,128)(2,1)S(1)}, bf16[32,512]{1,0:T(8,128)(2,1)S(1)}, u32[]{:S(2)}, u32[]{:S(2)}) collective-permute-start(bf16[32,512]{1,0:T(8,128)(2,1)S(1)} %get-tuple-element.52), channel_id=1, source_target_pairs={{0,1},{1,0},{2,3},{3,2},{4,5},{5,4},{6,7},{7,6},{8,9},{9,8},{10,11... | collective-permute-start | bytes 98312 | tf_op jit(solution)/shard_map/ppermute | solution.py:55
  12.9 4.1 %collective-permute-start.3 = (bf16[32,512]{1,0:T(8,128)(2,1)S(1)}, bf16[32,512]{1,0:T(8,128)(2,1)S(1)}, u32[]{:S(2)}, u32[]{:S(2)}) collective-permute-start(bf16[32,512]{1,0:T(8,128)(2,1)S(1)} %get-tuple-element.53), channel_id=1, source_target_pairs={{0,2},{1,3},{2,0},{3,1},{4,6},{5,7},{6,4},{7,5},{8,10},{9,11},{10,... | collective-permute-start | bytes 98312 | tf_op jit(solution)/shard_map/ppermute | solution.py:55
  15.0 3.3 %collective-permute-start.4 = (bf16[32,512]{1,0:T(8,128)(2,1)S(1)}, bf16[32,512]{1,0:T(8,128)(2,1)S(1)}, u32[]{:S(2)}, u32[]{:S(2)}) collective-permute-start(bf16[32,512]{1,0:T(8,128)(2,1)S(1)} %get-tuple-element.54), channel_id=1, source_target_pairs={{0,3},{1,2},{2,1},{3,0},{4,7},{5,6},{6,5},{7,4},{8,11},{9,10},{10,... | collective-permute-start | bytes 98312 | tf_op jit(solution)/shard_map/ppermute | solution.py:55
  18.4 9.4 %slice-start = ((s8[23068672]{0:T(1024)(128)(4,1)}), s8[4194304]{0:T(1024)(128)(4,1)S(1)}, s32[]{:S(2)}) async-start(s8[23068672]{0:T(1024)(128)(4,1)} %bitcast.14), calls=%async_computation.1 | async-start | bytes 8388608
  18.4 9.4 %slice-start.1 = ((s8[23068672]{0:T(1024)(128)(4,1)}), s8[4194304]{0:T(1024)(128)(4,1)S(1)}, s32[]{:S(2)}) async-start(s8[23068672]{0:T(1024)(128)(4,1)} %bitcast.14), calls=%async_computation.2 | async-start | bytes 8388608
  18.4 9.4 %slice-start.2 = ((s8[23068672]{0:T(1024)(128)(4,1)}), s8[4194304]{0:T(1024)(128)(4,1)S(1)}, s32[]{:S(2)}) async-start(s8[23068672]{0:T(1024)(128)(4,1)} %bitcast.14), calls=%async_computation.3 | async-start | bytes 8388608
  18.8 9.0 %slice-start.3 = ((s8[23068672]{0:T(1024)(128)(4,1)}), s8[4194304]{0:T(1024)(128)(4,1)S(1)}, s32[]{:S(2)}) async-start(s8[23068672]{0:T(1024)(128)(4,1)} %bitcast.14), calls=%async_computation.4 | async-start | bytes 8388608
  18.8 9.0 %slice-start.4 = ((s8[23068672]{0:T(1024)(128)(4,1)}), s8[4194304]{0:T(1024)(128)(4,1)S(1)}, s32[]{:S(2)}) async-start(s8[23068672]{0:T(1024)(128)(4,1)} %bitcast.14), calls=%async_computation.5 | async-start | bytes 8388608
  18.8 9.0 %slice-start.5 = ((s8[23068672]{0:T(1024)(128)(4,1)}), s8[2097152]{0:T(1024)(128)(4,1)S(1)}, s32[]{:S(2)}) async-start(s8[23068672]{0:T(1024)(128)(4,1)} %bitcast.14), calls=%async_computation.6 | async-start | bytes 4194304
  18.8 5.9 %collective-permute-start.7 = (bf16[32,640]{1,0:T(8,128)(2,1)S(1)}, bf16[32,640]{1,0:T(8,128)(2,1)S(1)}, u32[]{:S(2)}, u32[]{:S(2)}) collective-permute-start(bf16[32,640]{1,0:T(8,128)(2,1)S(1)} %get-tuple-element.56.refs_0_), channel_id=1, source_target_pairs={{0,24},{4,28},{8,16},{12,20},{16,8},{20,12},{24,0},{28,4},{1,25},{... | collective-permute-start | bytes 122888 | tf_op jit(solution)/shard_map/ppermute | solution.py:55
  22.5 4.9 %collective-permute-start.6 = (bf16[32,640]{1,0:T(8,128)(2,1)S(1)}, bf16[32,640]{1,0:T(8,128)(2,1)S(1)}, u32[]{:S(2)}, u32[]{:S(2)}) collective-permute-start(bf16[32,640]{1,0:T(8,128)(2,1)S(1)} %get-tuple-element.56.refs_0_), channel_id=1, source_target_pairs={{0,16},{4,20},{8,24},{12,28},{16,0},{20,4},{24,8},{28,12},{1,17},{... | collective-permute-start | bytes 122888 | tf_op jit(solution)/shard_map/ppermute | solution.py:55
  22.5 4.9 %collective-permute-start.5 = (bf16[32,640]{1,0:T(8,128)(2,1)S(1)}, bf16[32,640]{1,0:T(8,128)(2,1)S(1)}, u32[]{:S(2)}, u32[]{:S(2)}) collective-permute-start(bf16[32,640]{1,0:T(8,128)(2,1)S(1)} %get-tuple-element.56.refs_0_), channel_id=1, source_target_pairs={{0,8},{4,12},{8,0},{12,4},{16,24},{20,28},{24,16},{28,20},{1,9},{5... | collective-permute-start | bytes 122888 | tf_op jit(solution)/shard_map/ppermute | solution.py:55
  28.4 1.4 %collective-permute-start.8 = (bf16[24,2944]{1,0:T(8,128)(2,1)S(1)}, bf16[24,2944]{1,0:T(8,128)(2,1)S(1)}, u32[]{:S(2)}, u32[]{:S(2)}) collective-permute-start(bf16[24,2944]{1,0:T(8,128)(2,1)S(1)} %shard_map.143.refs_2_), channel_id=1, source_target_pairs={{0,1},{1,0},{2,3},{3,2},{4,5},{5,4},{6,7},{7,6},{8,9},{9,8},{10,11... | collective-permute-start | bytes 423944 | tf_op jit(solution)/shard_map/ppermute | solution.py:55
  29.1 2.3 %collective-permute-start.10 = (bf16[24,2816]{1,0:T(8,128)(2,1)S(1)}, bf16[24,2816]{1,0:T(8,128)(2,1)S(1)}, u32[]{:S(2)}, u32[]{:S(2)}) collective-permute-start(bf16[24,2816]{1,0:T(8,128)(2,1)S(1)} %shard_map.144.refs_4_), channel_id=1, source_target_pairs={{0,1},{1,0},{2,3},{3,2},{4,5},{5,4},{6,7},{7,6},{8,9},{9,8},{10,11... | collective-permute-start | bytes 405512 | tf_op jit(solution)/shard_map/ppermute | solution.py:55
  30.4 6.6 %collective-permute-start.9 = (bf16[24,2944]{1,0:T(8,128)(2,1)S(1)}, bf16[24,2944]{1,0:T(8,128)(2,1)S(1)}, u32[]{:S(2)}, u32[]{:S(2)}) collective-permute-start(bf16[24,2944]{1,0:T(8,128)(2,1)S(1)} %get-tuple-element.62.refs_3_), channel_id=1, source_target_pairs={{0,2},{1,3},{2,0},{3,1},{4,6},{5,7},{6,4},{7,5},{8,10},{9,11},{10,... | collective-permute-start | bytes 423944 | tf_op jit(solution)/shard_map/ppermute | solution.py:55
  31.9 7.2 %collective-permute-start.13 = (bf16[24,2816]{1,0:T(8,128)(2,1)S(1)}, bf16[24,2816]{1,0:T(8,128)(2,1)S(1)}, u32[]{:S(2)}, u32[]{:S(2)}) collective-permute-start(bf16[24,2816]{1,0:T(8,128)(2,1)S(1)} %shard_map.146.refs_2_), channel_id=1, source_target_pairs={{0,2},{1,3},{2,0},{3,1},{4,6},{5,7},{6,4},{7,5},{8,10},{9,11},{10,... | collective-permute-start | bytes 405512 | tf_op jit(solution)/shard_map/ppermute | solution.py:55
  34.2 1.6 %collective-permute-start.11 = (bf16[24,2816]{1,0:T(8,128)(2,1)S(1)}, bf16[24,2816]{1,0:T(8,128)(2,1)S(1)}, u32[]{:S(2)}, u32[]{:S(2)}) collective-permute-start(bf16[24,2816]{1,0:T(8,128)(2,1)S(1)} %get-tuple-element.64), channel_id=1, source_target_pairs={{0,1},{1,0},{2,3},{3,2},{4,5},{5,4},{6,7},{7,6},{8,9},{9,8},{10,11... | collective-permute-start | bytes 405512 | tf_op jit(solution)/shard_map/ppermute | solution.py:55
  34.2 6.1 %slice-start.6 = ((s8[11534336]{0:T(1024)(128)(4,1)}), s8[4194304]{0:T(1024)(128)(4,1)S(1)}, s32[]{:S(2)}) async-start(s8[11534336]{0:T(1024)(128)(4,1)} %bitcast.16), calls=%async_computation.7 | async-start | bytes 8388608
  34.2 6.1 %slice-start.7 = ((s8[11534336]{0:T(1024)(128)(4,1)}), s8[4194304]{0:T(1024)(128)(4,1)S(1)}, s32[]{:S(2)}) async-start(s8[11534336]{0:T(1024)(128)(4,1)} %bitcast.16), calls=%async_computation.8 | async-start | bytes 8388608
  34.2 6.1 %slice-start.8 = ((s8[11534336]{0:T(1024)(128)(4,1)}), s8[3145728]{0:T(1024)(128)(4,1)S(1)}, s32[]{:S(2)}) async-start(s8[11534336]{0:T(1024)(128)(4,1)} %bitcast.16), calls=%async_computation.9 | async-start | bytes 6291456
  35.3 3.8 %collective-permute-start.12 = (bf16[24,2816]{1,0:T(8,128)(2,1)S(1)}, bf16[24,2816]{1,0:T(8,128)(2,1)S(1)}, u32[]{:S(2)}, u32[]{:S(2)}) collective-permute-start(bf16[24,2816]{1,0:T(8,128)(2,1)S(1)} %get-tuple-element.68), channel_id=1, source_target_pairs={{0,1},{1,0},{2,3},{3,2},{4,5},{5,4},{6,7},{7,6},{8,9},{9,8},{10,11... | collective-permute-start | bytes 405512 | tf_op jit(solution)/shard_map/ppermute | solution.py:55
  37.2 3.1 %collective-permute-start.17 = (bf16[24,1408]{1,0:T(8,128)(2,1)S(1)}, bf16[24,1408]{1,0:T(8,128)(2,1)S(1)}, u32[]{:S(2)}, u32[]{:S(2)}) collective-permute-start(bf16[24,1408]{1,0:T(8,128)(2,1)S(1)} %shard_map.149.refs_4_.refs_3_), channel_id=1, source_target_pairs={{0,1},{1,0},{2,3},{3,2},{4,5},{5,4},{6,7},{7,6},{8,9},{9,8},{10,11... | collective-permute-start | bytes 202760 | tf_op jit(solution)/shard_map/ppermute | solution.py:55
  37.2 4.6 %collective-permute-start.16 = (bf16[24,1408]{1,0:T(8,128)(2,1)S(1)}, bf16[24,1408]{1,0:T(8,128)(2,1)S(1)}, u32[]{:S(2)}, u32[]{:S(2)}) collective-permute-start(bf16[24,1408]{1,0:T(8,128)(2,1)S(1)} %shard_map.149.refs_4_.refs_3_), channel_id=1, source_target_pairs={{0,2},{1,3},{2,0},{3,1},{4,6},{5,7},{6,4},{7,5},{8,10},{9,11},{10,... | collective-permute-start | bytes 202760 | tf_op jit(solution)/shard_map/ppermute | solution.py:55
  39.3 2.6 %collective-permute-start.15 = (bf16[24,1408]{1,0:T(8,128)(2,1)S(1)}, bf16[24,1408]{1,0:T(8,128)(2,1)S(1)}, u32[]{:S(2)}, u32[]{:S(2)}) collective-permute-start(bf16[24,1408]{1,0:T(8,128)(2,1)S(1)} %shard_map.151.refs_5_.refs_0_), channel_id=1, source_target_pairs={{0,1},{1,0},{2,3},{3,2},{4,5},{5,4},{6,7},{7,6},{8,9},{9,8},{10,11... | collective-permute-start | bytes 202760 | tf_op jit(solution)/shard_map/ppermute | solution.py:55
  39.3 4.6 %collective-permute-start.14 = (bf16[24,1408]{1,0:T(8,128)(2,1)S(1)}, bf16[24,1408]{1,0:T(8,128)(2,1)S(1)}, u32[]{:S(2)}, u32[]{:S(2)}) collective-permute-start(bf16[24,1408]{1,0:T(8,128)(2,1)S(1)} %shard_map.151.refs_5_.refs_0_), channel_id=1, source_target_pairs={{0,2},{1,3},{2,0},{3,1},{4,6},{5,7},{6,4},{7,5},{8,10},{9,11},{10,... | collective-permute-start | bytes 202760 | tf_op jit(solution)/shard_map/ppermute | solution.py:55
  41.8 2.5 %collective-permute-start.19 = (bf16[24,1408]{1,0:T(8,128)(2,1)S(1)}, bf16[24,1408]{1,0:T(8,128)(2,1)S(1)}, u32[]{:S(2)}, u32[]{:S(2)}) collective-permute-start(bf16[24,1408]{1,0:T(8,128)(2,1)S(1)} %collective-permute-done.16.refs_2_), channel_id=1, source_target_pairs={{0,1},{1,0},{2,3},{3,2},{4,5},{5,4},{6,7},{7,6},{8,9},{9,8},{10,11... | collective-permute-start | bytes 202760 | tf_op jit(solution)/shard_map/ppermute | solution.py:55
  43.9 1.7 %collective-permute-start.18 = (bf16[24,1408]{1,0:T(8,128)(2,1)S(1)}, bf16[24,1408]{1,0:T(8,128)(2,1)S(1)}, u32[]{:S(2)}, u32[]{:S(2)}) collective-permute-start(bf16[24,1408]{1,0:T(8,128)(2,1)S(1)} %collective-permute-done.14.refs_1_), channel_id=1, source_target_pairs={{0,1},{1,0},{2,3},{3,2},{4,5},{5,4},{6,7},{7,6},{8,9},{9,8},{10,11... | collective-permute-start | bytes 202760 | tf_op jit(solution)/shard_map/ppermute | solution.py:55

commit v5 on v4

--- a/solution.py
+++ b/solution.py
@@ -197,36 +197,34 @@
     spread = jnp.where(owner, spread.astype(F32), 0.0).astype(BF)
     cap = kp.shape[0]
     scale = HDIM ** (-0.5)
-    live = iota((cap, lanes), 0) < parts[0]
-    s_p = jnp.where(live, dot_t(kp[...], spread) * scale, NEGATIVE)
-    s_t = jnp.where(dot_t(tail_at[...], held) > 0.5, dot_t(tk[...], spread) * scale, NEGATIVE)
+    live = iota((lanes, cap), 1) < parts[0]
+    s_p = jnp.where(live, dot_t(spread, kp[...]) * scale, NEGATIVE)
+    s_t = jnp.where(dot_t(held, tail_at[...]) > 0.5, dot_t(spread, tk[...]) * scale, NEGATIVE)
     s_n = jnp.where(
-        dot_t(new_at[...], held) > 0.5, dot_t(key_new[...], spread) * scale, NEGATIVE
+        dot_t(held, new_at[...]) > 0.5, dot_t(spread, key_new[...]) * scale, NEGATIVE
     )
     top = jnp.maximum(
-        jnp.max(s_p, axis=0, keepdims=True),
-        jnp.maximum(jnp.max(s_t, axis=0, keepdims=True), jnp.max(s_n, axis=0, keepdims=True)),
+        jnp.max(s_p, axis=1, keepdims=True),
+        jnp.maximum(jnp.max(s_t, axis=1, keepdims=True), jnp.max(s_n, axis=1, keepdims=True)),
     )
     p_p, p_t, p_n = [jnp.exp(part - top) for part in (s_p, s_t, s_n)]
     total = (
-        jnp.sum(p_p, axis=0, keepdims=True)
-        + jnp.sum(p_t, axis=0, keepdims=True)
-        + jnp.sum(p_n, axis=0, keepdims=True)
+        jnp.sum(p_p, axis=1, keepdims=True)
+        + jnp.sum(p_t, axis=1, keepdims=True)
+        + jnp.sum(p_n, axis=1, keepdims=True)
     )
     mix = (
-        t_dot(p_p.astype(BF), vp[...])
-        + t_dot(p_t.astype(BF), tv[...])
-        + t_dot(p_n.astype(BF), value_new[...])
-    )
-    columns = jnp.concatenate([top, total, jnp.zeros((6, lanes), F32)], axis=0).T
+        dot(p_p.astype(BF), vp[...])
+        + dot(p_t.astype(BF), tv[...])
+        + dot(p_n.astype(BF), value_new[...])
+    )
     info = jnp.zeros((PAIR, LANES), F32)
     info_lane = iota((PAIR, LANES), 1)
     for head in range(heads):
         at = slice(head * HDIM, (head + 1) * HDIM)
         these = slice(head * PAIR, (head + 1) * PAIR)
         out[:, at] = mix[these, at].astype(BF)
-        parts_of = pieces(columns[these, 0:1], 3) + pieces(columns[these, 1:2], 2)
-        for k, column in enumerate(parts_of):
+        for k, column in enumerate(pieces(top[these], 3) + pieces(total[these], 2)):
             info = jnp.where(info_lane == k * heads + head, column, info)
     out[:, width:] = info.astype(BF)
 
@@ -284,16 +282,15 @@
 
 
 def gather_kernel(local, *refs):
-    messages, (picked, stats, target, choice, rows, infos) = refs[:-6], refs[-6:]
+    messages, (picked, stats, target, choice, rows) = refs[:-5], refs[-5:]
     blocks = len(messages)
     tokens = blocks * PAIR
     features = rows.shape[1]
-    request = lax.axis_index("grp") // 2
+    parts = []
     for k, message in enumerate(messages):
-        at = pl.ds(pl.multiple_of((request ^ k) * PAIR, PAIR), PAIR)
-        rows[at, :] = message[:, :features]
-        infos[at, :] = message[:, features:].astype(F32)
-    info = infos[...].T
+        rows[k * PAIR : (k + 1) * PAIR, :] = message[:, :features]
+        parts.append(message[:, features:].astype(F32))
+    info = jnp.concatenate(parts, axis=0).T
     stats[...] = jnp.concatenate(
         [info[:STATS] + info[STATS : 2 * STATS], jnp.zeros((8 - STATS, tokens), F32)], axis=0
     )
@@ -374,7 +371,7 @@
     )
 
 
-def place_kernel(local, target, choice, stats, far, high, low):
+def place_kernel(local, target, choice, stats, far, shared):
     stats = stats[...] + joined_rows(far[:, far.shape[1] - target.shape[1] :])
     inverse = lax.rsqrt(stats[0:1] / MODEL + EPSILON)
     logits = [stats[1 + k : 2 + k] * inverse for k in range(TOPK)]
@@ -385,12 +382,12 @@
     share = jnp.zeros(chosen.shape, F32)
     for k in range(TOPK):
         share = jnp.where(chosen == float(k), weights[k] / whole, share)
-    row = iota(high.shape[1:], 0).astype(F32)
+    capacity = shared.shape[2] // 2
+    row = iota((capacity, target.shape[1]), 0).astype(F32)
     for e in range(local):
         place = jnp.where(row == target[e : e + 1, :], share[e : e + 1], 0.0)
-        rounded = place.astype(BF)
-        high[e] = rounded
-        low[e] = (place - rounded.astype(F32)).astype(BF)
+        high = place.astype(BF).astype(F32)
+        shared[e] = jnp.concatenate([high, place - high], axis=0).T.astype(BF)
 
 
 def hidden_kernel(block, pick, near, mid, far, target, stats, far_stats, hidden):
@@ -407,46 +404,67 @@
     hidden[...] = (gate / (1.0 + jnp.exp(-gate)) * up).astype(BF)
 
 
-def down_kernel(places, block, last, count, weights, high, low, *refs):
+def down_kernel(places, block, last, count, weights, shared, *refs):
     hiddens, refs = refs[: len(places)], refs[len(places) :]
     before, refs = refs[:count], refs[count:]
     me = lax.axis_index("exp")
     mixed = before[0][...] if before else 0.0
     for hidden, (mask, pick) in zip(hiddens, places):
         at = (me ^ mask) * block + pick
-        result = dot_t(hidden[...], weights[at]).astype(BF)
-        mixed = mixed + (t_dot(high[at], result) + t_dot(low[at], result))
+        result = dot_t(hidden[...], weights[at]).astype(BF).astype(F32)
+        result = jnp.concatenate([result, result], axis=0).astype(BF)
+        mixed = mixed + dot(shared[at], result)
     if not last:
         refs[0][...] = mixed
         return
-    refs[0][...] = mixed.astype(BF).reshape(refs[0].shape)
-
-
-def down_blocks(places, hiddens, weights, high, low, block, before=(), last=False, after=()):
+    keep, send, last_send = refs
+    first = lax.axis_index("grp") % 2 == 0
+    for k in range(keep.shape[0]):
+        low = mixed[k * PAIR : k * PAIR + ROWS]
+        high = mixed[k * PAIR + ROWS : (k + 1) * PAIR]
+        keep[k] = jnp.where(first, low, high)
+        given = jnp.where(first, high, low).astype(BF)
+        if k:
+            send[k - 1] = given
+        else:
+            last_send[...] = given
+
+
+def down_blocks(places, hiddens, weights, shared, block, before=(), last=False, after=()):
     features, width = weights.shape[1:]
-    tokens = high.shape[2]
+    tokens = shared.shape[1]
     if last:
-        out = shape((tokens // ROWS, ROWS, features), BF)
+        count = tokens // PAIR
+        out = (
+            shape((count, ROWS, features), F32),
+            shape((count - 1, ROWS, features), BF),
+            shape((ROWS, features), BF),
+        )
     else:
         out = shape((tokens, features), F32)
     return call(
         functools.partial(down_kernel, places, block, last, len(before)),
         out,
-        [VMEM] * (3 + len(hiddens) + len(before)),
+        [VMEM] * (2 + len(hiddens) + len(before)),
         weights,
-        high,
-        low,
+        shared,
         *hiddens,
         *before,
         after=after,
     )
 
 
-def finish_kernel(residual, back, out):
+def fold_kernel(keep, far, *outs):
+    for k, out in enumerate(outs):
+        out[...] = (keep[k + 1] + far[k].astype(F32)).astype(out.dtype)
+
+
+def finish_kernel(residual, keep, far, *rest):
+    others, out = rest[:-1], rest[-1]
     half = lax.axis_index("grp") % 2
-    value = residual[pl.ds(pl.multiple_of(half * ROWS, ROWS), ROWS), :]
-    for group in range(back.shape[0]):
-        value = value + back[group].astype(F32)
+    value = residual[pl.ds(pl.multiple_of(half * ROWS, ROWS), ROWS), :] + keep[0] + far[...].astype(F32)
+    for other in others:
+        value = value + other[...].astype(F32)
     out[...] = value.astype(out.dtype)
 
 
@@ -566,7 +584,7 @@
         ),
         [VMEM] * requests,
         *messages,
-        scratch=[pltpu.VMEM((tokens, features), BF), pltpu.VMEM((tokens, LANES), F32)],
+        scratch=[pltpu.VMEM((tokens, features), BF)],
         flops=HINT,
     )
     if splits == 4 and local == 2 * splits:
@@ -602,10 +620,9 @@
         own0 = hidden_of(0, d0, far_b0, far_c0, after=(d1,))
         core0 = exchanged(own0, "exp", 1)
         y0 = exchanged(own0, "exp", 2)
-        place = shape((local, picked.shape[1], tokens), BF)
-        high, low = call(
+        shared = call(
             functools.partial(place_kernel, local),
-            (place, place),
+            shape((local, tokens, 2 * picked.shape[1]), BF),
             [VMEM] * 4,
             target,
             choice,
@@ -614,8 +631,8 @@
             after=(own0,),
             flops=10 * HINT // 100,
         )
-        down = functools.partial(down_blocks, weights=w_down, high=high, low=low, block=2)
-        own1 = hidden_of(1, d1, far_b1, far_c1, after=(high,))
+        down = functools.partial(down_blocks, weights=w_down, shared=shared, block=2)
+        own1 = hidden_of(1, d1, far_b1, far_c1, after=(shared,))
         core1 = exchanged(own1, "exp", 1)
         y1 = exchanged(own1, "exp", 2)
         mixed = down(((0, 0), (1, 0)), (own0, core0), after=(own1,))
@@ -625,7 +642,7 @@
         y1, mixed = lax.optimization_barrier((y1, mixed))
         far1 = exchanged(y1, "exp", 1)
         mixed = down(((3, 0), (2, 1)), (far0, y1), before=(mixed,))
-        send = down(((3, 1),), (far1,), before=(mixed,), last=True)
+        keep, send, last_send = down(((3, 1),), (far1,), before=(mixed,), last=True)
     else:
         stats = lax.psum(stats, "exp")
         sums = jnp.einsum("lcd,ldf->lcf", picked, w_gate_up, preferred_element_type=F32)
@@ -645,10 +662,27 @@
             result.astype(BF).astype(F32),
             precision=lax.Precision.HIGHEST,
         )
-        send = mixed.reshape(groups, ROWS, features).astype(BF)
-    back = lax.all_to_all(send, "grp", split_axis=0, concat_axis=0, tiled=True)
+        mixed = mixed.reshape(requests, 2, ROWS, features)
+        half = lax.axis_index("grp") % 2
+        keep = lax.dynamic_index_in_dim(mixed, half, 1, False)
+        send = lax.dynamic_index_in_dim(mixed, 1 - half, 1, False).astype(BF)
+        send, last_send = send[1:], send[0]
+    folded = call(
+        fold_kernel,
+        tuple(shape((ROWS, features), BF) for _ in range(1, requests)),
+        [VMEM] * 2,
+        keep,
+        exchanged(send, "grp", 1),
+    )
+    back = [exchanged(folded[k - 1], "grp", 2 * k) for k in range(1, requests)]
     result = call(
-        finish_kernel, shape((ROWS, features), BF), [VMEM] * 2, residual, back
+        finish_kernel,
+        shape((ROWS, features), BF),
+        [VMEM] * (3 + len(back)),
+        residual,
+        keep,
+        exchanged(last_send, "grp", 1),
+        *back[::-1],
     )
     return result.reshape(1, STEPS, HALF, features)
 

time: 58.6 us -> 57.5 us (0.981)
  blocking collectives: 11.4 us -> 0 us
  starting transfers between devices: 17.3 us -> 23.7 us
  waiting for transfers between devices: 12.6 us -> 17.2 us
  Pallas kernels: 14.6 us -> 13.9 us
    all_to_all x1 -> x0, blocking collectives: 11.4 us -> none  [on_device(): back = lax.all_to_all(send, 'grp', split_axis=0, concat_axis=0, tiled=True)]
    ppermute x20 -> x25, starting transfers between devices: 17.3 us -> 23.7 us  [exchanged(): return lax.ppermute(value, axis, pairs)]
    ppermute x20 -> x25, waiting for transfers between devices: 12.6 us -> 17.2 us  [exchanged(): return lax.ppermute(value, axis, pairs)]
    pallas_call x21 -> x22, Pallas kernels: 14.6 us -> 13.9 us  [call(): pl.pallas_call(ordered if after else body, out_shape=outs, in_specs=list(...]
  transfers between devices with their start and end apart: 20 -> 25, of which waited for: 11 -> 14; matrix products, arithmetic and copies ran while one was open for 0% -> 0% of each run, Pallas kernels for 17% -> 17%
where the time goes in v5:
time: 57.5 us; the launch traced here: 57.3 us
  starting transfers between devices  23.7 us (41%)
  waiting for transfers between devices  17.2 us (30%)
  Pallas kernels  13.9 us (24%)
  local copies, waits for them, and re-layouts  1.48 us (3%)
  between operations  0.99 us (2%)
    ppermute x25, starting transfers between devices, exchanged(): return lax.ppermute(value, axis, pairs)  23.7 us
    ppermute x25, waiting for transfers between devices, exchanged(): return lax.ppermute(value, axis, pairs)  17.2 us
    pallas_call x22, Pallas kernels, call(): pl.pallas_call(ordered if after else body, out_shape=outs, in_specs=list(...  13.9 us
  transfers between devices with their start and end apart: 25, of which 14 were waited for; matrix products, arithmetic and copies ran while one was open for 0% of the time, Pallas kernels for 17%

profile of v5, /device:TPU:0, one launch (start us, length us, event | category | flops | bytes accessed | tf_op | source)
XLA Modules:
  0.0 57.3 jit_solution(11419626780107260117)
XLA Ops:
  0.1 0.6 %copy-done.1 = s32[1,4,4,6]{3,2,1,0:T(4,128)S(1)} copy-done((s32[1,4,4,6]{3,2,1,0:T(4,128)S(1)}, s32[1,4,4,6]{3,2,1,0:T(4,128)}, u32[]{:S(2)}) %copy-start.1) | copy-done | bytes 408
  1.0 3.0 %collective-permute-start = (bf16[16,2176]{1,0:T(8,128)(2,1)S(1)}, bf16[16,2176]{1,0:T(8,128)(2,1)S(1)}, u32[]{:S(2)}, u32[]{:S(2)}) collective-permute-start(bf16[16,2176]{1,0:T(8,128)(2,1)S(1)} %shard_map.137.sent), channel_id=1, source_target_pairs={{0,4},{4,0},{8,12},{12,8},{16,20},{20,16},{24,28},{28,24},{1,5},{5... | collective-permute-start | bytes 208904 | tf_op jit(solution)/shard_map/ppermute | solution.py:55
  4.0 0.9 %shard_map.138 = (bf16[16,512]{1,0:T(8,128)(2,1)S(1)}, bf16[16,512]{1,0:T(8,128)(2,1)S(1)}, bf16[16,512]{1,0:T(8,128)(2,1)S(1)}, f32[16,512]{1,0:T(8,128)S(1)}, ...) custom-call(bf16[16,2176]{1,0:T(8,128)(2,1)S(1)} %shard_map.137.sent, bf16[3,2048,512]{2,1,0:T(8,128)(2,1)S(1)} %bitcast.21, ...), custom_call_target="tpu_custom_call" | custom-call | flops 2500000000 | tf_op jit(solution)/shard_map/pallas_call | solution.py:64
  5.6 0.7 %collective-permute-done.came = bf16[16,2176]{1,0:T(8,128)(2,1)S(1)} collective-permute-done((bf16[16,2176]{1,0:T(8,128)(2,1)S(1)}, bf16[16,2176]{1,0:T(8,128)(2,1)S(1)}, u32[]{:S(2)}, u32[]{:S(2)}) %collective-permute-start) | collective-permute-done | bytes 69664 | tf_op jit(solution)/shard_map/ppermute | solution.py:55
  6.3 1.4 %shard_map.139 = (bf16[32,640]{1,0:T(8,128)(2,1)S(1)}, f32[32,512]{1,0:T(8,128)S(1)}, f32[32,128]{1,0:T(8,128)S(1)}) custom-call(s32[1]{0:T(128)S(6)} %copy.15.parts, bf16[32,32]{1,0:T(8,128)(2,1)S(1)} %get-tuple-element.43.refs_3_.order, bf16[240,128]{1,0:T(8,128)(2,1)S(1)} %get-tuple-element.44.tail_at, bf16[16,128]{1,0:T(8,128)(2,1)S(1)} %get-tuple-element.45.new_at, ...), custom_call_target="tpu_custom_call" | custom-call | flops 10000000000 | tf_op jit(solution)/shard_map/pallas_call | solution.py:64
  7.8 2.1 %collective-permute-start.1 = (bf16[32,640]{1,0:T(8,128)(2,1)S(1)}, bf16[32,640]{1,0:T(8,128)(2,1)S(1)}, u32[]{:S(2)}, u32[]{:S(2)}) collective-permute-start(bf16[32,640]{1,0:T(8,128)(2,1)S(1)} %get-tuple-element.54.near), channel_id=1, source_target_pairs={{0,4},{4,0},{8,12},{12,8},{16,20},{20,16},{24,28},{28,24},{1,5},{5... | collective-permute-start | bytes 122888 | tf_op jit(solution)/shard_map/ppermute | solution.py:55
  9.8 2.0 %collective-permute-done.1.far = bf16[32,640]{1,0:T(8,128)(2,1)S(1)} collective-permute-done((bf16[32,640]{1,0:T(8,128)(2,1)S(1)}, bf16[32,640]{1,0:T(8,128)(2,1)S(1)}, u32[]{:S(2)}, u32[]{:S(2)}) %collective-permute-start.1) | collective-permute-done | bytes 40992 | tf_op jit(solution)/shard_map/ppermute | solution.py:55
  11.8 0.6 %shard_map.140 = (f32[32,512]{1,0:T(8,128)S(1)}, bf16[32,512]{1,0:T(8,128)(2,1)S(1)}, bf16[32,512]{1,0:T(8,128)(2,1)S(1)}, bf16[32,512]{1,0:T(8,128)(2,1)S(1)}) custom-call(bf16[32,640]{1,0:T(8,128)(2,1)S(1)} %get-tuple-element.54.near, bf16[32,640]{1,0:T(8,128)(2,1)S(1)} %collective-permute-done.1.far, bf16[512,2048]{1,0:T(8,128)(2,1)S(1)} %copy-done.4), custom_call_target="tpu_custom_call" | custom-call | flops 10000000000 | tf_op jit(solution)/shard_map/pallas_call | solution.py:64
  12.5 2.1 %collective-permute-start.3 = (bf16[32,512]{1,0:T(8,128)(2,1)S(1)}, bf16[32,512]{1,0:T(8,128)(2,1)S(1)}, u32[]{:S(2)}, u32[]{:S(2)}) collective-permute-start(bf16[32,512]{1,0:T(8,128)(2,1)S(1)} %get-tuple-element.57), channel_id=1, source_target_pairs={{0,2},{1,3},{2,0},{3,1},{4,6},{5,7},{6,4},{7,5},{8,10},{9,11},{10,... | collective-permute-start | bytes 98312 | tf_op jit(solution)/shard_map/ppermute | solution.py:55
  14.7 1.9 %collective-permute-done.3.rest_1_ = bf16[32,512]{1,0:T(8,128)(2,1)S(1)} collective-permute-done((bf16[32,512]{1,0:T(8,128)(2,1)S(1)}, bf16[32,512]{1,0:T(8,128)(2,1)S(1)}, u32[]{:S(2)}, u32[]{:S(2)}) %collective-permute-start.3) | collective-permute-done | bytes 32800 | tf_op jit(solution)/shard_map/ppermute | solution.py:55
  16.6 1.4 %collective-permute-done.4.rest_2_ = bf16[32,512]{1,0:T(8,128)(2,1)S(1)} collective-permute-done((bf16[32,512]{1,0:T(8,128)(2,1)S(1)}, bf16[32,512]{1,0:T(8,128)(2,1)S(1)}, u32[]{:S(2)}, u32[]{:S(2)}) %collective-permute-start.4) | collective-permute-done | bytes 32800 | tf_op jit(solution)/shard_map/ppermute | solution.py:55
  18.0 0.4 shard_map.141
  18.4 3.7 %collective-permute-start.7 = (bf16[32,640]{1,0:T(8,128)(2,1)S(1)}, bf16[32,640]{1,0:T(8,128)(2,1)S(1)}, u32[]{:S(2)}, u32[]{:S(2)}) collective-permute-start(bf16[32,640]{1,0:T(8,128)(2,1)S(1)} %get-tuple-element.60.refs_0_), channel_id=1, source_target_pairs={{0,24},{4,28},{8,16},{12,20},{16,8},{20,12},{24,0},{28,4},{1,25},{... | collective-permute-start | bytes 122888 | tf_op jit(solution)/shard_map/ppermute | solution.py:55
  22.0 0.8 %collective-permute-start.5 = (bf16[32,640]{1,0:T(8,128)(2,1)S(1)}, bf16[32,640]{1,0:T(8,128)(2,1)S(1)}, u32[]{:S(2)}, u32[]{:S(2)}) collective-permute-start(bf16[32,640]{1,0:T(8,128)(2,1)S(1)} %get-tuple-element.60.refs_0_), channel_id=1, source_target_pairs={{0,8},{4,12},{8,0},{12,4},{16,24},{20,28},{24,16},{28,20},{1,9},{5... | collective-permute-start | bytes 122888 | tf_op jit(solution)/shard_map/ppermute | solution.py:55
  22.8 1.5 %collective-permute-done.7.refs_3_ = bf16[32,640]{1,0:T(8,128)(2,1)S(1)} collective-permute-done((bf16[32,640]{1,0:T(8,128)(2,1)S(1)}, bf16[32,640]{1,0:T(8,128)(2,1)S(1)}, u32[]{:S(2)}, u32[]{:S(2)}) %collective-permute-start.7) | collective-permute-done | bytes 40992 | tf_op jit(solution)/shard_map/ppermute | solution.py:55
  24.3 2.7 %collective-permute-done.6.refs_2_ = bf16[32,640]{1,0:T(8,128)(2,1)S(1)} collective-permute-done((bf16[32,640]{1,0:T(8,128)(2,1)S(1)}, bf16[32,640]{1,0:T(8,128)(2,1)S(1)}, u32[]{:S(2)}, u32[]{:S(2)}) %collective-permute-start.6) | collective-permute-done | bytes 40992 | tf_op jit(solution)/shard_map/ppermute | solution.py:55
  26.9 0.4 shard_map.142
  27.4 0.6 %shard_map.143.refs_2_ = bf16[24,2944]{1,0:T(8,128)(2,1)S(1)} custom-call(bf16[8,512,2816]{2,1,0:T(8,128)(2,1)S(1)} %bitcast.15, bf16[8,24,512]{2,1,0:T(8,128)(2,1)S(1)} %get-tuple-element.63.picked.refs_1_, f32[8,128]{1,0:T(8,128)S(1)} %get-tuple-element.64.refs_0_.refs_2_), custom_call_target="tpu_custom_call" | custom-call | tf_op jit(solution)/shard_map/pallas_call | solution.py:64
  28.0 0.6 %shard_map.144.refs_4_ = bf16[24,2816]{1,0:T(8,128)(2,1)S(1)} custom-call(bf16[8,512,2816]{2,1,0:T(8,128)(2,1)S(1)} %bitcast.15, bf16[8,24,512]{2,1,0:T(8,128)(2,1)S(1)} %get-tuple-element.63.picked.refs_1_, bf16[24,2944]{1,0:T(8,128)(2,1)S(1)} %shard_map.143.refs_2_), custom_call_target="tpu_custom_call" | custom-call | tf_op jit(solution)/shard_map/pallas_call | solution.py:64
  28.6 0.5 collective-permute-start.10
  29.1 0.2 collective-permute-done.8.refs_3_
  29.4 0.6 %shard_map.145 = (bf16[24,2944]{1,0:T(8,128)(2,1)S(1)}, f32[8,128]{1,0:T(8,128)S(1)}) custom-call(bf16[8,512,2816]{2,1,0:T(8,128)(2,1)S(1)} %bitcast.15, bf16[8,24,512]{2,1,0:T(8,128)(2,1)S(1)} %get-tuple-element.63.picked.refs_1_, f32[8,128]{1,0:T(8,128)S(1)} %get-tuple-element.64.refs_0_.refs_2_, bf16[24,2944]{1,0:T(8,128)(2,1)S(1)} %collective-permute-done.8.refs_3_, ...), custom_call_target="tpu_custom_call" | custom-call | tf_op jit(solution)/shard_map/pallas_call | solution.py:64
  30.0 0.9 %collective-permute-start.9 = (bf16[24,2944]{1,0:T(8,128)(2,1)S(1)}, bf16[24,2944]{1,0:T(8,128)(2,1)S(1)}, u32[]{:S(2)}, u32[]{:S(2)}) collective-permute-start(bf16[24,2944]{1,0:T(8,128)(2,1)S(1)} %get-tuple-element.66.refs_3_), channel_id=1, source_target_pairs={{0,2},{1,3},{2,0},{3,1},{4,6},{5,7},{6,4},{7,5},{8,10},{9,11},{10,... | collective-permute-start | bytes 423944 | tf_op jit(solution)/shard_map/ppermute | solution.py:55
  30.9 0.6 %shard_map.146.refs_2_ = bf16[24,2816]{1,0:T(8,128)(2,1)S(1)} custom-call(bf16[8,512,2816]{2,1,0:T(8,128)(2,1)S(1)} %bitcast.15, bf16[8,24,512]{2,1,0:T(8,128)(2,1)S(1)} %get-tuple-element.63.picked.refs_1_, bf16[24,2816]{1,0:T(8,128)(2,1)S(1)} %collective-permute-done.10.refs_2_, bf16[24,2944]{1,0:T(8,128)(2,1)S(1)} %get-tuple-element.66.refs_3_), custom_call_target="tpu_custom_call" | custom-call | tf_op jit(solution)/shard_map/pallas_call | solution.py:64
  31.5 1.2 %collective-permute-start.13 = (bf16[24,2816]{1,0:T(8,128)(2,1)S(1)}, bf16[24,2816]{1,0:T(8,128)(2,1)S(1)}, u32[]{:S(2)}, u32[]{:S(2)}) collective-permute-start(bf16[24,2816]{1,0:T(8,128)(2,1)S(1)} %shard_map.146.refs_2_), channel_id=1, source_target_pairs={{0,2},{1,3},{2,0},{3,1},{4,6},{5,7},{6,4},{7,5},{8,10},{9,11},{10,... | collective-permute-start | bytes 405512 | tf_op jit(solution)/shard_map/ppermute | solution.py:55
  32.7 1.1 %shard_map.147 = (bf16[24,2816]{1,0:T(8,128)(2,1)S(1)}, f32[24,2816]{1,0:T(8,128)S(1)}) custom-call(bf16[8,512,2816]{2,1,0:T(8,128)(2,1)S(1)} %bitcast.15, bf16[8,24,512]{2,1,0:T(8,128)(2,1)S(1)} %get-tuple-element.63.picked.refs_1_, bf16[24,2816]{1,0:T(8,128)(2,1)S(1)} %shard_map.146.refs_2_), custom_call_target="tpu_custom_call" | custom-call | flops 3000000000 | tf_op jit(solution)/shard_map/pallas_call | solution.py:64
  33.8 1.1 %shard_map.148 = (bf16[24,2816]{1,0:T(8,128)(2,1)S(1)}, f32[24,2816]{1,0:T(8,128)S(1)}) custom-call(bf16[8,512,2816]{2,1,0:T(8,128)(2,1)S(1)} %bitcast.15, bf16[8,24,512]{2,1,0:T(8,128)(2,1)S(1)} %get-tuple-element.63.picked.refs_1_, f32[24,2816]{1,0:T(8,128)S(1)} %get-tuple-element.67.refs_2_.refs_0_), custom_call_target="tpu_custom_call" | custom-call | flops 3000000000 | tf_op jit(solution)/shard_map/pallas_call | solution.py:64
  34.9 0.5 collective-permute-start.12
  35.4 1.2 %collective-permute-done.9.refs_2_.refs_5_.refs_3_ = bf16[24,2944]{1,0:T(8,128)(2,1)S(1)} collective-permute-done((bf16[24,2944]{1,0:T(8,128)(2,1)S(1)}, bf16[24,2944]{1,0:T(8,128)(2,1)S(1)}, u32[]{:S(2)}, u32[]{:S(2)}) %collective-permute-start.9) | collective-permute-done | bytes 141344 | tf_op jit(solution)/shard_map/ppermute | solution.py:55
  36.8 0.9 %collective-permute-start.16 = (bf16[24,1408]{1,0:T(8,128)(2,1)S(1)}, bf16[24,1408]{1,0:T(8,128)(2,1)S(1)}, u32[]{:S(2)}, u32[]{:S(2)}) collective-permute-start(bf16[24,1408]{1,0:T(8,128)(2,1)S(1)} %shard_map.149.refs_4_.refs_2_), channel_id=1, source_target_pairs={{0,2},{1,3},{2,0},{3,1},{4,6},{5,7},{6,4},{7,5},{8,10},{9,11},{10,... | collective-permute-start | bytes 202760 | tf_op jit(solution)/shard_map/ppermute | solution.py:55
  37.9 0.7 %collective-permute-done.13.refs_2_ = bf16[24,2816]{1,0:T(8,128)(2,1)S(1)} collective-permute-done((bf16[24,2816]{1,0:T(8,128)(2,1)S(1)}, bf16[24,2816]{1,0:T(8,128)(2,1)S(1)}, u32[]{:S(2)}, u32[]{:S(2)}) %collective-permute-start.13) | collective-permute-done | bytes 135200 | tf_op jit(solution)/shard_map/ppermute | solution.py:55
  38.9 0.9 %collective-permute-start.14 = (bf16[24,1408]{1,0:T(8,128)(2,1)S(1)}, bf16[24,1408]{1,0:T(8,128)(2,1)S(1)}, u32[]{:S(2)}, u32[]{:S(2)}) collective-permute-start(bf16[24,1408]{1,0:T(8,128)(2,1)S(1)} %shard_map.151.refs_4_.refs_0_), channel_id=1, source_target_pairs={{0,2},{1,3},{2,0},{3,1},{4,6},{5,7},{6,4},{7,5},{8,10},{9,11},{10,... | collective-permute-start | bytes 202760 | tf_op jit(solution)/shard_map/ppermute | solution.py:55
  39.9 1.2 %shard_map.152.refs_3_ = f32[128,512]{1,0:T(8,128)S(1)} custom-call(bf16[8,512,1408]{2,1,0:T(8,128)(2,1)S(1)} %bitcast.17, bf16[8,128,48]{2,1,0:T(8,128)(2,1)S(1)} %shard_map.150.refs_6_.refs_1_.shared, bf16[24,1408]{1,0:T(8,128)(2,1)S(1)} %shard_map.149.refs_4_.refs_2_, bf16[24,1408]{1,0:T(8,128)(2,1)S(1)} %collective-permute-done.17.refs_3_, ...), custom_call_target="tpu_custom_call" | custom-call | tf_op jit(solution)/shard_map/pallas_call | solution.py:64
  41.0 0.3 collective-permute-done.16.refs_2_
  41.4 1.8 %shard_map.153.refs_2_ = f32[128,512]{1,0:T(8,128)S(1)} custom-call(bf16[8,512,1408]{2,1,0:T(8,128)(2,1)S(1)} %bitcast.17, bf16[8,128,48]{2,1,0:T(8,128)(2,1)S(1)} %shard_map.150.refs_6_.refs_1_.shared, bf16[24,1408]{1,0:T(8,128)(2,1)S(1)} %shard_map.151.refs_4_.refs_0_, bf16[24,1408]{1,0:T(8,128)(2,1)S(1)} %collective-permute-done.15.refs_1_, ...), custom_call_target="tpu_custom_call" | custom-call | tf_op jit(solution)/shard_map/pallas_call | solution.py:64
  43.2 0.3 collective-permute-done.14.refs_1_
  43.5 0.3 collective-permute-start.18
  43.8 1.2 %shard_map.154.refs_1_ = f32[128,512]{1,0:T(8,128)S(1)} custom-call(bf16[8,512,1408]{2,1,0:T(8,128)(2,1)S(1)} %bitcast.17, bf16[8,128,48]{2,1,0:T(8,128)(2,1)S(1)} %shard_map.150.refs_6_.refs_1_.shared, bf16[24,1408]{1,0:T(8,128)(2,1)S(1)} %collective-permute-done.19.refs_0_, bf16[24,1408]{1,0:T(8,128)(2,1)S(1)} %collective-permute-done.14.refs_1_, ...), custom_call_target="tpu_custom_call" | custom-call | tf_op jit(solution)/shard_map/pallas_call | solution.py:64
  45.0 0.7 %shard_map.155 = (f32[4,16,512]{2,1,0:T(8,128)S(1)}, bf16[3,16,512]{2,1,0:T(8,128)(2,1)S(1)}, bf16[16,512]{1,0:T(8,128)(2,1)S(1)}) custom-call(bf16[8,512,1408]{2,1,0:T(8,128)(2,1)S(1)} %bitcast.17, bf16[8,128,48]{2,1,0:T(8,128)(2,1)S(1)} %shard_map.150.refs_6_.refs_1_.shared, bf16[24,1408]{1,0:T(8,128)(2,1)S(1)} %collective-permute-done.18.refs_0_, ...), custom_call_target="tpu_custom_call" | custom-call | tf_op jit(solution)/shard_map/pallas_call | solution.py:64
  45.7 1.6 %collective-permute-start.21 = (bf16[3,16,512]{2,1,0:T(8,128)(2,1)S(1)}, bf16[3,16,512]{2,1,0:T(8,128)(2,1)S(1)}, u32[]{:S(2)}, u32[]{:S(2)}) collective-permute-start(bf16[3,16,512]{2,1,0:T(8,128)(2,1)S(1)} %get-tuple-element.77), channel_id=1, source_target_pairs={{0,4},{4,0},{8,12},{12,8},{16,20},{20,16},{24,28},{28,24},{1,5},{5... | collective-permute-start | bytes 147464 | tf_op jit(solution)/shard_map/ppermute | solution.py:55
  47.3 0.5 collective-permute-start.20
  47.8 2.2 %collective-permute-done.21.far = bf16[3,16,512]{2,1,0:T(8,128)(2,1)S(1)} collective-permute-done((bf16[3,16,512]{2,1,0:T(8,128)(2,1)S(1)}, bf16[3,16,512]{2,1,0:T(8,128)(2,1)S(1)}, u32[]{:S(2)}, u32[]{:S(2)}) %collective-permute-start.21) | collective-permute-done | bytes 49184 | tf_op jit(solution)/shard_map/ppermute | solution.py:55
  50.1 1.9 %collective-permute-start.22 = (bf16[16,512]{1,0:T(8,128)(2,1)S(1)}, bf16[16,512]{1,0:T(8,128)(2,1)S(1)}, u32[]{:S(2)}, u32[]{:S(2)}) collective-permute-start(bf16[16,512]{1,0:T(8,128)(2,1)S(1)} %get-tuple-element.78), channel_id=1, source_target_pairs={{0,24},{4,28},{8,16},{12,20},{16,8},{20,12},{24,0},{28,4},{1,25},{... | collective-permute-start | bytes 49160 | tf_op jit(solution)/shard_map/ppermute | solution.py:55
  52.0 0.2 collective-permute-start.23
  52.2 2.3 %collective-permute-start.24 = (bf16[16,512]{1,0:T(8,128)(2,1)S(1)}, bf16[16,512]{1,0:T(8,128)(2,1)S(1)}, u32[]{:S(2)}, u32[]{:S(2)}) collective-permute-start(bf16[16,512]{1,0:T(8,128)(2,1)S(1)} %get-tuple-element.80), channel_id=1, source_target_pairs={{0,8},{4,12},{8,0},{12,4},{16,24},{20,28},{24,16},{28,20},{1,9},{5... | collective-permute-start | bytes 49160 | tf_op jit(solution)/shard_map/ppermute | solution.py:55
  54.5 1.2 %collective-permute-done.22.rest_0_ = bf16[16,512]{1,0:T(8,128)(2,1)S(1)} collective-permute-done((bf16[16,512]{1,0:T(8,128)(2,1)S(1)}, bf16[16,512]{1,0:T(8,128)(2,1)S(1)}, u32[]{:S(2)}, u32[]{:S(2)}) %collective-permute-start.22) | collective-permute-done | bytes 16416 | tf_op jit(solution)/shard_map/ppermute | solution.py:55
  55.7 0.9 %collective-permute-done.23.rest_1_ = bf16[16,512]{1,0:T(8,128)(2,1)S(1)} collective-permute-done((bf16[16,512]{1,0:T(8,128)(2,1)S(1)}, bf16[16,512]{1,0:T(8,128)(2,1)S(1)}, u32[]{:S(2)}, u32[]{:S(2)}) %collective-permute-start.23) | collective-permute-done | bytes 16416 | tf_op jit(solution)/shard_map/ppermute | solution.py:55
  56.7 0.6 %reshape.7 = bf16[1,4,4,512]{3,2,1,0:T(4,128)(2,1)} reshape(bf16[16,512]{1,0:T(8,128)(2,1)S(1)} %shard_map.157) | data formatting | bytes 32768 | tf_op jit(solution)/shard_map/reshape | solution.py:687
  (67 shorter events, 1.3 us)
Async XLA Ops:
  0.0 0.7 %copy-start.1 = (s32[1,4,4,6]{3,2,1,0:T(4,128)S(1)}, s32[1,4,4,6]{3,2,1,0:T(4,128)}, u32[]{:S(2)}) copy-start(s32[1,4,4,6]{3,2,1,0:T(4,128)} %param.16) | copy-start | bytes 1156
  0.0 0.7 %copy-start.2 = (s32[1,4,4]{2,1,0:T(4,128)S(1)}, s32[1,4,4]{2,1,0:T(4,128)}, u32[]{:S(2)}) copy-start(s32[1,4,4]{2,1,0:T(4,128)} %param.15) | copy-start | bytes 196
  0.0 0.9 %copy-start = (bf16[1,4,4,2048]{3,2,1,0:T(4,128)(2,1)S(1)}, bf16[1,4,4,2048]{3,2,1,0:T(4,128)(2,1)}, u32[]{:S(2)}) copy-start(bf16[1,4,4,2048]{3,2,1,0:T(4,128)(2,1)} %param.14) | copy-start | bytes 196612
  0.0 4.0 %copy-start.8 = (bf16[1,4,60,512]{3,1,2,0:T(4,128)(2,1)S(1)}, bf16[1,4,60,512]{3,1,2,0:T(4,128)(2,1)}, u32[]{:S(2)}) copy-start(bf16[1,4,60,512]{3,1,2,0:T(4,128)(2,1)} %param.23) | copy-start | bytes 737284
  0.0 4.0 %copy-start.7 = (bf16[1,4,60,512]{3,1,2,0:T(4,128)(2,1)S(1)}, bf16[1,4,60,512]{3,1,2,0:T(4,128)(2,1)}, u32[]{:S(2)}) copy-start(bf16[1,4,60,512]{3,1,2,0:T(4,128)(2,1)} %param.22) | copy-start | bytes 737284
  0.0 4.0 %copy-start.3 = (bf16[2048,3,512]{2,0,1:T(8,128)(2,1)S(1)}, bf16[2048,3,512]{2,0,1:T(8,128)(2,1)}, u32[]{:S(2)}) copy-start(bf16[2048,3,512]{2,0,1:T(8,128)(2,1)} %param.17) | copy-start | bytes 18874372
  0.0 6.3 %copy-start.6 = (bf16[1,1024,512]{2,1,0:T(8,128)(2,1)S(1)}, bf16[1,1024,512]{2,1,0:T(8,128)(2,1)}, u32[]{:S(2)}) copy-start(bf16[1,1024,512]{2,1,0:T(8,128)(2,1)} %param.20) | copy-start | bytes 3145732
  0.0 6.3 %copy-start.5 = (bf16[1,1024,512]{2,1,0:T(8,128)(2,1)S(1)}, bf16[1,1024,512]{2,1,0:T(8,128)(2,1)}, u32[]{:S(2)}) copy-start(bf16[1,1024,512]{2,1,0:T(8,128)(2,1)} %param.19) | copy-start | bytes 3145732
  1.0 5.2 %collective-permute-start = (bf16[16,2176]{1,0:T(8,128)(2,1)S(1)}, bf16[16,2176]{1,0:T(8,128)(2,1)S(1)}, u32[]{:S(2)}, u32[]{:S(2)}) collective-permute-start(bf16[16,2176]{1,0:T(8,128)(2,1)S(1)} %shard_map.137.sent), channel_id=1, source_target_pairs={{0,4},{4,0},{8,12},{12,8},{16,20},{20,16},{24,28},{28,24},{1,5},{5... | collective-permute-start | bytes 208904 | tf_op jit(solution)/shard_map/ppermute | solution.py:55
  6.3 5.5 %copy-start.4 = (bf16[512,2048]{1,0:T(8,128)(2,1)S(1)}, bf16[512,2048]{1,0:T(8,128)(2,1)}, u32[]{:S(2)}) copy-start(bf16[512,2048]{1,0:T(8,128)(2,1)} %w_out.1) | copy-start | bytes 6291460
  7.7 10.2 %copy-start.9 = (bf16[512,64]{0,1:T(8,128)(2,1)S(1)}, bf16[512,64]{0,1:T(8,128)(2,1)}, u32[]{:S(2)}) copy-start(bf16[512,64]{0,1:T(8,128)(2,1)} %param.24) | copy-start | bytes 196612
  7.8 10.2 %copy-start.10 = (f32[512]{0:T(512)S(1)}, f32[512]{0:T(512)}, u32[]{:S(2)}) copy-start(f32[512]{0:T(512)} %param.25) | copy-start | bytes 6148
  7.8 4.1 %collective-permute-start.1 = (bf16[32,640]{1,0:T(8,128)(2,1)S(1)}, bf16[32,640]{1,0:T(8,128)(2,1)S(1)}, u32[]{:S(2)}, u32[]{:S(2)}) collective-permute-start(bf16[32,640]{1,0:T(8,128)(2,1)S(1)} %get-tuple-element.54.near), channel_id=1, source_target_pairs={{0,4},{4,0},{8,12},{12,8},{16,20},{20,16},{24,28},{28,24},{1,5},{5... | collective-permute-start | bytes 122888 | tf_op jit(solution)/shard_map/ppermute | solution.py:55
  12.5 2.2 %collective-permute-start.2 = (bf16[32,512]{1,0:T(8,128)(2,1)S(1)}, bf16[32,512]{1,0:T(8,128)(2,1)S(1)}, u32[]{:S(2)}, u32[]{:S(2)}) collective-permute-start(bf16[32,512]{1,0:T(8,128)(2,1)S(1)} %get-tuple-element.56), channel_id=1, source_target_pairs={{0,1},{1,0},{2,3},{3,2},{4,5},{5,4},{6,7},{7,6},{8,9},{9,8},{10,11... | collective-permute-start | bytes 98312 | tf_op jit(solution)/shard_map/ppermute | solution.py:55
  12.5 4.1 %collective-permute-start.3 = (bf16[32,512]{1,0:T(8,128)(2,1)S(1)}, bf16[32,512]{1,0:T(8,128)(2,1)S(1)}, u32[]{:S(2)}, u32[]{:S(2)}) collective-permute-start(bf16[32,512]{1,0:T(8,128)(2,1)S(1)} %get-tuple-element.57), channel_id=1, source_target_pairs={{0,2},{1,3},{2,0},{3,1},{4,6},{5,7},{6,4},{7,5},{8,10},{9,11},{10,... | collective-permute-start | bytes 98312 | tf_op jit(solution)/shard_map/ppermute | solution.py:55
  14.6 3.3 %collective-permute-start.4 = (bf16[32,512]{1,0:T(8,128)(2,1)S(1)}, bf16[32,512]{1,0:T(8,128)(2,1)S(1)}, u32[]{:S(2)}, u32[]{:S(2)}) collective-permute-start(bf16[32,512]{1,0:T(8,128)(2,1)S(1)} %get-tuple-element.58), channel_id=1, source_target_pairs={{0,3},{1,2},{2,1},{3,0},{4,7},{5,6},{6,5},{7,4},{8,11},{9,10},{10,... | collective-permute-start | bytes 98312 | tf_op jit(solution)/shard_map/ppermute | solution.py:55
  18.0 9.4 %slice-start = ((s8[23068672]{0:T(1024)(128)(4,1)}), s8[4194304]{0:T(1024)(128)(4,1)S(1)}, s32[]{:S(2)}) async-start(s8[23068672]{0:T(1024)(128)(4,1)} %bitcast.14), calls=%async_computation | async-start | bytes 8388608
  18.0 9.4 %slice-start.1 = ((s8[23068672]{0:T(1024)(128)(4,1)}), s8[4194304]{0:T(1024)(128)(4,1)S(1)}, s32[]{:S(2)}) async-start(s8[23068672]{0:T(1024)(128)(4,1)} %bitcast.14), calls=%async_computation.1 | async-start | bytes 8388608
  18.0 9.4 %slice-start.2 = ((s8[23068672]{0:T(1024)(128)(4,1)}), s8[4194304]{0:T(1024)(128)(4,1)S(1)}, s32[]{:S(2)}) async-start(s8[23068672]{0:T(1024)(128)(4,1)} %bitcast.14), calls=%async_computation.2 | async-start | bytes 8388608
  18.4 9.0 %slice-start.3 = ((s8[23068672]{0:T(1024)(128)(4,1)}), s8[4194304]{0:T(1024)(128)(4,1)S(1)}, s32[]{:S(2)}) async-start(s8[23068672]{0:T(1024)(128)(4,1)} %bitcast.14), calls=%async_computation.3 | async-start | bytes 8388608
  18.4 9.0 %slice-start.4 = ((s8[23068672]{0:T(1024)(128)(4,1)}), s8[4194304]{0:T(1024)(128)(4,1)S(1)}, s32[]{:S(2)}) async-start(s8[23068672]{0:T(1024)(128)(4,1)} %bitcast.14), calls=%async_computation.4 | async-start | bytes 8388608
  18.4 9.0 %slice-start.5 = ((s8[23068672]{0:T(1024)(128)(4,1)}), s8[2097152]{0:T(1024)(128)(4,1)S(1)}, s32[]{:S(2)}) async-start(s8[23068672]{0:T(1024)(128)(4,1)} %bitcast.14), calls=%async_computation.5 | async-start | bytes 4194304
  18.4 5.9 %collective-permute-start.7 = (bf16[32,640]{1,0:T(8,128)(2,1)S(1)}, bf16[32,640]{1,0:T(8,128)(2,1)S(1)}, u32[]{:S(2)}, u32[]{:S(2)}) collective-permute-start(bf16[32,640]{1,0:T(8,128)(2,1)S(1)} %get-tuple-element.60.refs_0_), channel_id=1, source_target_pairs={{0,24},{4,28},{8,16},{12,20},{16,8},{20,12},{24,0},{28,4},{1,25},{... | collective-permute-start | bytes 122888 | tf_op jit(solution)/shard_map/ppermute | solution.py:55
  22.0 4.9 %collective-permute-start.6 = (bf16[32,640]{1,0:T(8,128)(2,1)S(1)}, bf16[32,640]{1,0:T(8,128)(2,1)S(1)}, u32[]{:S(2)}, u32[]{:S(2)}) collective-permute-start(bf16[32,640]{1,0:T(8,128)(2,1)S(1)} %get-tuple-element.60.refs_0_), channel_id=1, source_target_pairs={{0,16},{4,20},{8,24},{12,28},{16,0},{20,4},{24,8},{28,12},{1,17},{... | collective-permute-start | bytes 122888 | tf_op jit(solution)/shard_map/ppermute | solution.py:55
  22.0 4.9 %collective-permute-start.5 = (bf16[32,640]{1,0:T(8,128)(2,1)S(1)}, bf16[32,640]{1,0:T(8,128)(2,1)S(1)}, u32[]{:S(2)}, u32[]{:S(2)}) collective-permute-start(bf16[32,640]{1,0:T(8,128)(2,1)S(1)} %get-tuple-element.60.refs_0_), channel_id=1, source_target_pairs={{0,8},{4,12},{8,0},{12,4},{16,24},{20,28},{24,16},{28,20},{1,9},{5... | collective-permute-start | bytes 122888 | tf_op jit(solution)/shard_map/ppermute | solution.py:55
  28.0 1.4 %collective-permute-start.8 = (bf16[24,2944]{1,0:T(8,128)(2,1)S(1)}, bf16[24,2944]{1,0:T(8,128)(2,1)S(1)}, u32[]{:S(2)}, u32[]{:S(2)}) collective-permute-start(bf16[24,2944]{1,0:T(8,128)(2,1)S(1)} %shard_map.143.refs_2_), channel_id=1, source_target_pairs={{0,1},{1,0},{2,3},{3,2},{4,5},{5,4},{6,7},{7,6},{8,9},{9,8},{10,11... | collective-permute-start | bytes 423944 | tf_op jit(solution)/shard_map/ppermute | solution.py:55
  28.6 2.3 %collective-permute-start.10 = (bf16[24,2816]{1,0:T(8,128)(2,1)S(1)}, bf16[24,2816]{1,0:T(8,128)(2,1)S(1)}, u32[]{:S(2)}, u32[]{:S(2)}) collective-permute-start(bf16[24,2816]{1,0:T(8,128)(2,1)S(1)} %shard_map.144.refs_4_), channel_id=1, source_target_pairs={{0,1},{1,0},{2,3},{3,2},{4,5},{5,4},{6,7},{7,6},{8,9},{9,8},{10,11... | collective-permute-start | bytes 405512 | tf_op jit(solution)/shard_map/ppermute | solution.py:55
  30.0 6.6 %collective-permute-start.9 = (bf16[24,2944]{1,0:T(8,128)(2,1)S(1)}, bf16[24,2944]{1,0:T(8,128)(2,1)S(1)}, u32[]{:S(2)}, u32[]{:S(2)}) collective-permute-start(bf16[24,2944]{1,0:T(8,128)(2,1)S(1)} %get-tuple-element.66.refs_3_), channel_id=1, source_target_pairs={{0,2},{1,3},{2,0},{3,1},{4,6},{5,7},{6,4},{7,5},{8,10},{9,11},{10,... | collective-permute-start | bytes 423944 | tf_op jit(solution)/shard_map/ppermute | solution.py:55
  31.5 7.2 %collective-permute-start.13 = (bf16[24,2816]{1,0:T(8,128)(2,1)S(1)}, bf16[24,2816]{1,0:T(8,128)(2,1)S(1)}, u32[]{:S(2)}, u32[]{:S(2)}) collective-permute-start(bf16[24,2816]{1,0:T(8,128)(2,1)S(1)} %shard_map.146.refs_2_), channel_id=1, source_target_pairs={{0,2},{1,3},{2,0},{3,1},{4,6},{5,7},{6,4},{7,5},{8,10},{9,11},{10,... | collective-permute-start | bytes 405512 | tf_op jit(solution)/shard_map/ppermute | solution.py:55
  33.8 1.6 %collective-permute-start.11 = (bf16[24,2816]{1,0:T(8,128)(2,1)S(1)}, bf16[24,2816]{1,0:T(8,128)(2,1)S(1)}, u32[]{:S(2)}, u32[]{:S(2)}) collective-permute-start(bf16[24,2816]{1,0:T(8,128)(2,1)S(1)} %get-tuple-element.68), channel_id=1, source_target_pairs={{0,1},{1,0},{2,3},{3,2},{4,5},{5,4},{6,7},{7,6},{8,9},{9,8},{10,11... | collective-permute-start | bytes 405512 | tf_op jit(solution)/shard_map/ppermute | solution.py:55
  33.8 6.1 %slice-start.6 = ((s8[11534336]{0:T(1024)(128)(4,1)}), s8[4194304]{0:T(1024)(128)(4,1)S(1)}, s32[]{:S(2)}) async-start(s8[11534336]{0:T(1024)(128)(4,1)} %bitcast.16), calls=%async_computation.6 | async-start | bytes 8388608
  33.8 6.1 %slice-start.7 = ((s8[11534336]{0:T(1024)(128)(4,1)}), s8[4194304]{0:T(1024)(128)(4,1)S(1)}, s32[]{:S(2)}) async-start(s8[11534336]{0:T(1024)(128)(4,1)} %bitcast.16), calls=%async_computation.7 | async-start | bytes 8388608
  33.8 6.1 %slice-start.8 = ((s8[11534336]{0:T(1024)(128)(4,1)}), s8[3145728]{0:T(1024)(128)(4,1)S(1)}, s32[]{:S(2)}) async-start(s8[11534336]{0:T(1024)(128)(4,1)} %bitcast.16), calls=%async_computation.8 | async-start | bytes 6291456
  34.9 3.8 %collective-permute-start.12 = (bf16[24,2816]{1,0:T(8,128)(2,1)S(1)}, bf16[24,2816]{1,0:T(8,128)(2,1)S(1)}, u32[]{:S(2)}, u32[]{:S(2)}) collective-permute-start(bf16[24,2816]{1,0:T(8,128)(2,1)S(1)} %get-tuple-element.70), channel_id=1, source_target_pairs={{0,1},{1,0},{2,3},{3,2},{4,5},{5,4},{6,7},{7,6},{8,9},{9,8},{10,11... | collective-permute-start | bytes 405512 | tf_op jit(solution)/shard_map/ppermute | solution.py:55
  36.7 3.1 %collective-permute-start.17 = (bf16[24,1408]{1,0:T(8,128)(2,1)S(1)}, bf16[24,1408]{1,0:T(8,128)(2,1)S(1)}, u32[]{:S(2)}, u32[]{:S(2)}) collective-permute-start(bf16[24,1408]{1,0:T(8,128)(2,1)S(1)} %shard_map.149.refs_4_.refs_2_), channel_id=1, source_target_pairs={{0,1},{1,0},{2,3},{3,2},{4,5},{5,4},{6,7},{7,6},{8,9},{9,8},{10,11... | collective-permute-start | bytes 202760 | tf_op jit(solution)/shard_map/ppermute | solution.py:55
  36.8 4.6 %collective-permute-start.16 = (bf16[24,1408]{1,0:T(8,128)(2,1)S(1)}, bf16[24,1408]{1,0:T(8,128)(2,1)S(1)}, u32[]{:S(2)}, u32[]{:S(2)}) collective-permute-start(bf16[24,1408]{1,0:T(8,128)(2,1)S(1)} %shard_map.149.refs_4_.refs_2_), channel_id=1, source_target_pairs={{0,2},{1,3},{2,0},{3,1},{4,6},{5,7},{6,4},{7,5},{8,10},{9,11},{10,... | collective-permute-start | bytes 202760 | tf_op jit(solution)/shard_map/ppermute | solution.py:55
  38.8 2.5 %collective-permute-start.15 = (bf16[24,1408]{1,0:T(8,128)(2,1)S(1)}, bf16[24,1408]{1,0:T(8,128)(2,1)S(1)}, u32[]{:S(2)}, u32[]{:S(2)}) collective-permute-start(bf16[24,1408]{1,0:T(8,128)(2,1)S(1)} %shard_map.151.refs_4_.refs_0_), channel_id=1, source_target_pairs={{0,1},{1,0},{2,3},{3,2},{4,5},{5,4},{6,7},{7,6},{8,9},{9,8},{10,11... | collective-permute-start | bytes 202760 | tf_op jit(solution)/shard_map/ppermute | solution.py:55
  38.9 4.6 %collective-permute-start.14 = (bf16[24,1408]{1,0:T(8,128)(2,1)S(1)}, bf16[24,1408]{1,0:T(8,128)(2,1)S(1)}, u32[]{:S(2)}, u32[]{:S(2)}) collective-permute-start(bf16[24,1408]{1,0:T(8,128)(2,1)S(1)} %shard_map.151.refs_4_.refs_0_), channel_id=1, source_target_pairs={{0,2},{1,3},{2,0},{3,1},{4,6},{5,7},{6,4},{7,5},{8,10},{9,11},{10,... | collective-permute-start | bytes 202760 | tf_op jit(solution)/shard_map/ppermute | solution.py:55
  41.4 2.4 %collective-permute-start.19 = (bf16[24,1408]{1,0:T(8,128)(2,1)S(1)}, bf16[24,1408]{1,0:T(8,128)(2,1)S(1)}, u32[]{:S(2)}, u32[]{:S(2)}) collective-permute-start(bf16[24,1408]{1,0:T(8,128)(2,1)S(1)} %collective-permute-done.16.refs_2_), channel_id=1, source_target_pairs={{0,1},{1,0},{2,3},{3,2},{4,5},{5,4},{6,7},{7,6},{8,9},{9,8},{10,11... | collective-permute-start | bytes 202760 | tf_op jit(solution)/shard_map/ppermute | solution.py:55
  43.5 1.6 %collective-permute-start.18 = (bf16[24,1408]{1,0:T(8,128)(2,1)S(1)}, bf16[24,1408]{1,0:T(8,128)(2,1)S(1)}, u32[]{:S(2)}, u32[]{:S(2)}) collective-permute-start(bf16[24,1408]{1,0:T(8,128)(2,1)S(1)} %collective-permute-done.14.refs_1_), channel_id=1, source_target_pairs={{0,1},{1,0},{2,3},{3,2},{4,5},{5,4},{6,7},{7,6},{8,9},{9,8},{10,11... | collective-permute-start | bytes 202760 | tf_op jit(solution)/shard_map/ppermute | solution.py:55
  45.7 4.3 %collective-permute-start.21 = (bf16[3,16,512]{2,1,0:T(8,128)(2,1)S(1)}, bf16[3,16,512]{2,1,0:T(8,128)(2,1)S(1)}, u32[]{:S(2)}, u32[]{:S(2)}) collective-permute-start(bf16[3,16,512]{2,1,0:T(8,128)(2,1)S(1)} %get-tuple-element.77), channel_id=1, source_target_pairs={{0,4},{4,0},{8,12},{12,8},{16,20},{20,16},{24,28},{28,24},{1,5},{5... | collective-permute-start | bytes 147464 | tf_op jit(solution)/shard_map/ppermute | solution.py:55
  47.3 7.2 %collective-permute-start.20 = (bf16[16,512]{1,0:T(8,128)(2,1)S(1)}, bf16[16,512]{1,0:T(8,128)(2,1)S(1)}, u32[]{:S(2)}, u32[]{:S(2)}) collective-permute-start(bf16[16,512]{1,0:T(8,128)(2,1)S(1)} %get-tuple-element.76), channel_id=1, source_target_pairs={{0,4},{4,0},{8,12},{12,8},{16,20},{20,16},{24,28},{28,24},{1,5},{5... | collective-permute-start | bytes 49160 | tf_op jit(solution)/shard_map/ppermute | solution.py:55
  50.1 5.7 %collective-permute-start.22 = (bf16[16,512]{1,0:T(8,128)(2,1)S(1)}, bf16[16,512]{1,0:T(8,128)(2,1)S(1)}, u32[]{:S(2)}, u32[]{:S(2)}) collective-permute-start(bf16[16,512]{1,0:T(8,128)(2,1)S(1)} %get-tuple-element.78), channel_id=1, source_target_pairs={{0,24},{4,28},{8,16},{12,20},{16,8},{20,12},{24,0},{28,4},{1,25},{... | collective-permute-start | bytes 49160 | tf_op jit(solution)/shard_map/ppermute | solution.py:55
  52.0 4.6 %collective-permute-start.23 = (bf16[16,512]{1,0:T(8,128)(2,1)S(1)}, bf16[16,512]{1,0:T(8,128)(2,1)S(1)}, u32[]{:S(2)}, u32[]{:S(2)}) collective-permute-start(bf16[16,512]{1,0:T(8,128)(2,1)S(1)} %get-tuple-element.79), channel_id=1, source_target_pairs={{0,16},{4,20},{8,24},{12,28},{16,0},{20,4},{24,8},{28,12},{1,17},{... | collective-permute-start | bytes 49160 | tf_op jit(solution)/shard_map/ppermute | solution.py:55
  52.2 4.4 %collective-permute-start.24 = (bf16[16,512]{1,0:T(8,128)(2,1)S(1)}, bf16[16,512]{1,0:T(8,128)(2,1)S(1)}, u32[]{:S(2)}, u32[]{:S(2)}) collective-permute-start(bf16[16,512]{1,0:T(8,128)(2,1)S(1)} %get-tuple-element.80), channel_id=1, source_target_pairs={{0,8},{4,12},{8,0},{12,4},{16,24},{20,28},{24,16},{28,20},{1,9},{5... | collective-permute-start | bytes 49160 | tf_op jit(solution)/shard_map/ppermute | solution.py:55

commit v6 on v5

--- a/solution.py
+++ b/solution.py
@@ -229,8 +229,7 @@
     out[:, width:] = info.astype(BF)
 
 
-def project_kernel(near, far, w_out, *outs):
-    me = lax.axis_index("exp")
+def project_kernel(masks, near, far, w_out, joined, *outs):
     width = w_out.shape[0]
     heads = width // HDIM
     parts = []
@@ -250,10 +249,20 @@
         mix = near[:, at].astype(F32) * f_near + far[:, at].astype(F32) * f_far
         parts.append((mix / total).astype(BF))
     attention = jnp.concatenate(parts, axis=1)
+    joined[...] = attention
+    project_blocks(masks, attention, w_out, outs)
+
+
+def project_blocks(masks, attention, w_out, outs):
+    me = lax.axis_index("exp")
     features = outs[0].shape[1]
-    for k, out in enumerate(outs):
-        start = pl.multiple_of((me ^ k) * features, LANES)
+    for mask, out in zip(masks, outs):
+        start = pl.multiple_of((me ^ mask) * features, LANES)
         out[...] = dot(attention, w_out[:, pl.ds(start, features)]).astype(out.dtype)
+
+
+def near_kernel(masks, joined, w_out, *outs):
+    project_blocks(masks, joined[...], w_out, outs)
 
 
 def residual_kernel(x, named, gain, w_router, own, *rest):
@@ -550,15 +559,25 @@
         flops=HINT,
     )
     far = exchanged(near, "grp", 1)
-    terms = call(
-        project_kernel,
-        tuple(shape((PAIR, features), F32 if k == 0 else BF) for k in range(splits)),
+    remote = tuple(range(2, splits))
+    close = (1, 0)
+    joined, *terms = call(
+        functools.partial(project_kernel, remote),
+        (shape((PAIR, width), BF),) + tuple(shape((PAIR, features), BF) for _ in remote),
         [VMEM] * 3,
         near,
         far,
         w_out,
         flops=HINT,
     )
+    beside, own_term = call(
+        functools.partial(near_kernel, close),
+        (shape((PAIR, features), BF), shape((PAIR, features), F32)),
+        [VMEM] * 2,
+        joined,
+        w_out,
+    )
+    terms = [own_term, beside] + terms
     arrived = [exchanged(terms[k], "exp", k) for k in range(1, splits)]
     residual, message = call(
         residual_kernel,

time: 57.5 us -> 57.3 us (level)
    pallas_call x22 -> x23, Pallas kernels: 13.9 us -> 14 us  [call(): pl.pallas_call(ordered if after else body, out_shape=outs, in_specs=list(...]
where the time goes in v6:
time: 57.3 us; the launch traced here: 57.1 us
  starting transfers between devices  23.7 us (41%)
  waiting for transfers between devices  16.9 us (29%)
  Pallas kernels  14 us (24%)
  local copies, waits for them, and re-layouts  1.48 us (3%)
  between operations  0.99 us (2%)
    ppermute x25, starting transfers between devices, exchanged(): return lax.ppermute(value, axis, pairs)  23.7 us
    ppermute x25, waiting for transfers between devices, exchanged(): return lax.ppermute(value, axis, pairs)  16.9 us
    pallas_call x23, Pallas kernels, call(): pl.pallas_call(ordered if after else body, out_shape=outs, in_specs=list(...  14 us
  transfers between devices with their start and end apart: 25, of which 14 were waited for; matrix products, arithmetic and copies ran while one was open for 0% of the time, Pallas kernels for 17%

profile of v6, /device:TPU:0, one launch (start us, length us, event | category | flops | bytes accessed | tf_op | source)
XLA Modules:
  0.0 57.1 jit_solution(1340233349663413276)
XLA Ops:
  0.1 0.6 %copy-done.2 = s32[1,4,4,6]{3,2,1,0:T(4,128)S(1)} copy-done((s32[1,4,4,6]{3,2,1,0:T(4,128)S(1)}, s32[1,4,4,6]{3,2,1,0:T(4,128)}, u32[]{:S(2)}) %copy-start.2) | copy-done | bytes 408
  1.0 3.0 %collective-permute-start = (bf16[16,2176]{1,0:T(8,128)(2,1)S(1)}, bf16[16,2176]{1,0:T(8,128)(2,1)S(1)}, u32[]{:S(2)}, u32[]{:S(2)}) collective-permute-start(bf16[16,2176]{1,0:T(8,128)(2,1)S(1)} %shard_map.137.sent), channel_id=1, source_target_pairs={{0,4},{4,0},{8,12},{12,8},{16,20},{20,16},{24,28},{28,24},{1,5},{5... | collective-permute-start | bytes 208904 | tf_op jit(solution)/shard_map/ppermute | solution.py:55
  4.0 0.9 %shard_map.138 = (bf16[16,512]{1,0:T(8,128)(2,1)S(1)}, bf16[16,512]{1,0:T(8,128)(2,1)S(1)}, bf16[16,512]{1,0:T(8,128)(2,1)S(1)}, f32[16,512]{1,0:T(8,128)S(1)}, ...) custom-call(bf16[16,2176]{1,0:T(8,128)(2,1)S(1)} %shard_map.137.sent, bf16[3,2048,512]{2,1,0:T(8,128)(2,1)S(1)} %bitcast.21, ...), custom_call_target="tpu_custom_call" | custom-call | flops 2500000000 | tf_op jit(solution)/shard_map/pallas_call | solution.py:64
  5.6 0.7 %collective-permute-done.came = bf16[16,2176]{1,0:T(8,128)(2,1)S(1)} collective-permute-done((bf16[16,2176]{1,0:T(8,128)(2,1)S(1)}, bf16[16,2176]{1,0:T(8,128)(2,1)S(1)}, u32[]{:S(2)}, u32[]{:S(2)}) %collective-permute-start) | collective-permute-done | bytes 69664 | tf_op jit(solution)/shard_map/ppermute | solution.py:55
  6.3 1.4 %shard_map.139 = (bf16[32,640]{1,0:T(8,128)(2,1)S(1)}, f32[32,512]{1,0:T(8,128)S(1)}, f32[32,128]{1,0:T(8,128)S(1)}) custom-call(s32[1]{0:T(128)S(6)} %copy.15.parts, bf16[32,32]{1,0:T(8,128)(2,1)S(1)} %get-tuple-element.44.refs_3_.order, bf16[240,128]{1,0:T(8,128)(2,1)S(1)} %get-tuple-element.45.tail_at, bf16[16,128]{1,0:T(8,128)(2,1)S(1)} %get-tuple-element.46.new_at, ...), custom_call_target="tpu_custom_call" | custom-call | flops 10000000000 | tf_op jit(solution)/shard_map/pallas_call | solution.py:64
  7.8 2.1 %collective-permute-start.1 = (bf16[32,640]{1,0:T(8,128)(2,1)S(1)}, bf16[32,640]{1,0:T(8,128)(2,1)S(1)}, u32[]{:S(2)}, u32[]{:S(2)}) collective-permute-start(bf16[32,640]{1,0:T(8,128)(2,1)S(1)} %get-tuple-element.55.near), channel_id=1, source_target_pairs={{0,4},{4,0},{8,12},{12,8},{16,20},{20,16},{24,28},{28,24},{1,5},{5... | collective-permute-start | bytes 122888 | tf_op jit(solution)/shard_map/ppermute | solution.py:55
  9.8 2.0 %collective-permute-done.1.far = bf16[32,640]{1,0:T(8,128)(2,1)S(1)} collective-permute-done((bf16[32,640]{1,0:T(8,128)(2,1)S(1)}, bf16[32,640]{1,0:T(8,128)(2,1)S(1)}, u32[]{:S(2)}, u32[]{:S(2)}) %collective-permute-start.1) | collective-permute-done | bytes 40992 | tf_op jit(solution)/shard_map/ppermute | solution.py:55
  11.8 0.5 shard_map.140
  12.3 2.1 %collective-permute-start.3 = (bf16[32,512]{1,0:T(8,128)(2,1)S(1)}, bf16[32,512]{1,0:T(8,128)(2,1)S(1)}, u32[]{:S(2)}, u32[]{:S(2)}) collective-permute-start(bf16[32,512]{1,0:T(8,128)(2,1)S(1)} %get-tuple-element.59), channel_id=1, source_target_pairs={{0,2},{1,3},{2,0},{3,1},{4,6},{5,7},{6,4},{7,5},{8,10},{9,11},{10,... | collective-permute-start | bytes 98312 | tf_op jit(solution)/shard_map/ppermute | solution.py:55
  14.4 0.3 shard_map.141
  14.9 1.4 %collective-permute-done.3.rest_1_ = bf16[32,512]{1,0:T(8,128)(2,1)S(1)} collective-permute-done((bf16[32,512]{1,0:T(8,128)(2,1)S(1)}, bf16[32,512]{1,0:T(8,128)(2,1)S(1)}, u32[]{:S(2)}, u32[]{:S(2)}) %collective-permute-start.3) | collective-permute-done | bytes 32800 | tf_op jit(solution)/shard_map/ppermute | solution.py:55
  16.3 1.4 %collective-permute-done.4.rest_2_ = bf16[32,512]{1,0:T(8,128)(2,1)S(1)} collective-permute-done((bf16[32,512]{1,0:T(8,128)(2,1)S(1)}, bf16[32,512]{1,0:T(8,128)(2,1)S(1)}, u32[]{:S(2)}, u32[]{:S(2)}) %collective-permute-start.4) | collective-permute-done | bytes 32800 | tf_op jit(solution)/shard_map/ppermute | solution.py:55
  17.8 0.4 shard_map.142
  18.1 3.7 %collective-permute-start.7 = (bf16[32,640]{1,0:T(8,128)(2,1)S(1)}, bf16[32,640]{1,0:T(8,128)(2,1)S(1)}, u32[]{:S(2)}, u32[]{:S(2)}) collective-permute-start(bf16[32,640]{1,0:T(8,128)(2,1)S(1)} %get-tuple-element.62.refs_0_), channel_id=1, source_target_pairs={{0,24},{4,28},{8,16},{12,20},{16,8},{20,12},{24,0},{28,4},{1,25},{... | collective-permute-start | bytes 122888 | tf_op jit(solution)/shard_map/ppermute | solution.py:55
  21.8 0.8 %collective-permute-start.5 = (bf16[32,640]{1,0:T(8,128)(2,1)S(1)}, bf16[32,640]{1,0:T(8,128)(2,1)S(1)}, u32[]{:S(2)}, u32[]{:S(2)}) collective-permute-start(bf16[32,640]{1,0:T(8,128)(2,1)S(1)} %get-tuple-element.62.refs_0_), channel_id=1, source_target_pairs={{0,8},{4,12},{8,0},{12,4},{16,24},{20,28},{24,16},{28,20},{1,9},{5... | collective-permute-start | bytes 122888 | tf_op jit(solution)/shard_map/ppermute | solution.py:55
  22.6 1.6 %collective-permute-done.7.refs_3_ = bf16[32,640]{1,0:T(8,128)(2,1)S(1)} collective-permute-done((bf16[32,640]{1,0:T(8,128)(2,1)S(1)}, bf16[32,640]{1,0:T(8,128)(2,1)S(1)}, u32[]{:S(2)}, u32[]{:S(2)}) %collective-permute-start.7) | collective-permute-done | bytes 40992 | tf_op jit(solution)/shard_map/ppermute | solution.py:55
  24.2 2.5 %collective-permute-done.6.refs_2_ = bf16[32,640]{1,0:T(8,128)(2,1)S(1)} collective-permute-done((bf16[32,640]{1,0:T(8,128)(2,1)S(1)}, bf16[32,640]{1,0:T(8,128)(2,1)S(1)}, u32[]{:S(2)}, u32[]{:S(2)}) %collective-permute-start.6) | collective-permute-done | bytes 40992 | tf_op jit(solution)/shard_map/ppermute | solution.py:55
  26.7 0.4 shard_map.143
  27.2 0.6 %shard_map.144.refs_2_ = bf16[24,2944]{1,0:T(8,128)(2,1)S(1)} custom-call(bf16[8,512,2816]{2,1,0:T(8,128)(2,1)S(1)} %bitcast.15, bf16[8,24,512]{2,1,0:T(8,128)(2,1)S(1)} %get-tuple-element.65.picked.refs_1_, f32[8,128]{1,0:T(8,128)S(1)} %get-tuple-element.66.refs_0_.refs_2_), custom_call_target="tpu_custom_call" | custom-call | tf_op jit(solution)/shard_map/pallas_call | solution.py:64
  27.8 0.6 %shard_map.145.refs_4_ = bf16[24,2816]{1,0:T(8,128)(2,1)S(1)} custom-call(bf16[8,512,2816]{2,1,0:T(8,128)(2,1)S(1)} %bitcast.15, bf16[8,24,512]{2,1,0:T(8,128)(2,1)S(1)} %get-tuple-element.65.picked.refs_1_, bf16[24,2944]{1,0:T(8,128)(2,1)S(1)} %shard_map.144.refs_2_), custom_call_target="tpu_custom_call" | custom-call | tf_op jit(solution)/shard_map/pallas_call | solution.py:64
  28.4 0.5 collective-permute-start.10
  28.9 0.2 collective-permute-done.8.refs_3_
  29.2 0.6 %shard_map.146 = (bf16[24,2944]{1,0:T(8,128)(2,1)S(1)}, f32[8,128]{1,0:T(8,128)S(1)}) custom-call(bf16[8,512,2816]{2,1,0:T(8,128)(2,1)S(1)} %bitcast.15, bf16[8,24,512]{2,1,0:T(8,128)(2,1)S(1)} %get-tuple-element.65.picked.refs_1_, f32[8,128]{1,0:T(8,128)S(1)} %get-tuple-element.66.refs_0_.refs_2_, bf16[24,2944]{1,0:T(8,128)(2,1)S(1)} %collective-permute-done.8.refs_3_, ...), custom_call_target="tpu_custom_call" | custom-call | tf_op jit(solution)/shard_map/pallas_call | solution.py:64
  29.8 0.9 %collective-permute-start.9 = (bf16[24,2944]{1,0:T(8,128)(2,1)S(1)}, bf16[24,2944]{1,0:T(8,128)(2,1)S(1)}, u32[]{:S(2)}, u32[]{:S(2)}) collective-permute-start(bf16[24,2944]{1,0:T(8,128)(2,1)S(1)} %get-tuple-element.68.refs_3_), channel_id=1, source_target_pairs={{0,2},{1,3},{2,0},{3,1},{4,6},{5,7},{6,4},{7,5},{8,10},{9,11},{10,... | collective-permute-start | bytes 423944 | tf_op jit(solution)/shard_map/ppermute | solution.py:55
  30.7 0.6 %shard_map.147.refs_2_ = bf16[24,2816]{1,0:T(8,128)(2,1)S(1)} custom-call(bf16[8,512,2816]{2,1,0:T(8,128)(2,1)S(1)} %bitcast.15, bf16[8,24,512]{2,1,0:T(8,128)(2,1)S(1)} %get-tuple-element.65.picked.refs_1_, bf16[24,2816]{1,0:T(8,128)(2,1)S(1)} %collective-permute-done.10.refs_2_, bf16[24,2944]{1,0:T(8,128)(2,1)S(1)} %get-tuple-element.68.refs_3_), custom_call_target="tpu_custom_call" | custom-call | tf_op jit(solution)/shard_map/pallas_call | solution.py:64
  31.2 1.2 %collective-permute-start.13 = (bf16[24,2816]{1,0:T(8,128)(2,1)S(1)}, bf16[24,2816]{1,0:T(8,128)(2,1)S(1)}, u32[]{:S(2)}, u32[]{:S(2)}) collective-permute-start(bf16[24,2816]{1,0:T(8,128)(2,1)S(1)} %shard_map.147.refs_2_), channel_id=1, source_target_pairs={{0,2},{1,3},{2,0},{3,1},{4,6},{5,7},{6,4},{7,5},{8,10},{9,11},{10,... | collective-permute-start | bytes 405512 | tf_op jit(solution)/shard_map/ppermute | solution.py:55
  32.4 1.1 %shard_map.148 = (bf16[24,2816]{1,0:T(8,128)(2,1)S(1)}, f32[24,2816]{1,0:T(8,128)S(1)}) custom-call(bf16[8,512,2816]{2,1,0:T(8,128)(2,1)S(1)} %bitcast.15, bf16[8,24,512]{2,1,0:T(8,128)(2,1)S(1)} %get-tuple-element.65.picked.refs_1_, bf16[24,2816]{1,0:T(8,128)(2,1)S(1)} %shard_map.147.refs_2_), custom_call_target="tpu_custom_call" | custom-call | flops 3000000000 | tf_op jit(solution)/shard_map/pallas_call | solution.py:64
  33.6 1.1 %shard_map.149 = (bf16[24,2816]{1,0:T(8,128)(2,1)S(1)}, f32[24,2816]{1,0:T(8,128)S(1)}) custom-call(bf16[8,512,2816]{2,1,0:T(8,128)(2,1)S(1)} %bitcast.15, bf16[8,24,512]{2,1,0:T(8,128)(2,1)S(1)} %get-tuple-element.65.picked.refs_1_, f32[24,2816]{1,0:T(8,128)S(1)} %get-tuple-element.69.refs_2_.refs_0_), custom_call_target="tpu_custom_call" | custom-call | flops 3000000000 | tf_op jit(solution)/shard_map/pallas_call | solution.py:64
  34.7 0.5 collective-permute-start.12
  35.2 1.2 %collective-permute-done.9.refs_2_.refs_5_.refs_3_ = bf16[24,2944]{1,0:T(8,128)(2,1)S(1)} collective-permute-done((bf16[24,2944]{1,0:T(8,128)(2,1)S(1)}, bf16[24,2944]{1,0:T(8,128)(2,1)S(1)}, u32[]{:S(2)}, u32[]{:S(2)}) %collective-permute-start.9) | collective-permute-done | bytes 141344 | tf_op jit(solution)/shard_map/ppermute | solution.py:55
  36.6 0.9 %collective-permute-start.16 = (bf16[24,1408]{1,0:T(8,128)(2,1)S(1)}, bf16[24,1408]{1,0:T(8,128)(2,1)S(1)}, u32[]{:S(2)}, u32[]{:S(2)}) collective-permute-start(bf16[24,1408]{1,0:T(8,128)(2,1)S(1)} %shard_map.150.refs_4_.refs_2_), channel_id=1, source_target_pairs={{0,2},{1,3},{2,0},{3,1},{4,6},{5,7},{6,4},{7,5},{8,10},{9,11},{10,... | collective-permute-start | bytes 202760 | tf_op jit(solution)/shard_map/ppermute | solution.py:55
  37.7 0.8 %collective-permute-done.13.refs_2_ = bf16[24,2816]{1,0:T(8,128)(2,1)S(1)} collective-permute-done((bf16[24,2816]{1,0:T(8,128)(2,1)S(1)}, bf16[24,2816]{1,0:T(8,128)(2,1)S(1)}, u32[]{:S(2)}, u32[]{:S(2)}) %collective-permute-start.13) | collective-permute-done | bytes 135200 | tf_op jit(solution)/shard_map/ppermute | solution.py:55
  38.7 0.9 %collective-permute-start.14 = (bf16[24,1408]{1,0:T(8,128)(2,1)S(1)}, bf16[24,1408]{1,0:T(8,128)(2,1)S(1)}, u32[]{:S(2)}, u32[]{:S(2)}) collective-permute-start(bf16[24,1408]{1,0:T(8,128)(2,1)S(1)} %shard_map.152.refs_4_.refs_0_), channel_id=1, source_target_pairs={{0,2},{1,3},{2,0},{3,1},{4,6},{5,7},{6,4},{7,5},{8,10},{9,11},{10,... | collective-permute-start | bytes 202760 | tf_op jit(solution)/shard_map/ppermute | solution.py:55
  39.6 1.1 %shard_map.153.refs_3_ = f32[128,512]{1,0:T(8,128)S(1)} custom-call(bf16[8,512,1408]{2,1,0:T(8,128)(2,1)S(1)} %bitcast.17, bf16[8,128,48]{2,1,0:T(8,128)(2,1)S(1)} %shard_map.151.refs_6_.refs_1_.shared, bf16[24,1408]{1,0:T(8,128)(2,1)S(1)} %shard_map.150.refs_4_.refs_2_, bf16[24,1408]{1,0:T(8,128)(2,1)S(1)} %collective-permute-done.17.refs_3_, ...), custom_call_target="tpu_custom_call" | custom-call | tf_op jit(solution)/shard_map/pallas_call | solution.py:64
  40.8 0.3 collective-permute-done.16.refs_2_
  41.1 1.8 %shard_map.154.refs_2_ = f32[128,512]{1,0:T(8,128)S(1)} custom-call(bf16[8,512,1408]{2,1,0:T(8,128)(2,1)S(1)} %bitcast.17, bf16[8,128,48]{2,1,0:T(8,128)(2,1)S(1)} %shard_map.151.refs_6_.refs_1_.shared, bf16[24,1408]{1,0:T(8,128)(2,1)S(1)} %shard_map.152.refs_4_.refs_0_, bf16[24,1408]{1,0:T(8,128)(2,1)S(1)} %collective-permute-done.15.refs_1_, ...), custom_call_target="tpu_custom_call" | custom-call | tf_op jit(solution)/shard_map/pallas_call | solution.py:64
  42.9 0.3 collective-permute-done.14.refs_1_
  43.2 0.3 collective-permute-start.18
  43.5 1.2 %shard_map.155.refs_1_ = f32[128,512]{1,0:T(8,128)S(1)} custom-call(bf16[8,512,1408]{2,1,0:T(8,128)(2,1)S(1)} %bitcast.17, bf16[8,128,48]{2,1,0:T(8,128)(2,1)S(1)} %shard_map.151.refs_6_.refs_1_.shared, bf16[24,1408]{1,0:T(8,128)(2,1)S(1)} %collective-permute-done.19.refs_0_, bf16[24,1408]{1,0:T(8,128)(2,1)S(1)} %collective-permute-done.14.refs_1_, ...), custom_call_target="tpu_custom_call" | custom-call | tf_op jit(solution)/shard_map/pallas_call | solution.py:64
  44.8 0.7 %shard_map.156 = (f32[4,16,512]{2,1,0:T(8,128)S(1)}, bf16[3,16,512]{2,1,0:T(8,128)(2,1)S(1)}, bf16[16,512]{1,0:T(8,128)(2,1)S(1)}) custom-call(bf16[8,512,1408]{2,1,0:T(8,128)(2,1)S(1)} %bitcast.17, bf16[8,128,48]{2,1,0:T(8,128)(2,1)S(1)} %shard_map.151.refs_6_.refs_1_.shared, bf16[24,1408]{1,0:T(8,128)(2,1)S(1)} %collective-permute-done.18.refs_0_, ...), custom_call_target="tpu_custom_call" | custom-call | tf_op jit(solution)/shard_map/pallas_call | solution.py:64
  45.5 1.6 %collective-permute-start.21 = (bf16[3,16,512]{2,1,0:T(8,128)(2,1)S(1)}, bf16[3,16,512]{2,1,0:T(8,128)(2,1)S(1)}, u32[]{:S(2)}, u32[]{:S(2)}) collective-permute-start(bf16[3,16,512]{2,1,0:T(8,128)(2,1)S(1)} %get-tuple-element.79), channel_id=1, source_target_pairs={{0,4},{4,0},{8,12},{12,8},{16,20},{20,16},{24,28},{28,24},{1,5},{5... | collective-permute-start | bytes 147464 | tf_op jit(solution)/shard_map/ppermute | solution.py:55
  47.1 0.5 collective-permute-start.20
  47.6 2.2 %collective-permute-done.21.far = bf16[3,16,512]{2,1,0:T(8,128)(2,1)S(1)} collective-permute-done((bf16[3,16,512]{2,1,0:T(8,128)(2,1)S(1)}, bf16[3,16,512]{2,1,0:T(8,128)(2,1)S(1)}, u32[]{:S(2)}, u32[]{:S(2)}) %collective-permute-start.21) | collective-permute-done | bytes 49184 | tf_op jit(solution)/shard_map/ppermute | solution.py:55
  49.8 2.0 %collective-permute-start.22 = (bf16[16,512]{1,0:T(8,128)(2,1)S(1)}, bf16[16,512]{1,0:T(8,128)(2,1)S(1)}, u32[]{:S(2)}, u32[]{:S(2)}) collective-permute-start(bf16[16,512]{1,0:T(8,128)(2,1)S(1)} %get-tuple-element.80), channel_id=1, source_target_pairs={{0,24},{4,28},{8,16},{12,20},{16,8},{20,12},{24,0},{28,4},{1,25},{... | collective-permute-start | bytes 49160 | tf_op jit(solution)/shard_map/ppermute | solution.py:55
  52.0 2.3 %collective-permute-start.24 = (bf16[16,512]{1,0:T(8,128)(2,1)S(1)}, bf16[16,512]{1,0:T(8,128)(2,1)S(1)}, u32[]{:S(2)}, u32[]{:S(2)}) collective-permute-start(bf16[16,512]{1,0:T(8,128)(2,1)S(1)} %get-tuple-element.82), channel_id=1, source_target_pairs={{0,8},{4,12},{8,0},{12,4},{16,24},{20,28},{24,16},{28,20},{1,9},{5... | collective-permute-start | bytes 49160 | tf_op jit(solution)/shard_map/ppermute | solution.py:55
  54.3 1.2 %collective-permute-done.22.rest_0_ = bf16[16,512]{1,0:T(8,128)(2,1)S(1)} collective-permute-done((bf16[16,512]{1,0:T(8,128)(2,1)S(1)}, bf16[16,512]{1,0:T(8,128)(2,1)S(1)}, u32[]{:S(2)}, u32[]{:S(2)}) %collective-permute-start.22) | collective-permute-done | bytes 16416 | tf_op jit(solution)/shard_map/ppermute | solution.py:55
  55.5 1.0 %collective-permute-done.23.rest_1_ = bf16[16,512]{1,0:T(8,128)(2,1)S(1)} collective-permute-done((bf16[16,512]{1,0:T(8,128)(2,1)S(1)}, bf16[16,512]{1,0:T(8,128)(2,1)S(1)}, u32[]{:S(2)}, u32[]{:S(2)}) %collective-permute-start.23) | collective-permute-done | bytes 16416 | tf_op jit(solution)/shard_map/ppermute | solution.py:55
  56.5 0.6 %reshape.7 = bf16[1,4,4,512]{3,2,1,0:T(4,128)(2,1)} reshape(bf16[16,512]{1,0:T(8,128)(2,1)S(1)} %shard_map.158) | data formatting | bytes 32768 | tf_op jit(solution)/shard_map/reshape | solution.py:706
  (68 shorter events, 1.6 us)
Async XLA Ops:
  0.0 0.7 %copy-start.2 = (s32[1,4,4,6]{3,2,1,0:T(4,128)S(1)}, s32[1,4,4,6]{3,2,1,0:T(4,128)}, u32[]{:S(2)}) copy-start(s32[1,4,4,6]{3,2,1,0:T(4,128)} %param.16) | copy-start | bytes 1156
  0.0 0.7 %copy-start.3 = (s32[1,4,4]{2,1,0:T(4,128)S(1)}, s32[1,4,4]{2,1,0:T(4,128)}, u32[]{:S(2)}) copy-start(s32[1,4,4]{2,1,0:T(4,128)} %param.15) | copy-start | bytes 196
  0.0 0.9 %copy-start.1 = (bf16[1,4,4,2048]{3,2,1,0:T(4,128)(2,1)S(1)}, bf16[1,4,4,2048]{3,2,1,0:T(4,128)(2,1)}, u32[]{:S(2)}) copy-start(bf16[1,4,4,2048]{3,2,1,0:T(4,128)(2,1)} %param.14) | copy-start | bytes 196612
  0.0 4.0 %copy-start.8 = (bf16[1,4,60,512]{3,1,2,0:T(4,128)(2,1)S(1)}, bf16[1,4,60,512]{3,1,2,0:T(4,128)(2,1)}, u32[]{:S(2)}) copy-start(bf16[1,4,60,512]{3,1,2,0:T(4,128)(2,1)} %param.23) | copy-start | bytes 737284
  0.0 4.0 %copy-start.7 = (bf16[1,4,60,512]{3,1,2,0:T(4,128)(2,1)S(1)}, bf16[1,4,60,512]{3,1,2,0:T(4,128)(2,1)}, u32[]{:S(2)}) copy-start(bf16[1,4,60,512]{3,1,2,0:T(4,128)(2,1)} %param.22) | copy-start | bytes 737284
  0.0 4.0 %copy-start.4 = (bf16[2048,3,512]{2,0,1:T(8,128)(2,1)S(1)}, bf16[2048,3,512]{2,0,1:T(8,128)(2,1)}, u32[]{:S(2)}) copy-start(bf16[2048,3,512]{2,0,1:T(8,128)(2,1)} %param.17) | copy-start | bytes 18874372
  0.0 6.3 %copy-start.6 = (bf16[1,1024,512]{2,1,0:T(8,128)(2,1)S(1)}, bf16[1,1024,512]{2,1,0:T(8,128)(2,1)}, u32[]{:S(2)}) copy-start(bf16[1,1024,512]{2,1,0:T(8,128)(2,1)} %param.20) | copy-start | bytes 3145732
  0.0 6.3 %copy-start.5 = (bf16[1,1024,512]{2,1,0:T(8,128)(2,1)S(1)}, bf16[1,1024,512]{2,1,0:T(8,128)(2,1)}, u32[]{:S(2)}) copy-start(bf16[1,1024,512]{2,1,0:T(8,128)(2,1)} %param.19) | copy-start | bytes 3145732
  1.0 5.2 %collective-permute-start = (bf16[16,2176]{1,0:T(8,128)(2,1)S(1)}, bf16[16,2176]{1,0:T(8,128)(2,1)S(1)}, u32[]{:S(2)}, u32[]{:S(2)}) collective-permute-start(bf16[16,2176]{1,0:T(8,128)(2,1)S(1)} %shard_map.137.sent), channel_id=1, source_target_pairs={{0,4},{4,0},{8,12},{12,8},{16,20},{20,16},{24,28},{28,24},{1,5},{5... | collective-permute-start | bytes 208904 | tf_op jit(solution)/shard_map/ppermute | solution.py:55
  6.3 5.5 %copy-start = (bf16[512,2048]{1,0:T(8,128)(2,1)S(1)}, bf16[512,2048]{1,0:T(8,128)(2,1)}, u32[]{:S(2)}) copy-start(bf16[512,2048]{1,0:T(8,128)(2,1)} %w_out.3) | copy-start | bytes 6291460
  7.7 10.0 %copy-start.9 = (bf16[512,64]{0,1:T(8,128)(2,1)S(1)}, bf16[512,64]{0,1:T(8,128)(2,1)}, u32[]{:S(2)}) copy-start(bf16[512,64]{0,1:T(8,128)(2,1)} %param.24) | copy-start | bytes 196612
  7.8 10.0 %copy-start.10 = (f32[512]{0:T(512)S(1)}, f32[512]{0:T(512)}, u32[]{:S(2)}) copy-start(f32[512]{0:T(512)} %param.25) | copy-start | bytes 6148
  7.8 4.1 %collective-permute-start.1 = (bf16[32,640]{1,0:T(8,128)(2,1)S(1)}, bf16[32,640]{1,0:T(8,128)(2,1)S(1)}, u32[]{:S(2)}, u32[]{:S(2)}) collective-permute-start(bf16[32,640]{1,0:T(8,128)(2,1)S(1)} %get-tuple-element.55.near), channel_id=1, source_target_pairs={{0,4},{4,0},{8,12},{12,8},{16,20},{20,16},{24,28},{28,24},{1,5},{5... | collective-permute-start | bytes 122888 | tf_op jit(solution)/shard_map/ppermute | solution.py:55
  12.3 4.0 %collective-permute-start.3 = (bf16[32,512]{1,0:T(8,128)(2,1)S(1)}, bf16[32,512]{1,0:T(8,128)(2,1)S(1)}, u32[]{:S(2)}, u32[]{:S(2)}) collective-permute-start(bf16[32,512]{1,0:T(8,128)(2,1)S(1)} %get-tuple-element.59), channel_id=1, source_target_pairs={{0,2},{1,3},{2,0},{3,1},{4,6},{5,7},{6,4},{7,5},{8,10},{9,11},{10,... | collective-permute-start | bytes 98312 | tf_op jit(solution)/shard_map/ppermute | solution.py:55
  14.4 3.3 %collective-permute-start.4 = (bf16[32,512]{1,0:T(8,128)(2,1)S(1)}, bf16[32,512]{1,0:T(8,128)(2,1)S(1)}, u32[]{:S(2)}, u32[]{:S(2)}) collective-permute-start(bf16[32,512]{1,0:T(8,128)(2,1)S(1)} %get-tuple-element.60), channel_id=1, source_target_pairs={{0,3},{1,2},{2,1},{3,0},{4,7},{5,6},{6,5},{7,4},{8,11},{9,10},{10,... | collective-permute-start | bytes 98312 | tf_op jit(solution)/shard_map/ppermute | solution.py:55
  14.7 3.1 %collective-permute-start.2 = (bf16[32,512]{1,0:T(8,128)(2,1)S(1)}, bf16[32,512]{1,0:T(8,128)(2,1)S(1)}, u32[]{:S(2)}, u32[]{:S(2)}) collective-permute-start(bf16[32,512]{1,0:T(8,128)(2,1)S(1)} %get-tuple-element.58), channel_id=1, source_target_pairs={{0,1},{1,0},{2,3},{3,2},{4,5},{5,4},{6,7},{7,6},{8,9},{9,8},{10,11... | collective-permute-start | bytes 98312 | tf_op jit(solution)/shard_map/ppermute | solution.py:55
  17.7 9.4 %slice-start = ((s8[23068672]{0:T(1024)(128)(4,1)}), s8[4194304]{0:T(1024)(128)(4,1)S(1)}, s32[]{:S(2)}) async-start(s8[23068672]{0:T(1024)(128)(4,1)} %bitcast.14), calls=%async_computation | async-start | bytes 8388608
  17.8 9.4 %slice-start.1 = ((s8[23068672]{0:T(1024)(128)(4,1)}), s8[4194304]{0:T(1024)(128)(4,1)S(1)}, s32[]{:S(2)}) async-start(s8[23068672]{0:T(1024)(128)(4,1)} %bitcast.14), calls=%async_computation.1 | async-start | bytes 8388608
  17.8 9.4 %slice-start.2 = ((s8[23068672]{0:T(1024)(128)(4,1)}), s8[4194304]{0:T(1024)(128)(4,1)S(1)}, s32[]{:S(2)}) async-start(s8[23068672]{0:T(1024)(128)(4,1)} %bitcast.14), calls=%async_computation.2 | async-start | bytes 8388608
  18.1 9.0 %slice-start.3 = ((s8[23068672]{0:T(1024)(128)(4,1)}), s8[4194304]{0:T(1024)(128)(4,1)S(1)}, s32[]{:S(2)}) async-start(s8[23068672]{0:T(1024)(128)(4,1)} %bitcast.14), calls=%async_computation.3 | async-start | bytes 8388608
  18.1 9.0 %slice-start.4 = ((s8[23068672]{0:T(1024)(128)(4,1)}), s8[4194304]{0:T(1024)(128)(4,1)S(1)}, s32[]{:S(2)}) async-start(s8[23068672]{0:T(1024)(128)(4,1)} %bitcast.14), calls=%async_computation.4 | async-start | bytes 8388608
  18.1 9.0 %slice-start.5 = ((s8[23068672]{0:T(1024)(128)(4,1)}), s8[2097152]{0:T(1024)(128)(4,1)S(1)}, s32[]{:S(2)}) async-start(s8[23068672]{0:T(1024)(128)(4,1)} %bitcast.14), calls=%async_computation.5 | async-start | bytes 4194304
  18.1 6.1 %collective-permute-start.7 = (bf16[32,640]{1,0:T(8,128)(2,1)S(1)}, bf16[32,640]{1,0:T(8,128)(2,1)S(1)}, u32[]{:S(2)}, u32[]{:S(2)}) collective-permute-start(bf16[32,640]{1,0:T(8,128)(2,1)S(1)} %get-tuple-element.62.refs_0_), channel_id=1, source_target_pairs={{0,24},{4,28},{8,16},{12,20},{16,8},{20,12},{24,0},{28,4},{1,25},{... | collective-permute-start | bytes 122888 | tf_op jit(solution)/shard_map/ppermute | solution.py:55
  21.8 4.9 %collective-permute-start.6 = (bf16[32,640]{1,0:T(8,128)(2,1)S(1)}, bf16[32,640]{1,0:T(8,128)(2,1)S(1)}, u32[]{:S(2)}, u32[]{:S(2)}) collective-permute-start(bf16[32,640]{1,0:T(8,128)(2,1)S(1)} %get-tuple-element.62.refs_0_), channel_id=1, source_target_pairs={{0,16},{4,20},{8,24},{12,28},{16,0},{20,4},{24,8},{28,12},{1,17},{... | collective-permute-start | bytes 122888 | tf_op jit(solution)/shard_map/ppermute | solution.py:55
  21.8 4.9 %collective-permute-start.5 = (bf16[32,640]{1,0:T(8,128)(2,1)S(1)}, bf16[32,640]{1,0:T(8,128)(2,1)S(1)}, u32[]{:S(2)}, u32[]{:S(2)}) collective-permute-start(bf16[32,640]{1,0:T(8,128)(2,1)S(1)} %get-tuple-element.62.refs_0_), channel_id=1, source_target_pairs={{0,8},{4,12},{8,0},{12,4},{16,24},{20,28},{24,16},{28,20},{1,9},{5... | collective-permute-start | bytes 122888 | tf_op jit(solution)/shard_map/ppermute | solution.py:55
  27.8 1.4 %collective-permute-start.8 = (bf16[24,2944]{1,0:T(8,128)(2,1)S(1)}, bf16[24,2944]{1,0:T(8,128)(2,1)S(1)}, u32[]{:S(2)}, u32[]{:S(2)}) collective-permute-start(bf16[24,2944]{1,0:T(8,128)(2,1)S(1)} %shard_map.144.refs_2_), channel_id=1, source_target_pairs={{0,1},{1,0},{2,3},{3,2},{4,5},{5,4},{6,7},{7,6},{8,9},{9,8},{10,11... | collective-permute-start | bytes 423944 | tf_op jit(solution)/shard_map/ppermute | solution.py:55
  28.4 2.3 %collective-permute-start.10 = (bf16[24,2816]{1,0:T(8,128)(2,1)S(1)}, bf16[24,2816]{1,0:T(8,128)(2,1)S(1)}, u32[]{:S(2)}, u32[]{:S(2)}) collective-permute-start(bf16[24,2816]{1,0:T(8,128)(2,1)S(1)} %shard_map.145.refs_4_), channel_id=1, source_target_pairs={{0,1},{1,0},{2,3},{3,2},{4,5},{5,4},{6,7},{7,6},{8,9},{9,8},{10,11... | collective-permute-start | bytes 405512 | tf_op jit(solution)/shard_map/ppermute | solution.py:55
  29.8 6.6 %collective-permute-start.9 = (bf16[24,2944]{1,0:T(8,128)(2,1)S(1)}, bf16[24,2944]{1,0:T(8,128)(2,1)S(1)}, u32[]{:S(2)}, u32[]{:S(2)}) collective-permute-start(bf16[24,2944]{1,0:T(8,128)(2,1)S(1)} %get-tuple-element.68.refs_3_), channel_id=1, source_target_pairs={{0,2},{1,3},{2,0},{3,1},{4,6},{5,7},{6,4},{7,5},{8,10},{9,11},{10,... | collective-permute-start | bytes 423944 | tf_op jit(solution)/shard_map/ppermute | solution.py:55
  31.2 7.2 %collective-permute-start.13 = (bf16[24,2816]{1,0:T(8,128)(2,1)S(1)}, bf16[24,2816]{1,0:T(8,128)(2,1)S(1)}, u32[]{:S(2)}, u32[]{:S(2)}) collective-permute-start(bf16[24,2816]{1,0:T(8,128)(2,1)S(1)} %shard_map.147.refs_2_), channel_id=1, source_target_pairs={{0,2},{1,3},{2,0},{3,1},{4,6},{5,7},{6,4},{7,5},{8,10},{9,11},{10,... | collective-permute-start | bytes 405512 | tf_op jit(solution)/shard_map/ppermute | solution.py:55
  33.5 1.6 %collective-permute-start.11 = (bf16[24,2816]{1,0:T(8,128)(2,1)S(1)}, bf16[24,2816]{1,0:T(8,128)(2,1)S(1)}, u32[]{:S(2)}, u32[]{:S(2)}) collective-permute-start(bf16[24,2816]{1,0:T(8,128)(2,1)S(1)} %get-tuple-element.70), channel_id=1, source_target_pairs={{0,1},{1,0},{2,3},{3,2},{4,5},{5,4},{6,7},{7,6},{8,9},{9,8},{10,11... | collective-permute-start | bytes 405512 | tf_op jit(solution)/shard_map/ppermute | solution.py:55
  33.5 6.1 %slice-start.6 = ((s8[11534336]{0:T(1024)(128)(4,1)}), s8[4194304]{0:T(1024)(128)(4,1)S(1)}, s32[]{:S(2)}) async-start(s8[11534336]{0:T(1024)(128)(4,1)} %bitcast.16), calls=%async_computation.6 | async-start | bytes 8388608
  33.5 6.1 %slice-start.7 = ((s8[11534336]{0:T(1024)(128)(4,1)}), s8[4194304]{0:T(1024)(128)(4,1)S(1)}, s32[]{:S(2)}) async-start(s8[11534336]{0:T(1024)(128)(4,1)} %bitcast.16), calls=%async_computation.7 | async-start | bytes 8388608
  33.6 6.1 %slice-start.8 = ((s8[11534336]{0:T(1024)(128)(4,1)}), s8[3145728]{0:T(1024)(128)(4,1)S(1)}, s32[]{:S(2)}) async-start(s8[11534336]{0:T(1024)(128)(4,1)} %bitcast.16), calls=%async_computation.8 | async-start | bytes 6291456
  34.7 3.8 %collective-permute-start.12 = (bf16[24,2816]{1,0:T(8,128)(2,1)S(1)}, bf16[24,2816]{1,0:T(8,128)(2,1)S(1)}, u32[]{:S(2)}, u32[]{:S(2)}) collective-permute-start(bf16[24,2816]{1,0:T(8,128)(2,1)S(1)} %get-tuple-element.72), channel_id=1, source_target_pairs={{0,1},{1,0},{2,3},{3,2},{4,5},{5,4},{6,7},{7,6},{8,9},{9,8},{10,11... | collective-permute-start | bytes 405512 | tf_op jit(solution)/shard_map/ppermute | solution.py:55
  36.5 3.1 %collective-permute-start.17 = (bf16[24,1408]{1,0:T(8,128)(2,1)S(1)}, bf16[24,1408]{1,0:T(8,128)(2,1)S(1)}, u32[]{:S(2)}, u32[]{:S(2)}) collective-permute-start(bf16[24,1408]{1,0:T(8,128)(2,1)S(1)} %shard_map.150.refs_4_.refs_2_), channel_id=1, source_target_pairs={{0,1},{1,0},{2,3},{3,2},{4,5},{5,4},{6,7},{7,6},{8,9},{9,8},{10,11... | collective-permute-start | bytes 202760 | tf_op jit(solution)/shard_map/ppermute | solution.py:55
  36.6 4.6 %collective-permute-start.16 = (bf16[24,1408]{1,0:T(8,128)(2,1)S(1)}, bf16[24,1408]{1,0:T(8,128)(2,1)S(1)}, u32[]{:S(2)}, u32[]{:S(2)}) collective-permute-start(bf16[24,1408]{1,0:T(8,128)(2,1)S(1)} %shard_map.150.refs_4_.refs_2_), channel_id=1, source_target_pairs={{0,2},{1,3},{2,0},{3,1},{4,6},{5,7},{6,4},{7,5},{8,10},{9,11},{10,... | collective-permute-start | bytes 202760 | tf_op jit(solution)/shard_map/ppermute | solution.py:55
  38.6 2.5 %collective-permute-start.15 = (bf16[24,1408]{1,0:T(8,128)(2,1)S(1)}, bf16[24,1408]{1,0:T(8,128)(2,1)S(1)}, u32[]{:S(2)}, u32[]{:S(2)}) collective-permute-start(bf16[24,1408]{1,0:T(8,128)(2,1)S(1)} %shard_map.152.refs_4_.refs_0_), channel_id=1, source_target_pairs={{0,1},{1,0},{2,3},{3,2},{4,5},{5,4},{6,7},{7,6},{8,9},{9,8},{10,11... | collective-permute-start | bytes 202760 | tf_op jit(solution)/shard_map/ppermute | solution.py:55
  38.7 4.6 %collective-permute-start.14 = (bf16[24,1408]{1,0:T(8,128)(2,1)S(1)}, bf16[24,1408]{1,0:T(8,128)(2,1)S(1)}, u32[]{:S(2)}, u32[]{:S(2)}) collective-permute-start(bf16[24,1408]{1,0:T(8,128)(2,1)S(1)} %shard_map.152.refs_4_.refs_0_), channel_id=1, source_target_pairs={{0,2},{1,3},{2,0},{3,1},{4,6},{5,7},{6,4},{7,5},{8,10},{9,11},{10,... | collective-permute-start | bytes 202760 | tf_op jit(solution)/shard_map/ppermute | solution.py:55
  41.1 2.4 %collective-permute-start.19 = (bf16[24,1408]{1,0:T(8,128)(2,1)S(1)}, bf16[24,1408]{1,0:T(8,128)(2,1)S(1)}, u32[]{:S(2)}, u32[]{:S(2)}) collective-permute-start(bf16[24,1408]{1,0:T(8,128)(2,1)S(1)} %collective-permute-done.16.refs_2_), channel_id=1, source_target_pairs={{0,1},{1,0},{2,3},{3,2},{4,5},{5,4},{6,7},{7,6},{8,9},{9,8},{10,11... | collective-permute-start | bytes 202760 | tf_op jit(solution)/shard_map/ppermute | solution.py:55
  43.2 1.6 %collective-permute-start.18 = (bf16[24,1408]{1,0:T(8,128)(2,1)S(1)}, bf16[24,1408]{1,0:T(8,128)(2,1)S(1)}, u32[]{:S(2)}, u32[]{:S(2)}) collective-permute-start(bf16[24,1408]{1,0:T(8,128)(2,1)S(1)} %collective-permute-done.14.refs_1_), channel_id=1, source_target_pairs={{0,1},{1,0},{2,3},{3,2},{4,5},{5,4},{6,7},{7,6},{8,9},{9,8},{10,11... | collective-permute-start | bytes 202760 | tf_op jit(solution)/shard_map/ppermute | solution.py:55
  45.5 4.3 %collective-permute-start.21 = (bf16[3,16,512]{2,1,0:T(8,128)(2,1)S(1)}, bf16[3,16,512]{2,1,0:T(8,128)(2,1)S(1)}, u32[]{:S(2)}, u32[]{:S(2)}) collective-permute-start(bf16[3,16,512]{2,1,0:T(8,128)(2,1)S(1)} %get-tuple-element.79), channel_id=1, source_target_pairs={{0,4},{4,0},{8,12},{12,8},{16,20},{20,16},{24,28},{28,24},{1,5},{5... | collective-permute-start | bytes 147464 | tf_op jit(solution)/shard_map/ppermute | solution.py:55
  47.1 7.2 %collective-permute-start.20 = (bf16[16,512]{1,0:T(8,128)(2,1)S(1)}, bf16[16,512]{1,0:T(8,128)(2,1)S(1)}, u32[]{:S(2)}, u32[]{:S(2)}) collective-permute-start(bf16[16,512]{1,0:T(8,128)(2,1)S(1)} %get-tuple-element.78), channel_id=1, source_target_pairs={{0,4},{4,0},{8,12},{12,8},{16,20},{20,16},{24,28},{28,24},{1,5},{5... | collective-permute-start | bytes 49160 | tf_op jit(solution)/shard_map/ppermute | solution.py:55
  49.8 5.6 %collective-permute-start.22 = (bf16[16,512]{1,0:T(8,128)(2,1)S(1)}, bf16[16,512]{1,0:T(8,128)(2,1)S(1)}, u32[]{:S(2)}, u32[]{:S(2)}) collective-permute-start(bf16[16,512]{1,0:T(8,128)(2,1)S(1)} %get-tuple-element.80), channel_id=1, source_target_pairs={{0,24},{4,28},{8,16},{12,20},{16,8},{20,12},{24,0},{28,4},{1,25},{... | collective-permute-start | bytes 49160 | tf_op jit(solution)/shard_map/ppermute | solution.py:55
  51.8 4.6 %collective-permute-start.23 = (bf16[16,512]{1,0:T(8,128)(2,1)S(1)}, bf16[16,512]{1,0:T(8,128)(2,1)S(1)}, u32[]{:S(2)}, u32[]{:S(2)}) collective-permute-start(bf16[16,512]{1,0:T(8,128)(2,1)S(1)} %get-tuple-element.81), channel_id=1, source_target_pairs={{0,16},{4,20},{8,24},{12,28},{16,0},{20,4},{24,8},{28,12},{1,17},{... | collective-permute-start | bytes 49160 | tf_op jit(solution)/shard_map/ppermute | solution.py:55
  52.0 4.5 %collective-permute-start.24 = (bf16[16,512]{1,0:T(8,128)(2,1)S(1)}, bf16[16,512]{1,0:T(8,128)(2,1)S(1)}, u32[]{:S(2)}, u32[]{:S(2)}) collective-permute-start(bf16[16,512]{1,0:T(8,128)(2,1)S(1)} %get-tuple-element.82), channel_id=1, source_target_pairs={{0,8},{4,12},{8,0},{12,4},{16,24},{20,28},{24,16},{28,20},{1,9},{5... | collective-permute-start | bytes 49160 | tf_op jit(solution)/shard_map/ppermute | solution.py:55
